TPU v7x, 32 devices: a whole 2x2x4 slice. The times are simulated.
32 devices in a mesh: groups: 2 (over y), ensemble: 4 (over z), tensor: 2 (over x), seq: 2 (over core).
Axes of the slice: x: 2, y: 2, z: 4, core: 2. Of those that a mesh axis runs over, the one named last changes fastest.
Arguments:
- pre_act: bfloat16 [768, 4, 8192], P(('groups', 'seq'), 'ensemble', 'tensor'), parts along dimension 0, may hold values from -6 to 6
- weights: bfloat16 [4, 2048, 8192], P('ensemble', 'seq', 'tensor'), may hold values from -0.0625 to 0.0625
- cotangent: bfloat16 [768], P(('groups', 'seq')), parts along dimension 0, may hold values from -24576 to 24576
Outputs:
- weight_grads: bfloat16 [8, 2048, 8192], P(('groups', 'ensemble'), 'seq', 'tensor'), parts along dimension 0
- act_grads: bfloat16 [768, 4, 8192], P(('groups', 'seq'), 'ensemble', 'tensor'), parts along dimension 0
- reward: float32 [768], P(('groups', 'seq')), parts along dimension 0
There are 2 independent parts, one for each index of `groups`. A program takes and returns all parts, laid end to end along the dimension named above; an argument that names none is the same for every part. Nothing has to cross between parts.
All inputs are finite; a program needn't handle non-finite values.
Results may differ from a plain program's by a relative error of at most 0.0076.
Values may be sent and summed in bfloat16 or wider, within the bound.
No kernel may reach another device: no remote copies, remote signals or barrier semaphores. Data moves between devices by JAX's collectives and lax.ppermute only.
A program may use at most 128 MiB of HBM per device.

v0:
```python
import jax
import jax.numpy as jnp
from jax import lax
from jax.sharding import PartitionSpec as P

D = 2048


def spread_and_grad(partial_value, weighting, members):
    predicted = lax.psum(partial_value, "tensor")
    member_sum, squares = lax.psum(
        (jnp.sum(predicted, axis=1), jnp.sum(predicted * predicted, axis=(1, 2))), "ensemble"
    )
    member_mean = member_sum / members
    spread = squares / members - jnp.sum(member_mean * member_mean, axis=1)
    grad_pred = (weighting[:, None, None] * (predicted - member_mean[:, None, :])).astype(
        jnp.bfloat16
    )
    return (spread, grad_pred)


def body(pre_act, weights, cotangent):
    activation = pre_act.astype(jnp.float32)
    sigmoid_act = jax.nn.sigmoid(activation)
    hidden = (activation * sigmoid_act).astype(jnp.bfloat16)
    members = pre_act.shape[1] * lax.axis_size("ensemble")
    factor = 2.0 / (members * D)
    full_weights = lax.all_gather(weights, "seq", axis=1, tiled=True)
    partial_value = jnp.einsum(
        "smf,mdf->smd", hidden, full_weights, preferred_element_type=jnp.float32
    )
    weighting = cotangent.astype(jnp.float32) * factor
    spread, grad_pred = spread_and_grad(partial_value, weighting, members)
    reward = spread / D
    local_grads = jnp.einsum("smd,smf->mdf", grad_pred, hidden, preferred_element_type=jnp.float32)
    weight_grads = lax.psum_scatter(
        local_grads.astype(jnp.bfloat16), "seq", scatter_dimension=1, tiled=True
    )
    grad_hidden = jnp.einsum(
        "smd,mdf->smf", grad_pred, full_weights, preferred_element_type=jnp.float32
    )
    slope = sigmoid_act * (1.0 + activation * (1.0 - sigmoid_act))
    act_grads = (grad_hidden * slope).astype(jnp.bfloat16)
    return (weight_grads, act_grads, reward)


def solution(mesh):
    placed = (
        P(("groups", "seq"), "ensemble", "tensor"),
        P("ensemble", "seq", "tensor"),
        P(("groups", "seq")),
    )
    return jax.shard_map(
        body,
        mesh=mesh,
        in_specs=placed,
        out_specs=(
            P(("groups", "ensemble"), "seq", "tensor"),
            P(("groups", "seq"), "ensemble", "tensor"),
            P(("groups", "seq")),
        ),
        check_vma=False,
    )
```

profile of v0, /device:TPU:1, one launch (start us, length us, event | category | flops | bytes accessed | tf_op | source)
XLA Modules:
  0.0 221.7 jit_solution(16943270336892502396)
XLA Ops:
  7.2 0.0 copy-start.1
  7.2 0.0 all-gather.2.cloned.1.call-start
  7.2 0.7 all-gather.2.cloned.1.call-update
  7.9 0.0 all-reduce.3.cloned.1.call-start
  8.0 34.2 %all-gather.2.cloned.1.call-done = bf16[1,2048,4096]{2,1,0:T(8,128)(2,1)} async-done(((bf16[1,1024,4096]{2,1,0:T(8,128)(2,1)}), bf16[1,2048,4096]{2,1,0:T(8,128)(2,1)}) %all-gather.2.cloned.1.call-update) | async-done | bytes 16777232 | tf_op jit(solution)/shard_map/all_gather | solution.py:28
  42.1 0.0 copy-done.1
  42.1 12.6 %fusion.19 = f32[192,1,2048]{2,0,1:T(8,128)} fusion(bf16[1,2048,4096]{2,1,0:T(8,128)(2,1)} %all-gather.2.cloned.1.call-done, bf16[192,1,4096]{2,0,1:T(8,128)(2,1)S(1)} %copy-done.1), kind=kOutput, calls=%fused_computation.17 | convolution fusion | flops 3225944064 | bytes 19922944 | tf_op jit(solution)/shard_map/smf,mdf->smd/dot_general | solution.py:29
  54.7 0.0 copy-start.2
  54.7 0.0 all-reduce.3.cloned.1.call-update
  54.7 0.0 all-reduce.5.cloned.1.call-start
  54.8 52.4 %all-reduce.3.cloned.1.call-done = f32[192,1,2048]{2,0,1:T(8,128)} async-done(((f32[192,1,2048]{2,0,1:T(8,128)}), f32[192,1,2048]{2,0,1:T(8,128)}) %all-reduce.3.cloned.1.call-update) | async-done | bytes 1572880 | tf_op jit(solution)/shard_map/psum | solution.py:10
  107.2 0.0 all-reduce.5.cloned.1.call-update
  107.2 0.0 reduce-scatter.2.cloned.1.call-start
  107.2 0.0 copy-done.2
  107.2 70.5 %all-reduce.5.cloned.1.call-done = f32[192,2048]{1,0:T(8,128)} async-done(((f32[192,2048]{1,0:T(8,128)}), f32[192,2048]{1,0:T(8,128)}) %all-reduce.5.cloned.1.call-update) | async-done | bytes 1572880 | tf_op jit(solution)/shard_map/psum | solution.py:11
  177.7 2.2 %multiply_reduce_fusion.1 = (f32[192]{0:T(256)S(1)}, bf16[192,2048]{1,0:T(8,128)(2,1)S(1)}) fusion(f32[192,1,2048]{2,0,1:T(8,128)} %all-reduce.3.cloned.1.call-done, f32[192,2048]{1,0:T(8,128)} %all-reduce.5.cloned.1.call-done, f32[192]{0:T(256)S(1)} %convert_multiply_fusion.2), kind=kLoop, calls=%fused_computation.23 | loop fusion | flops 2359104 | bytes 3933696 | tf_op jit(solution)/shard_map/reduce_sum | solution.py:12
  179.9 8.2 %convert_bitcast_fusion = bf16[1,2048,4096]{2,1,0:T(8,128)(2,1)} fusion(bf16[192,2048]{1,0:T(8,128)(2,1)S(1)} %get-tuple-element.4, bf16[192,1,4096]{2,0,1:T(8,128)(2,1)S(1)} %copy-done.1), kind=kOutput, calls=%fused_computation.4 | convolution fusion | flops 3234332672 | bytes 19136512 | tf_op jit(solution)/shard_map/smd,smf->mdf/dot_general | solution.py:35
  188.1 0.0 copy-start
  188.1 0.0 reduce-scatter.2.cloned.1.call-update
  188.1 9.0 %psum.23 = f32[192]{0:T(256)S(1)} all-reduce(f32[192]{0:T(256)S(1)} %get-tuple-element.3), channel_id=1, replica_groups=mesh['groups'=2,'ensemble'=4,'tensor'=2,'seq'=2] {'ensemble'}, use_global_device_ids=true, to_apply=%region_4.0 | all-reduce | flops 192 | bytes 1536 | tf_op jit(solution)/shard_map/psum | solution.py:11
  197.1 0.0 copy-done
  197.1 0.2 multiply_reduce_fusion
  197.3 0.6 subtract_multiply_fusion
  197.9 15.1 %fusion.10 = bf16[192,1,4096]{2,0,1:T(8,128)(2,1)} fusion(bf16[192,2048]{1,0:T(8,128)(2,1)S(1)} %get-tuple-element.4, bf16[1,2048,4096]{2,1,0:T(8,128)(2,1)} %all-gather.2.cloned.1.call-done, bf16[192,1,4096]{2,0,1:T(8,128)(2,1)} %param.3), kind=kOutput, calls=%fused_computation.7 | convolution fusion | flops 3229089792 | bytes 20709376 | tf_op jit(solution)/shard_map/smd,mdf->smf/dot_general | solution.py:39
  213.0 2.2 reduce-scatter.2.cloned.1.call-done
  (1 shorter events, 0.0 us)
Async XLA Ops:
  7.2 35.0 %copy-start.1 = (bf16[192,1,4096]{2,0,1:T(8,128)(2,1)S(1)}, bf16[192,1,4096]{2,0,1:T(8,128)(2,1)}, u32[]{:S(2)}) copy-start(bf16[192,1,4096]{2,0,1:T(8,128)(2,1)} %param.3) | copy-start | bytes 4718596
  7.2 34.9 %all-gather.2.cloned.1.call-start = ((), (), s32[]{:S(2)}) async-start(), calls=%async_computation.1 | async-start | bytes 25165824 | tf_op jit(solution)/shard_map/all_gather | solution.py:28
  7.9 99.2 %all-reduce.3.cloned.1.call-start = ((), (), s32[]{:S(2)}) async-start(), calls=%async_computation.2 | async-start | bytes 3145728 | tf_op jit(solution)/shard_map/psum | solution.py:10
  54.7 52.5 %copy-start.2 = (bf16[192]{0:T(256)(128)(2,1)S(1)}, bf16[192]{0:T(256)(128)(2,1)}, u32[]{:S(2)}) copy-start(bf16[192]{0:T(256)(128)(2,1)} %param.5) | copy-start | bytes 1156
  54.7 123.0 %all-reduce.5.cloned.1.call-start = ((), (), s32[]{:S(2)}) async-start(), calls=%async_computation.3 | async-start | bytes 3145728 | tf_op jit(solution)/shard_map/psum | solution.py:11
  107.2 108.0 %reduce-scatter.2.cloned.1.call-start = ((), (), s32[]{:S(2)}) async-start(), calls=%async_computation.4 | async-start | bytes 25165824 | tf_op jit(solution)/shard_map/reduce_scatter | solution.py:36
  188.1 9.0 %copy-start = (f32[192,2048]{1,0:T(8,128)S(1)}, f32[192,2048]{1,0:T(8,128)}, u32[]{:S(2)}) copy-start(f32[192,2048]{1,0:T(8,128)} %all-reduce.5.cloned.1.call-done) | copy-start | bytes 4718596
Sparse Core Ops, SparseCore 0:
  9.6 32.5 all-gather.1
  54.8 52.2 all-reduce.2
  109.7 68.0 all-reduce.4
  188.2 26.8 reduce-scatter.1
where the time goes:
time: 223 us; the launch traced here: 222 us
  waiting for transfers between devices  160 us (72%)
  matrix products  35.8 us (16%)
  between operations  13.8 us (6%)
  blocking collectives  8.98 us (4%)
  other arithmetic  3.04 us (1%)
    psum x1, waiting for transfers between devices, spread_and_grad(): lax.psum((jnp.sum(predicted, axis=1), jnp.sum(predicted * predicted, axis...  70.5 us
    psum x1, waiting for transfers between devices, spread_and_grad(): predicted = lax.psum(partial_value, 'tensor')  52.4 us
    all_gather x1, waiting for transfers between devices, body(): full_weights = lax.all_gather(weights, 'seq', axis=1, tiled=True)  34.2 us
    dot_general x1, matrix products, body(): jnp.einsum('smd,mdf->smf', grad_pred, full_weights, preferred_element_typ...  15.1 us
    dot_general x1, matrix products, body(): jnp.einsum('smf,mdf->smd', hidden, full_weights, preferred_element_type=j...  12.6 us
    psum x1, blocking collectives, spread_and_grad(): lax.psum((jnp.sum(predicted, axis=1), jnp.sum(predicted * predicted, axis...  8.98 us
    dot_general x1, matrix products, body(): jnp.einsum('smd,smf->mdf', grad_pred, hidden, preferred_element_type=jnp....  8.17 us
  transfers between devices with their start and end apart: 4, of which 4 were waited for; matrix products, arithmetic and copies ran while one was open for 7% of the time, Pallas kernels for 0%

commit v1 on v0

v1 whole, which is shorter than its diff:
```python
import jax
import jax.numpy as jnp
from jax import lax
from jax.sharding import PartitionSpec as P

F32, BF16 = jnp.float32, jnp.bfloat16
NT = (((1,), (1,)), ((), ()))
TN = (((0,), (0,)), ((), ()))
PIECES = 2


def swap(value, axis, distance):
    size = lax.axis_size(axis)
    return lax.ppermute(value, axis, [(i, i ^ distance) for i in range(size)])


def shares(size):
    return [1 << bit for bit in range(size.bit_length() - 1)]


def silu(value):
    wide = value.astype(F32)
    return (wide * jax.nn.sigmoid(wide)).astype(BF16)


def project(hidden, weights, start, width):
    rows = lax.dynamic_slice_in_dim(weights, start, width, 0)
    return lax.dot_general(hidden, rows, NT, preferred_element_type=F32)


def own_prediction(hidden, weights, start, width):
    place = lax.axis_index("tensor")
    offset = start
    kept = None
    for distance in reversed(shares(lax.axis_size("tensor"))):
        width //= 2
        high = (place // distance) % 2
        if kept is None:
            sent = project(hidden, weights, offset + (1 - high) * width, width)
            mine = project(hidden, weights, offset + high * width, width)
        else:
            sent = lax.dynamic_slice_in_dim(kept, (1 - high) * width, width, 1)
            mine = lax.dynamic_slice_in_dim(kept, high * width, width, 1)
        offset = offset + high * width
        kept = mine + swap(sent.astype(BF16), "tensor", distance).astype(F32)
    return kept


def member_mean_of(predicted):
    total = predicted
    for distance in shares(lax.axis_size("ensemble")):
        total = total + swap(total.astype(BF16), "ensemble", distance).astype(F32)
    return total / lax.axis_size("ensemble")


def all_features(share):
    place = lax.axis_index("tensor")
    for distance in shares(lax.axis_size("tensor")):
        other = swap(share, "tensor", distance)
        high = (place // distance) % 2
        first = jnp.where(high == 0, share, other)
        second = jnp.where(high == 0, other, share)
        share = jnp.concatenate([first, second], axis=1)
    return share


def body(pre_act, weights, cotangent):
    pre_act, weights = pre_act[:, 0, :], weights[0]
    steps, hidden_units = pre_act.shape
    features = weights.shape[0]
    members = lax.axis_size("ensemble")
    model_width = features * lax.axis_size("seq")
    factor = 2.0 / (members * model_width)

    pre_other = swap(pre_act, "seq", 1)
    cot_other = swap(cotangent, "seq", 1)
    hidden = (silu(pre_act), silu(pre_other))
    weighting = [c.astype(F32)[:, None] * factor for c in (cotangent, cot_other)]
    width = features // PIECES
    order = [(0, 0), (1, 0), (1, 1), (0, 1)]
    grads, spreads = {}, {}
    for side, piece in order:
        predicted = own_prediction(hidden[side], weights, piece * width, width)
        gap = predicted - member_mean_of(predicted)
        spreads[side, piece] = jnp.sum(gap * gap, axis=1)
        grads[side, piece] = all_features((weighting[side] * gap).astype(BF16))
    weight_grads, grad_hidden = [], [None, None]
    for piece in range(PIECES):
        terms = [
            lax.dot_general(grads[s, piece], hidden[s], TN, preferred_element_type=F32)
            for s in range(2)
        ]
        weight_grads.append((terms[0] + terms[1]).astype(BF16))
        rows = weights[piece * width : (piece + 1) * width]
        for side in range(2):
            term = jnp.dot(grads[side, piece], rows, preferred_element_type=F32)
            before = grad_hidden[side]
            grad_hidden[side] = term if before is None else before + term
    arrived = swap(grad_hidden[1].astype(BF16), "seq", 1).astype(F32)
    activation = pre_act.astype(F32)
    sigmoid_act = jax.nn.sigmoid(activation)
    slope = sigmoid_act * (1.0 + activation * (1.0 - sigmoid_act))
    act_grads = ((grad_hidden[0] + arrived) * slope).astype(BF16)
    both = jnp.stack([sum(spreads[s, p] for p in range(PIECES)) for s in range(2)])
    for axis in ("ensemble", "tensor"):
        for distance in shares(lax.axis_size(axis)):
            both = both + swap(both, axis, distance)
    spread = both[0] + swap(both[1], "seq", 1)
    reward = spread / (members * model_width)
    return (jnp.concatenate(weight_grads)[None], act_grads[:, None, :], reward)


def solution(mesh):
    placed = (
        P(("groups", "seq"), "ensemble", "tensor"),
        P("ensemble", "seq", "tensor"),
        P(("groups", "seq")),
    )
    return jax.shard_map(
        body,
        mesh=mesh,
        in_specs=placed,
        out_specs=(
            P(("groups", "ensemble"), "seq", "tensor"),
            P(("groups", "seq"), "ensemble", "tensor"),
            P(("groups", "seq")),
        ),
        check_vma=False,
    )
```

time: 223 us -> 102 us (0.46)
  waiting for transfers between devices: 160 us -> 26.4 us
  starting transfers between devices: 0.16 us -> 22.6 us
  between operations: 13.8 us -> 0.97 us
  other arithmetic: 3.04 us -> 12.8 us
  blocking collectives: 8.98 us -> 0 us
  matrix products: 35.8 us -> 39.2 us
    psum x2 -> x0, waiting for transfers between devices: 123 us -> none  [the longest x1 70.5 us: spread_and_grad(): lax.psum((jnp.sum(predicted, axis=1), jnp.sum(predicted * predicted, axis...]
    all_gather x1 -> x0, waiting for transfers between devices: 34.2 us -> none  [body(): full_weights = lax.all_gather(weights, 'seq', axis=1, tiled=True)]
    ppermute x0 -> x23, waiting for transfers between devices: none -> 26.4 us  [swap(): return lax.ppermute(value, axis, [(i, i ^ distance) for i in range(size)])]
    ppermute x0 -> x23, starting transfers between devices: none -> 22.6 us  [swap(): return lax.ppermute(value, axis, [(i, i ^ distance) for i in range(size)])]
    psum x1 -> x0, blocking collectives: 8.98 us -> none  [spread_and_grad(): lax.psum((jnp.sum(predicted, axis=1), jnp.sum(predicted * predicted, axis...]
    broadcast_in_dim x0 -> x1, other arithmetic: none -> 8.11 us  [body(): return (jnp.concatenate(weight_grads)[None], act_grads[:, None, :], reward)]
    dot_general x3 -> x16, matrix products: 35.8 us -> 39.2 us  [the longest x8 15.1 us: project(): return lax.dot_general(hidden, rows, NT, preferred_element_type=F32)]
    convert_element_type x0 -> x6, other arithmetic: none -> 3.32 us  [the longest x2 3.2 us: silu(): return (wide * jax.nn.sigmoid(wide)).astype(BF16)]
  transfers between devices with their start and end apart: 4 -> 23, of which waited for: 4 -> 13; matrix products, arithmetic and copies ran while one was open for 7% -> 39% of each run, Pallas kernels for 0% -> 0%
where the time goes in v1:
time: 102 us
  matrix products  39.2 us (38%)
  waiting for transfers between devices  26.4 us (26%)
  starting transfers between devices  22.6 us (22%)
  other arithmetic  12.8 us (13%)
    ppermute x23, waiting for transfers between devices, swap(): return lax.ppermute(value, axis, [(i, i ^ distance) for i in range(size)])  26.4 us
    ppermute x23, starting transfers between devices, swap(): return lax.ppermute(value, axis, [(i, i ^ distance) for i in range(size)])  22.6 us
    dot_general x8, matrix products, project(): return lax.dot_general(hidden, rows, NT, preferred_element_type=F32)  15.1 us
    dot_general x4, matrix products, body(): term = jnp.dot(grads[side, piece], rows, preferred_element_type=F32)  14.4 us
    dot_general x4, matrix products, body(): lax.dot_general(grads[s, piece], hidden[s], TN, preferred_element_type=F32)  9.69 us
    broadcast_in_dim x1, other arithmetic, body(): return (jnp.concatenate(weight_grads)[None], act_grads[:, None, :], reward)  8.11 us
    convert_element_type x2, other arithmetic, silu(): return (wide * jax.nn.sigmoid(wide)).astype(BF16)  3.2 us
  transfers between devices with their start and end apart: 23, of which 13 were waited for; matrix products, arithmetic and copies ran while one was open for 39% of the time, Pallas kernels for 0%

profile of v1, /device:TPU:1, one launch (start us, length us, event | category | flops | bytes accessed | tf_op | source)
XLA Modules:
  0.0 102.2 jit_solution(16477466331983193990)
XLA Ops:
  0.6 0.1 collective-permute-start.5
  0.8 0.5 collective-permute-start.4
  1.2 2.3 %fusion.53 = bf16[192,4096]{1,0:T(8,128)(2,1)S(1)} fusion(bf16[192,1,4096]{2,0,1:T(8,128)(2,1)} %param.3), kind=kLoop, calls=%fused_computation.65 | loop fusion | flops 4718592 | bytes 3145728 | tf_op jit(solution)/shard_map/convert_element_type | solution.py:23
  3.5 2.4 %fusion.66 = bf16[192,256]{1,0:T(8,128)(2,1)S(1)} fusion(bf16[192,4096]{1,0:T(8,128)(2,1)S(1)} %fusion.53, bf16[1,1024,4096]{2,1,0:T(8,128)(2,1)} %param.4, s32[]{:T(128)S(6)} %select_n.91), kind=kOutput, calls=%fused_computation.70 | convolution fusion | flops 402702336 | bytes 3768324 | tf_op jit(solution)/shard_map/dot_general | solution.py:28
  6.0 0.0 copy-start.2
  6.0 2.4 %collective-permute-start.10 = (bf16[192,256]{1,0:T(8,128)(2,1)S(1)}, bf16[192,256]{1,0:T(8,128)(2,1)S(1)}, u32[]{:S(2)}, u32[]{:S(2)}) collective-permute-start(bf16[192,256]{1,0:T(8,128)(2,1)S(1)} %fusion.66), channel_id=1, source_target_pairs={{0,2},{2,0},{1,3},{3,1},{4,6},{6,4},{5,7},{7,5},{8,10},{10,8},{9,1... | collective-permute-start | bytes 294920 | tf_op jit(solution)/shard_map/ppermute | solution.py:14
  8.3 2.4 %fusion.60 = bf16[192,256]{1,0:T(8,128)(2,1)S(1)} fusion(bf16[192,4096]{1,0:T(8,128)(2,1)S(1)} %fusion.53, bf16[1,1024,4096]{2,1,0:T(8,128)(2,1)} %param.4, s32[]{:T(128)S(6)} %select_n.85), kind=kOutput, calls=%fused_computation.68 | convolution fusion | flops 402702336 | bytes 3768324 | tf_op jit(solution)/shard_map/dot_general | solution.py:28
  10.8 0.1 collective-permute-start
  10.9 0.2 collective-permute-done.10
  11.1 2.6 %fusion.79 = (bf16[192,256]{1,0:T(8,128)(2,1)S(1)}, f32[192,256]{1,0:T(8,128)S(1)}) fusion(bf16[192,256]{1,0:T(8,128)(2,1)S(1)} %collective-permute-done.10, bf16[192,4096]{1,0:T(8,128)(2,1)S(1)} %fusion.53, bf16[1,1024,4096]{2,1,0:T(8,128)(2,1)} %param.4, s32[]{:T(128)S(6)} %select_n.90), kind=kOutput, calls=%fused_computation.109 | convolution fusion | flops 402800640 | bytes 4063236 | tf_op jit(solution)/shard_map/dot_general | solution.py:28
  13.7 1.4 %collective-permute-start.11 = (bf16[192,256]{1,0:T(8,128)(2,1)S(1)}, bf16[192,256]{1,0:T(8,128)(2,1)S(1)}, u32[]{:S(2)}, u32[]{:S(2)}) collective-permute-start(bf16[192,256]{1,0:T(8,128)(2,1)S(1)} %get-tuple-element.23), channel_id=1, source_target_pairs={{0,4},{4,0},{8,12},{12,8},{1,5},{5,1},{9,13},{13,9},{2,6},{6,2},{1... | collective-permute-start | bytes 294920 | tf_op jit(solution)/shard_map/ppermute | solution.py:14
  15.1 2.4 %fusion.78 = (bf16[192,256]{1,0:T(8,128)(2,1)S(1)}, f32[192,256]{1,0:T(8,128)S(1)}) fusion(bf16[192,256]{1,0:T(8,128)(2,1)S(1)} %collective-permute-done, bf16[192,4096]{1,0:T(8,128)(2,1)S(1)} %fusion.53, bf16[1,1024,4096]{2,1,0:T(8,128)(2,1)} %param.4, s32[]{:T(128)S(6)} %select_n.84), kind=kOutput, calls=%fused_computation.108 | convolution fusion | flops 402800640 | bytes 4063236 | tf_op jit(solution)/shard_map/dot_general | solution.py:28
  17.6 0.6 collective-permute-start.1
  18.2 2.4 %collective-permute-start.12 = (bf16[192,256]{1,0:T(8,128)(2,1)S(1)}, bf16[192,256]{1,0:T(8,128)(2,1)S(1)}, u32[]{:S(2)}, u32[]{:S(2)}) collective-permute-start(bf16[192,256]{1,0:T(8,128)(2,1)S(1)} %fusion.73), channel_id=1, source_target_pairs={{0,8},{4,12},{8,0},{12,4},{1,9},{5,13},{9,1},{13,5},{2,10},{6,14},... | collective-permute-start | bytes 294920 | tf_op jit(solution)/shard_map/ppermute | solution.py:14
  20.5 0.6 collective-permute-done.1
  21.1 2.4 %collective-permute-start.2 = (bf16[192,256]{1,0:T(8,128)(2,1)S(1)}, bf16[192,256]{1,0:T(8,128)(2,1)S(1)}, u32[]{:S(2)}, u32[]{:S(2)}) collective-permute-start(bf16[192,256]{1,0:T(8,128)(2,1)S(1)} %fusion.75), channel_id=1, source_target_pairs={{0,8},{4,12},{8,0},{12,4},{1,9},{5,13},{9,1},{13,5},{2,10},{6,14},... | collective-permute-start | bytes 294920 | tf_op jit(solution)/shard_map/ppermute | solution.py:14
  23.5 0.2 multiply_reduce_fusion.2
  23.7 5.2 %collective-permute-done.2 = bf16[192,256]{1,0:T(8,128)(2,1)S(1)} collective-permute-done((bf16[192,256]{1,0:T(8,128)(2,1)S(1)}, bf16[192,256]{1,0:T(8,128)(2,1)S(1)}, u32[]{:S(2)}, u32[]{:S(2)}) %collective-permute-start.2) | collective-permute-done | bytes 98336 | tf_op jit(solution)/shard_map/ppermute | solution.py:14
  28.9 0.2 multiply_reduce_fusion.3
  29.1 0.9 fusion.22
  30.0 2.4 %fusion.69 = bf16[192,256]{1,0:T(8,128)(2,1)S(1)} fusion(bf16[192,4096]{1,0:T(8,128)(2,1)S(1)} %fusion.22, bf16[1,1024,4096]{2,1,0:T(8,128)(2,1)} %param.4, s32[]{:T(128)S(6)} %select_n.91), kind=kOutput, calls=%fused_computation.71 | convolution fusion | flops 402702336 | bytes 3768324 | tf_op jit(solution)/shard_map/dot_general | solution.py:28
  32.4 2.4 %collective-permute-start.14 = (bf16[192,256]{1,0:T(8,128)(2,1)S(1)}, bf16[192,256]{1,0:T(8,128)(2,1)S(1)}, u32[]{:S(2)}, u32[]{:S(2)}) collective-permute-start(bf16[192,256]{1,0:T(8,128)(2,1)S(1)} %fusion.69), channel_id=1, source_target_pairs={{0,2},{2,0},{1,3},{3,1},{4,6},{6,4},{5,7},{7,5},{8,10},{10,8},{9,1... | collective-permute-start | bytes 294920 | tf_op jit(solution)/shard_map/ppermute | solution.py:14
  34.8 0.9 fusion.63
  35.7 0.1 collective-permute-start.6
  35.9 1.0 collective-permute-done.14
  36.8 0.9 fusion.100
  37.8 0.1 collective-permute-start.15
  37.8 2.0 %collective-permute-done.6 = bf16[192,256]{1,0:T(8,128)(2,1)S(1)} collective-permute-done((bf16[192,256]{1,0:T(8,128)(2,1)S(1)}, bf16[192,256]{1,0:T(8,128)(2,1)S(1)}, u32[]{:S(2)}, u32[]{:S(2)}) %collective-permute-start.6) | collective-permute-done | bytes 98336 | tf_op jit(solution)/shard_map/ppermute | solution.py:14
  39.8 0.9 fusion.101
  40.7 0.1 collective-permute-start.7
  40.8 0.7 collective-permute-done.15
  41.5 0.3 collective-permute-start.16
  41.8 3.1 %collective-permute-done.7 = bf16[192,256]{1,0:T(8,128)(2,1)S(1)} collective-permute-done((bf16[192,256]{1,0:T(8,128)(2,1)S(1)}, bf16[192,256]{1,0:T(8,128)(2,1)S(1)}, u32[]{:S(2)}, u32[]{:S(2)}) %collective-permute-start.7) | collective-permute-done | bytes 98336 | tf_op jit(solution)/shard_map/ppermute | solution.py:14
  45.0 0.1 collective-permute-start.8
  45.0 2.1 %collective-permute-done.16 = bf16[192,256]{1,0:T(8,128)(2,1)S(1)} collective-permute-done((bf16[192,256]{1,0:T(8,128)(2,1)S(1)}, bf16[192,256]{1,0:T(8,128)(2,1)S(1)}, u32[]{:S(2)}, u32[]{:S(2)}) %collective-permute-start.16) | collective-permute-done | bytes 98336 | tf_op jit(solution)/shard_map/ppermute | solution.py:14
  47.1 0.2 multiply_reduce_fusion
  47.3 4.7 %collective-permute-done.8 = bf16[192,256]{1,0:T(8,128)(2,1)S(1)} collective-permute-done((bf16[192,256]{1,0:T(8,128)(2,1)S(1)}, bf16[192,256]{1,0:T(8,128)(2,1)S(1)}, u32[]{:S(2)}, u32[]{:S(2)}) %collective-permute-start.8) | collective-permute-done | bytes 98336 | tf_op jit(solution)/shard_map/ppermute | solution.py:14
  52.0 0.2 multiply_reduce_fusion.1
  52.2 0.1 collective-permute-start.19
  52.3 0.1 collective-permute-start.13
  52.4 1.5 %collective-permute-start.3 = (bf16[192,256]{1,0:T(8,128)(2,1)S(1)}, bf16[192,256]{1,0:T(8,128)(2,1)S(1)}, u32[]{:S(2)}, u32[]{:S(2)}) collective-permute-start(bf16[192,256]{1,0:T(8,128)(2,1)S(1)} %get-tuple-element.6), channel_id=1, source_target_pairs={{0,2},{2,0},{1,3},{3,1},{4,6},{6,4},{5,7},{7,5},{8,10},{10,8},{9,1... | collective-permute-start | bytes 294920 | tf_op jit(solution)/shard_map/ppermute | solution.py:14
  53.8 1.1 %collective-permute-done.19 = f32[2,192]{1,0:T(2,128)S(1)} collective-permute-done((f32[2,192]{1,0:T(2,128)S(1)}, f32[2,192]{1,0:T(2,128)S(1)}, u32[]{:S(2)}, u32[]{:S(2)}) %collective-permute-start.19) | collective-permute-done | bytes 1568 | tf_op jit(solution)/shard_map/ppermute | solution.py:14
  55.0 0.1 collective-permute-start.20
  55.1 0.8 collective-permute-done.13
  55.9 2.5 %collective-permute-done.20 = f32[2,192]{1,0:T(2,128)S(1)} collective-permute-done((f32[2,192]{1,0:T(2,128)S(1)}, f32[2,192]{1,0:T(2,128)S(1)}, u32[]{:S(2)}, u32[]{:S(2)}) %collective-permute-start.20) | collective-permute-done | bytes 1568 | tf_op jit(solution)/shard_map/ppermute | solution.py:14
  58.4 0.1 collective-permute-start.21
  58.5 4.9 %fusion.7 = f32[192,4096]{1,0:T(8,128)} fusion(bf16[1,1024,4096]{2,1,0:T(8,128)(2,1)} %param.4, bf16[192,256]{1,0:T(8,128)(2,1)S(1)} %get-tuple-element.16, bf16[192,256]{1,0:T(8,128)(2,1)S(1)} %get-tuple-element.15), kind=kOutput, calls=%fused_computation.15 | convolution fusion | flops 805699584 | bytes 7536640 | tf_op jit(solution)/shard_map/dot_general | solution.py:96
  63.3 5.5 %collective-permute-start.22 = (f32[192]{0:T(256)S(1)}, f32[192]{0:T(256)S(1)}, u32[]{:S(2)}, u32[]{:S(2)}) collective-permute-start(f32[192]{0:T(256)S(1)} %bitcast.87), channel_id=1, source_target_pairs={{0,1},{1,0},{2,3},{3,2},{4,5},{5,4},{6,7},{7,6},{8,9},{9,8},{10,11... | collective-permute-start | bytes 2312 | tf_op jit(solution)/shard_map/ppermute | solution.py:14
  68.8 1.8 %collective-permute-start.17 = (bf16[192,256]{1,0:T(8,128)(2,1)S(1)}, bf16[192,256]{1,0:T(8,128)(2,1)S(1)}, u32[]{:S(2)}, u32[]{:S(2)}) collective-permute-start(bf16[192,256]{1,0:T(8,128)(2,1)S(1)} %get-tuple-element.8), channel_id=1, source_target_pairs={{0,2},{2,0},{1,3},{3,1},{4,6},{6,4},{5,7},{7,5},{8,10},{10,8},{9,1... | collective-permute-start | bytes 294920 | tf_op jit(solution)/shard_map/ppermute | solution.py:14
  70.7 0.1 collective-permute-start.9
  70.7 0.6 add_multiply_fusion
  71.3 2.5 %collective-permute-done.17 = bf16[192,256]{1,0:T(8,128)(2,1)S(1)} collective-permute-done((bf16[192,256]{1,0:T(8,128)(2,1)S(1)}, bf16[192,256]{1,0:T(8,128)(2,1)S(1)}, u32[]{:S(2)}, u32[]{:S(2)}) %collective-permute-start.17) | collective-permute-done | bytes 98336 | tf_op jit(solution)/shard_map/ppermute | solution.py:14
  73.8 0.0 copy-start.1
  73.8 0.0 slice-start.2
  73.8 1.3 %fusion.76 = f32[512,4096]{1,0:T(8,128)S(1)} fusion(bf16[192,4096]{1,0:T(8,128)(2,1)S(1)} %fusion.22, bf16[192,256]{1,0:T(8,128)(2,1)S(1)} %get-tuple-element.18, bf16[192,256]{1,0:T(8,128)(2,1)S(1)} %get-tuple-element.17), kind=kOutput, calls=%fused_computation.98 | convolution fusion | flops 805699584 | bytes 10158080 | tf_op jit(solution)/shard_map/dot_general | solution.py:90
  75.1 0.1 copy-done.1
  75.2 3.6 %add_convert_fusion = bf16[512,4096]{1,0:T(8,128)(2,1)} fusion(f32[512,4096]{1,0:T(8,128)S(1)} %fusion.76, bf16[192,256]{1,0:T(8,128)(2,1)S(1)} %get-tuple-element.16, bf16[192,256]{1,0:T(8,128)(2,1)S(1)} %get-tuple-element.15, bf16[192,1,4096]{2,0,1:T(8,128)(2,1)S(1)} %copy-done.1), kind=kOutput, calls=%fused_computation.1 | convolution fusion | flops 814612480 | bytes 14352384 | tf_op jit(solution)/shard_map/dot_general | solution.py:90
  78.8 1.0 fusion.5
  79.9 2.2 %fusion.3 = bf16[192,4096]{1,0:T(8,128)(2,1)} fusion(f32[192,4096]{1,0:T(8,128)S(1)} %fusion.5, bf16[1,1024,4096]{2,1,0:T(8,128)(2,1)S(1)} %bitcast.78, bf16[192,256]{1,0:T(8,128)(2,1)S(1)} %get-tuple-element.14, bf16[192,256]{1,0:T(8,128)(2,1)S(1)} %get-tuple-element.13), kind=kOutput, calls=%fused_computation.8 | convolution fusion | flops 807272448 | bytes 9109504 | tf_op jit(solution)/shard_map/dot_general | solution.py:96
  82.1 0.8 collective-permute-start.18
  82.9 1.3 %fusion.77 = f32[512,4096]{1,0:T(8,128)S(1)} fusion(bf16[192,4096]{1,0:T(8,128)(2,1)S(1)} %fusion.22, bf16[192,256]{1,0:T(8,128)(2,1)S(1)} %get-tuple-element.14, bf16[192,256]{1,0:T(8,128)(2,1)S(1)} %get-tuple-element.13), kind=kOutput, calls=%fused_computation.99 | convolution fusion | flops 805699584 | bytes 10158080 | tf_op jit(solution)/shard_map/dot_general | solution.py:90
  84.2 3.5 %add_convert_fusion.1 = bf16[512,4096]{1,0:T(8,128)(2,1)} fusion(f32[512,4096]{1,0:T(8,128)S(1)} %fusion.77, bf16[192,256]{1,0:T(8,128)(2,1)S(1)} %get-tuple-element.12, bf16[192,256]{1,0:T(8,128)(2,1)S(1)} %get-tuple-element.11, bf16[192,1,4096]{2,0,1:T(8,128)(2,1)S(1)} %copy-done.1), kind=kOutput, calls=%fused_computation.2 | convolution fusion | flops 814612480 | bytes 14352384 | tf_op jit(solution)/shard_map/dot_general | solution.py:90
  87.7 8.1 %maximum_bitcast_fusion = bf16[1,1024,4096]{2,1,0:T(8,128)(2,1)} fusion(bf16[512,4096]{1,0:T(8,128)(2,1)} %add_convert_fusion, bf16[512,4096]{1,0:T(8,128)(2,1)} %add_convert_fusion.1), kind=kLoop, calls=%fused_computation | loop fusion | flops 16777216 | bytes 16777216 | tf_op jit(solution)/shard_map/broadcast_in_dim | solution.py:110
  95.8 6.3 %fusion.4 = bf16[192,1,4096]{2,0,1:T(8,128)(2,1)} fusion(f32[192,4096]{1,0:T(8,128)S(1)} %copy-done, bf16[1,1024,4096]{2,1,0:T(8,128)(2,1)} %param.4, bf16[192,4096]{1,0:T(8,128)(2,1)} %collective-permute-done.18, bf16[192,256]{1,0:T(8,128)(2,1)S(1)} %get-tuple-element.12, bf16[192,256]{1,0:T(8,128)(2,1)S(1)} %get-tuple-element.11, ...), kind=kOutput, calls=%fused_computation.9 | convolution fusion | flops 815923200 | bytes 12255232 | tf_op jit(solution)/shard_map/dot_general | solution.py:96
  (39 shorter events, 0.3 us)
Async XLA Ops:
  0.6 28.4 %collective-permute-start.5 = (bf16[192,4096]{1,0:T(8,128)(2,1)}, bf16[192,4096]{1,0:T(8,128)(2,1)S(1)}, u32[]{:S(2)}, u32[]{:S(2)}) collective-permute-start(bf16[192,4096]{1,0:T(8,128)(2,1)} %bitcast.79), channel_id=1, source_target_pairs={{0,1},{1,0},{2,3},{3,2},{4,5},{5,4},{6,7},{7,6},{8,9},{9,8},{10,11... | collective-permute-start | bytes 4718600 | tf_op jit(solution)/shard_map/ppermute | solution.py:14
  0.8 10.1 %collective-permute-start.4 = (bf16[192]{0:T(256)(128)(2,1)}, bf16[192]{0:T(256)(128)(2,1)S(1)}, u32[]{:S(2)}, u32[]{:S(2)}) collective-permute-start(bf16[192]{0:T(256)(128)(2,1)} %param.5), channel_id=1, source_target_pairs={{0,1},{1,0},{2,3},{3,2},{4,5},{5,4},{6,7},{7,6},{8,9},{9,8},{10,11... | collective-permute-start | bytes 1160 | tf_op jit(solution)/shard_map/ppermute | solution.py:14
  6.0 4.9 %copy-start.2 = (bf16[192]{0:T(256)(128)(2,1)S(1)}, bf16[192]{0:T(256)(128)(2,1)}, u32[]{:S(2)}) copy-start(bf16[192]{0:T(256)(128)(2,1)} %param.5) | copy-start | bytes 1156
  6.0 5.1 %collective-permute-start.10 = (bf16[192,256]{1,0:T(8,128)(2,1)S(1)}, bf16[192,256]{1,0:T(8,128)(2,1)S(1)}, u32[]{:S(2)}, u32[]{:S(2)}) collective-permute-start(bf16[192,256]{1,0:T(8,128)(2,1)S(1)} %fusion.66), channel_id=1, source_target_pairs={{0,2},{2,0},{1,3},{3,1},{4,6},{6,4},{5,7},{7,5},{8,10},{10,8},{9,1... | collective-permute-start | bytes 294920 | tf_op jit(solution)/shard_map/ppermute | solution.py:14
  10.8 4.3 %collective-permute-start = (bf16[192,256]{1,0:T(8,128)(2,1)S(1)}, bf16[192,256]{1,0:T(8,128)(2,1)S(1)}, u32[]{:S(2)}, u32[]{:S(2)}) collective-permute-start(bf16[192,256]{1,0:T(8,128)(2,1)S(1)} %fusion.60), channel_id=1, source_target_pairs={{0,2},{2,0},{1,3},{3,1},{4,6},{6,4},{5,7},{7,5},{8,10},{10,8},{9,1... | collective-permute-start | bytes 294920 | tf_op jit(solution)/shard_map/ppermute | solution.py:14
  11.1 23.7 %slice-start = ((s8[8388608]{0:T(1024)(128)(4,1)}), s8[4194304]{0:T(1024)(128)(4,1)S(1)}, s32[]{:S(2)}) async-start(s8[8388608]{0:T(1024)(128)(4,1)} %bitcast.75), calls=%async_computation | async-start | bytes 8388608
  13.7 4.4 %collective-permute-start.11 = (bf16[192,256]{1,0:T(8,128)(2,1)S(1)}, bf16[192,256]{1,0:T(8,128)(2,1)S(1)}, u32[]{:S(2)}, u32[]{:S(2)}) collective-permute-start(bf16[192,256]{1,0:T(8,128)(2,1)S(1)} %get-tuple-element.23), channel_id=1, source_target_pairs={{0,4},{4,0},{8,12},{12,8},{1,5},{5,1},{9,13},{13,9},{2,6},{6,2},{1... | collective-permute-start | bytes 294920 | tf_op jit(solution)/shard_map/ppermute | solution.py:14
  17.6 3.5 %collective-permute-start.1 = (bf16[192,256]{1,0:T(8,128)(2,1)S(1)}, bf16[192,256]{1,0:T(8,128)(2,1)S(1)}, u32[]{:S(2)}, u32[]{:S(2)}) collective-permute-start(bf16[192,256]{1,0:T(8,128)(2,1)S(1)} %get-tuple-element.27), channel_id=1, source_target_pairs={{0,4},{4,0},{8,12},{12,8},{1,5},{5,1},{9,13},{13,9},{2,6},{6,2},{1... | collective-permute-start | bytes 294920 | tf_op jit(solution)/shard_map/ppermute | solution.py:14
  18.1 16.7 %slice-start.1 = ((s8[8388608]{0:T(1024)(128)(4,1)}), s8[4194304]{0:T(1024)(128)(4,1)S(1)}, s32[]{:S(2)}) async-start(s8[8388608]{0:T(1024)(128)(4,1)} %bitcast.75), calls=%async_computation.1 | async-start | bytes 8388608
  18.2 5.3 %collective-permute-start.12 = (bf16[192,256]{1,0:T(8,128)(2,1)S(1)}, bf16[192,256]{1,0:T(8,128)(2,1)S(1)}, u32[]{:S(2)}, u32[]{:S(2)}) collective-permute-start(bf16[192,256]{1,0:T(8,128)(2,1)S(1)} %fusion.73), channel_id=1, source_target_pairs={{0,8},{4,12},{8,0},{12,4},{1,9},{5,13},{9,1},{13,5},{2,10},{6,14},... | collective-permute-start | bytes 294920 | tf_op jit(solution)/shard_map/ppermute | solution.py:14
  21.1 7.7 %collective-permute-start.2 = (bf16[192,256]{1,0:T(8,128)(2,1)S(1)}, bf16[192,256]{1,0:T(8,128)(2,1)S(1)}, u32[]{:S(2)}, u32[]{:S(2)}) collective-permute-start(bf16[192,256]{1,0:T(8,128)(2,1)S(1)} %fusion.75), channel_id=1, source_target_pairs={{0,8},{4,12},{8,0},{12,4},{1,9},{5,13},{9,1},{13,5},{2,10},{6,14},... | collective-permute-start | bytes 294920 | tf_op jit(solution)/shard_map/ppermute | solution.py:14
  32.4 4.4 %collective-permute-start.14 = (bf16[192,256]{1,0:T(8,128)(2,1)S(1)}, bf16[192,256]{1,0:T(8,128)(2,1)S(1)}, u32[]{:S(2)}, u32[]{:S(2)}) collective-permute-start(bf16[192,256]{1,0:T(8,128)(2,1)S(1)} %fusion.69), channel_id=1, source_target_pairs={{0,2},{2,0},{1,3},{3,1},{4,6},{6,4},{5,7},{7,5},{8,10},{10,8},{9,1... | collective-permute-start | bytes 294920 | tf_op jit(solution)/shard_map/ppermute | solution.py:14
  35.7 4.1 %collective-permute-start.6 = (bf16[192,256]{1,0:T(8,128)(2,1)S(1)}, bf16[192,256]{1,0:T(8,128)(2,1)S(1)}, u32[]{:S(2)}, u32[]{:S(2)}) collective-permute-start(bf16[192,256]{1,0:T(8,128)(2,1)S(1)} %fusion.63), channel_id=1, source_target_pairs={{0,2},{2,0},{1,3},{3,1},{4,6},{6,4},{5,7},{7,5},{8,10},{10,8},{9,1... | collective-permute-start | bytes 294920 | tf_op jit(solution)/shard_map/ppermute | solution.py:14
  37.8 3.7 %collective-permute-start.15 = (bf16[192,256]{1,0:T(8,128)(2,1)S(1)}, bf16[192,256]{1,0:T(8,128)(2,1)S(1)}, u32[]{:S(2)}, u32[]{:S(2)}) collective-permute-start(bf16[192,256]{1,0:T(8,128)(2,1)S(1)} %get-tuple-element.21), channel_id=1, source_target_pairs={{0,4},{4,0},{8,12},{12,8},{1,5},{5,1},{9,13},{13,9},{2,6},{6,2},{1... | collective-permute-start | bytes 294920 | tf_op jit(solution)/shard_map/ppermute | solution.py:14
  40.7 4.2 %collective-permute-start.7 = (bf16[192,256]{1,0:T(8,128)(2,1)S(1)}, bf16[192,256]{1,0:T(8,128)(2,1)S(1)}, u32[]{:S(2)}, u32[]{:S(2)}) collective-permute-start(bf16[192,256]{1,0:T(8,128)(2,1)S(1)} %get-tuple-element.25), channel_id=1, source_target_pairs={{0,4},{4,0},{8,12},{12,8},{1,5},{5,1},{9,13},{13,9},{2,6},{6,2},{1... | collective-permute-start | bytes 294920 | tf_op jit(solution)/shard_map/ppermute | solution.py:14
  41.5 5.6 %collective-permute-start.16 = (bf16[192,256]{1,0:T(8,128)(2,1)S(1)}, bf16[192,256]{1,0:T(8,128)(2,1)S(1)}, u32[]{:S(2)}, u32[]{:S(2)}) collective-permute-start(bf16[192,256]{1,0:T(8,128)(2,1)S(1)} %fusion.72), channel_id=1, source_target_pairs={{0,8},{4,12},{8,0},{12,4},{1,9},{5,13},{9,1},{13,5},{2,10},{6,14},... | collective-permute-start | bytes 294920 | tf_op jit(solution)/shard_map/ppermute | solution.py:14
  45.0 7.1 %collective-permute-start.8 = (bf16[192,256]{1,0:T(8,128)(2,1)S(1)}, bf16[192,256]{1,0:T(8,128)(2,1)S(1)}, u32[]{:S(2)}, u32[]{:S(2)}) collective-permute-start(bf16[192,256]{1,0:T(8,128)(2,1)S(1)} %fusion.74), channel_id=1, source_target_pairs={{0,8},{4,12},{8,0},{12,4},{1,9},{5,13},{9,1},{13,5},{2,10},{6,14},... | collective-permute-start | bytes 294920 | tf_op jit(solution)/shard_map/ppermute | solution.py:14
  52.2 2.7 %collective-permute-start.19 = (f32[2,192]{1,0:T(2,128)S(1)}, f32[2,192]{1,0:T(2,128)S(1)}, u32[]{:S(2)}, u32[]{:S(2)}) collective-permute-start(f32[2,192]{1,0:T(2,128)S(1)} %pad_maximum_fusion.12), channel_id=1, source_target_pairs={{0,4},{4,0},{8,12},{12,8},{1,5},{5,1},{9,13},{13,9},{2,6},{6,2},{1... | collective-permute-start | bytes 4616 | tf_op jit(solution)/shard_map/ppermute | solution.py:14
  52.3 3.5 %collective-permute-start.13 = (bf16[192,256]{1,0:T(8,128)(2,1)S(1)}, bf16[192,256]{1,0:T(8,128)(2,1)S(1)}, u32[]{:S(2)}, u32[]{:S(2)}) collective-permute-start(bf16[192,256]{1,0:T(8,128)(2,1)S(1)} %get-tuple-element.4), channel_id=1, source_target_pairs={{0,2},{2,0},{1,3},{3,1},{4,6},{6,4},{5,7},{7,5},{8,10},{10,8},{9,1... | collective-permute-start | bytes 294920 | tf_op jit(solution)/shard_map/ppermute | solution.py:14
  52.4 16.4 %collective-permute-start.3 = (bf16[192,256]{1,0:T(8,128)(2,1)S(1)}, bf16[192,256]{1,0:T(8,128)(2,1)S(1)}, u32[]{:S(2)}, u32[]{:S(2)}) collective-permute-start(bf16[192,256]{1,0:T(8,128)(2,1)S(1)} %get-tuple-element.6), channel_id=1, source_target_pairs={{0,2},{2,0},{1,3},{3,1},{4,6},{6,4},{5,7},{7,5},{8,10},{10,8},{9,1... | collective-permute-start | bytes 294920 | tf_op jit(solution)/shard_map/ppermute | solution.py:14
  55.0 3.4 %collective-permute-start.20 = (f32[2,192]{1,0:T(2,128)S(1)}, f32[2,192]{1,0:T(2,128)S(1)}, u32[]{:S(2)}, u32[]{:S(2)}) collective-permute-start(f32[2,192]{1,0:T(2,128)S(1)} %fusion.96), channel_id=1, source_target_pairs={{0,8},{4,12},{8,0},{12,4},{1,9},{5,13},{9,1},{13,5},{2,10},{6,14},... | collective-permute-start | bytes 4616 | tf_op jit(solution)/shard_map/ppermute | solution.py:14
  58.4 4.9 %collective-permute-start.21 = (f32[2,192]{1,0:T(2,128)S(1)}, f32[2,192]{1,0:T(2,128)S(1)}, u32[]{:S(2)}, u32[]{:S(2)}) collective-permute-start(f32[2,192]{1,0:T(2,128)S(1)} %fusion.112), channel_id=1, source_target_pairs={{0,2},{2,0},{1,3},{3,1},{4,6},{6,4},{5,7},{7,5},{8,10},{10,8},{9,1... | collective-permute-start | bytes 4616 | tf_op jit(solution)/shard_map/ppermute | solution.py:14
  63.3 7.4 %collective-permute-start.22 = (f32[192]{0:T(256)S(1)}, f32[192]{0:T(256)S(1)}, u32[]{:S(2)}, u32[]{:S(2)}) collective-permute-start(f32[192]{0:T(256)S(1)} %bitcast.87), channel_id=1, source_target_pairs={{0,1},{1,0},{2,3},{3,2},{4,5},{5,4},{6,7},{7,6},{8,9},{9,8},{10,11... | collective-permute-start | bytes 2312 | tf_op jit(solution)/shard_map/ppermute | solution.py:14
  68.8 4.9 %collective-permute-start.17 = (bf16[192,256]{1,0:T(8,128)(2,1)S(1)}, bf16[192,256]{1,0:T(8,128)(2,1)S(1)}, u32[]{:S(2)}, u32[]{:S(2)}) collective-permute-start(bf16[192,256]{1,0:T(8,128)(2,1)S(1)} %get-tuple-element.8), channel_id=1, source_target_pairs={{0,2},{2,0},{1,3},{3,1},{4,6},{6,4},{5,7},{7,5},{8,10},{10,8},{9,1... | collective-permute-start | bytes 294920 | tf_op jit(solution)/shard_map/ppermute | solution.py:14
  70.7 9.2 %collective-permute-start.9 = (bf16[192,256]{1,0:T(8,128)(2,1)S(1)}, bf16[192,256]{1,0:T(8,128)(2,1)S(1)}, u32[]{:S(2)}, u32[]{:S(2)}) collective-permute-start(bf16[192,256]{1,0:T(8,128)(2,1)S(1)} %get-tuple-element.10), channel_id=1, source_target_pairs={{0,2},{2,0},{1,3},{3,1},{4,6},{6,4},{5,7},{7,5},{8,10},{10,8},{9,1... | collective-permute-start | bytes 294920 | tf_op jit(solution)/shard_map/ppermute | solution.py:14
  73.8 1.4 %copy-start.1 = (bf16[192,1,4096]{2,0,1:T(8,128)(2,1)S(1)}, bf16[192,1,4096]{2,0,1:T(8,128)(2,1)}, u32[]{:S(2)}) copy-start(bf16[192,1,4096]{2,0,1:T(8,128)(2,1)} %param.3) | copy-start | bytes 4718596
  73.8 5.0 %slice-start.2 = ((s8[8388608]{0:T(1024)(128)(4,1)}), s8[4194304]{0:T(1024)(128)(4,1)S(1)}, s32[]{:S(2)}) async-start(s8[8388608]{0:T(1024)(128)(4,1)} %bitcast.77), calls=%async_computation.2 | async-start | bytes 8388608
  75.2 3.6 %slice-start.3 = ((s8[8388608]{0:T(1024)(128)(4,1)}), s8[4194304]{0:T(1024)(128)(4,1)S(1)}, s32[]{:S(2)}) async-start(s8[8388608]{0:T(1024)(128)(4,1)} %bitcast.77), calls=%async_computation.3 | async-start | bytes 8388608
  82.1 13.7 %collective-permute-start.18 = (bf16[192,4096]{1,0:T(8,128)(2,1)}, bf16[192,4096]{1,0:T(8,128)(2,1)}, u32[]{:S(2)}, u32[]{:S(2)}) collective-permute-start(bf16[192,4096]{1,0:T(8,128)(2,1)} %fusion.3), channel_id=1, source_target_pairs={{0,1},{1,0},{2,3},{3,2},{4,5},{5,4},{6,7},{7,6},{8,9},{9,8},{10,11... | collective-permute-start | bytes 4718600 | tf_op jit(solution)/shard_map/ppermute | solution.py:14
  87.7 8.1 %copy-start = (f32[192,4096]{1,0:T(8,128)S(1)}, f32[192,4096]{1,0:T(8,128)}, u32[]{:S(2)}) copy-start(f32[192,4096]{1,0:T(8,128)} %fusion.7) | copy-start | bytes 9437188

commit v2 on v0

v2 whole, which is shorter than its diff:
```python
import functools

import jax
import jax.numpy as jnp
from jax import lax
from jax.experimental import pallas as pl
from jax.experimental.pallas import tpu as pltpu
from jax.sharding import PartitionSpec as P

F32, BF16 = jnp.float32, jnp.bfloat16
NT = (((1,), (1,)), ((), ()))
TN = (((0,), (0,)), ((), ()))
PIECES = 2
SCALE = 0.2
VMEM_LIMIT = 16 * 2**20


def swap(value, axis, distance):
    size = lax.axis_size(axis)
    return lax.ppermute(value, axis, [(i, i ^ distance) for i in range(size)])


def shares(size):
    return [1 << bit for bit in range(size.bit_length() - 1)]


def sigmoid(wide):
    return jax.nn.sigmoid(wide)


def silu(value):
    wide = value.astype(F32)
    return (wide * sigmoid(wide)).astype(BF16)


VMEM = pl.BlockSpec(memory_space=pltpu.VMEM)
HBM = pl.BlockSpec(memory_space=pltpu.HBM)


def in_vmem(shape, dtype):
    return pltpu.VMEM(shape, dtype)


def in_hbm(shape, dtype):
    return pltpu.HBM(shape, dtype)


def call(kernel, out_shape, in_specs, scratch=(), aliases=None, work=0.1, name=None):
    outs = out_shape if isinstance(out_shape, list) else [out_shape]
    out_specs = [pl.BlockSpec(memory_space=out.memory_space) for out in outs]
    run = pl.pallas_call(
        kernel,
        out_shape=outs,
        in_specs=in_specs,
        out_specs=out_specs,
        scratch_shapes=list(scratch),
        input_output_aliases=aliases or {},
        compiler_params=pltpu.CompilerParams(vmem_limit_bytes=VMEM_LIMIT),
        cost_estimate=pl.CostEstimate(
            flops=int(work * SCALE * 1e9), bytes_accessed=1, transcendentals=0
        ),
        name=name,
    )

    def placed(*operands):
        operands = [
            pltpu.with_memory_space_constraint(value, spec.memory_space)
            for value, spec in zip(operands, in_specs)
        ]
        result = run(*operands)
        return result if isinstance(out_shape, list) else result[0]

    return placed


def cuts(whole, parts):
    return [pl.ds(at * (whole // parts), whole // parts) for at in range(parts)]


def number(numbers_ref, at, step):
    return pl.multiple_of(numbers_ref[at, 0], step)


def start_copy(source, target, sem):
    copy = pltpu.make_async_copy(source, target, sem)
    copy.start()
    return copy


def split(rows, width):
    count, steps = rows.shape
    parts = []
    for _ in range(3):
        part = rows.astype(BF16).astype(F32)
        parts.append(part)
        rows = rows - part
    parts.append(jnp.zeros((16 - 3 * count, steps), F32))
    out = jnp.concatenate(parts, axis=0)
    if width > steps:
        out = jnp.concatenate([out, jnp.zeros((16, width - steps), F32)], axis=1)
    return out.astype(BF16)


def joined(parts, steps):
    wide = parts[:, :steps].astype(F32)
    return wide[:2] + wide[2:4] + wide[4:6]


def load_first(source, weights, starts, half):
    steps, units = source.shape
    spans = 4
    width = units // spans

    def kernel(starts_ref, source_ref, weights_ref, sent_ref, hidden_ref, held, pre, total, sems):
        rows = pl.ds(number(starts_ref, 0, half), half)

        def copies(at):
            span = pl.ds(pl.multiple_of(at * width, width), width)
            return span, (
                pltpu.make_async_copy(source_ref.at[:, span], pre.at[:, span], sems.at[0, at]),
                pltpu.make_async_copy(
                    weights_ref.at[rows, span], held.at[:, span], sems.at[1, at]
                ),
            )

        def start(at):
            for copy in copies(at)[1]:
                copy.start()

        start(0)
        start(1)
        total[...] = jnp.zeros_like(total)

        def step(at, carry):
            @pl.when(at + 2 < spans)
            def _():
                start(at + 2)

            span, pair = copies(at)
            for copy in pair:
                copy.wait()
            hidden = silu(pre[:, span])
            hidden_ref[:, span] = hidden
            total[...] += lax.dot_general(
                hidden, held[:, span], NT, preferred_element_type=F32
            )
            return carry

        lax.fori_loop(0, spans, step, 0)
        sent_ref[...] = total[...].astype(BF16)

    return call(
        kernel,
        [
            in_vmem((steps, half), BF16),
            in_vmem((steps, units), BF16),
            in_vmem((half, units), BF16),
            in_vmem((steps, units), BF16),
        ],
        [VMEM, HBM, HBM],
        [pltpu.VMEM((steps, half), F32), pltpu.SemaphoreType.DMA((2, spans))],
        work=3.2, name="load_first",
    )(starts, source, weights)


def load_second(source, weights, starts, held, own_sent):
    steps, units = source.shape
    half = held.shape[0]

    def kernel(
        starts_ref, source_ref, weights_ref, held_ref, own_ref, out_ref, hidden_ref, block, sem
    ):
        first = number(starts_ref, 1, half)
        copy = start_copy(weights_ref.at[pl.ds(first, half), :], block, sem)

        @pl.when(first >= 0)
        def _():
            out_ref[pl.ds(0, steps), :] = own_ref[...]
            total = None
            for span in cuts(units, 4):
                hidden = silu(source_ref[:, span])
                hidden_ref[:, span] = hidden
                term = lax.dot_general(hidden, held_ref[:, span], NT, preferred_element_type=F32)
                total = term if total is None else total + term
            out_ref[pl.ds(steps, steps), :] = total.astype(BF16)

        copy.wait()

    return call(
        kernel,
        [
            in_vmem((2 * steps, half), BF16),
            in_vmem((steps, units), BF16),
            in_vmem((half, units), BF16),
        ],
        [VMEM, VMEM, HBM, VMEM, VMEM],
        [pltpu.SemaphoreType.DMA],
        work=1.6, name="load_second",
    )(starts, source, weights, held, own_sent)


def project(hidden, rows, out_type, weights, starts, following):
    steps, units = hidden[0].shape
    half = rows.shape[0]
    more = following is not None

    def products(hidden_refs, rows_ref, out_ref):
        for at, hidden_ref in enumerate(hidden_refs):
            total = lax.dot_general(
                hidden_ref[...], rows_ref[...], NT, preferred_element_type=F32
            )
            out_ref[pl.ds(at * steps, steps), :] = total.astype(out_type)

    def kernel(first, second, rows_ref, out_ref):
        products((first, second), rows_ref, out_ref)

    def loading(starts_ref, weights_ref, first, second, rows_ref, out_ref, block, sem):
        start = number(starts_ref, following, half)
        copy = start_copy(weights_ref.at[pl.ds(start, half), :], block, sem)

        @pl.when(start >= 0)
        def _():
            products((first, second), rows_ref, out_ref)

        copy.wait()

    out_shape = in_vmem((2 * steps, half), out_type)
    if not more:
        return [call(kernel, out_shape, [VMEM] * 3, work=1.6, name="project")(*hidden, rows)]
    return call(
        loading,
        [out_shape, in_vmem((half, units), BF16)],
        [VMEM, HBM, VMEM, VMEM, VMEM],
        [pltpu.SemaphoreType.DMA],
        work=1.6, name="project",
    )(starts, weights, *hidden, rows)


def lane_sums(value):
    width = value.shape[1]
    if width % 128 == 0:
        squares = value * value
        squares = sum(squares[:, at : at + 128] for at in range(0, width, 128))
        return jnp.sum(squares.T, axis=0, keepdims=True)
    ones = jnp.ones((8, value.shape[1]), F32)
    sums = lax.dot_general(
        ones, value * value, NT, precision=lax.Precision.HIGHEST, preferred_element_type=F32
    )
    return sums[:1]


def half_of(place, steps):
    return pl.ds(pl.multiple_of(place * steps, steps), steps)


def predicted_of(kept, arriving, starts, squares, packed):
    steps, width = kept.shape[0] // 2, kept.shape[1]

    def kernel(starts_ref, kept_ref, arriving_ref, *refs):
        sent_ref, total_ref, squares_ref = refs[-3:]
        rows = []
        for at in range(2):
            part = pl.ds(at * steps, steps)
            total = kept_ref[part, :] + arriving_ref[part, :].astype(F32)
            total_ref[part, :] = total
            rows.append(lane_sums(total))
        sent_ref[pl.ds(0, steps), :] = total_ref[half_of(1 - starts_ref[7, 0], steps), :].astype(BF16)
        both = jnp.concatenate(rows, axis=0)
        if squares is not None:
            both += refs[0][...]
        squares_ref[...] = both
        if packed:
            sent_ref[pl.ds(steps, 16), :] = split(both, width)

    shapes = [
        in_vmem((steps + 16 * packed, width), BF16),
        in_vmem((2 * steps, width), F32),
        in_vmem((2, steps), F32),
    ]
    more = [] if squares is None else [squares]
    return call(kernel, shapes, [VMEM] + [VMEM] * (2 + len(more)), work=0.2, name="predicted")(
        starts, kept, arriving, *more
    )


def sum_of(total, arriving, starts, squares, packed, out_packed):
    steps, width = arriving.shape[0] - 16 * packed, arriving.shape[1]

    def kernel(starts_ref, total_ref, arriving_ref, squares_ref, sent_ref, out_ref, both_ref):
        held = total_ref[half_of(starts_ref[7, 0], steps), :] if total.shape[0] > steps else total_ref[...]
        out = held + arriving_ref[pl.ds(0, steps), :].astype(F32)
        sent_ref[pl.ds(0, steps), :] = out.astype(BF16)
        out_ref[...] = out
        both = squares_ref[...]
        if packed:
            both += joined(arriving_ref[pl.ds(steps, 16), :], both.shape[1])
        both_ref[...] = both
        if out_packed:
            sent_ref[pl.ds(steps, 16), :] = split(both, width)

    shapes = [
        in_vmem((steps + 16 * out_packed, width), BF16),
        in_vmem((steps, width), F32),
        in_vmem(squares.shape, F32),
    ]
    return call(kernel, shapes, [VMEM, VMEM, VMEM, VMEM], name="sum_of")(
        starts, total, arriving, squares
    )


def gradient_of(total, arriving, predicted, starts, cotangents, before, members, factor, packed):
    steps, width = total.shape
    last, previous = before

    def kernel(starts_ref, total_ref, arriving_ref, predicted_ref, own, other, *refs):
        grad_ref, sums_ref, mean_ref = refs[-3:]
        mean_ref[half_of(starts_ref[7, 0], steps), :] = total_ref[...] / members
        mean_ref[half_of(1 - starts_ref[7, 0], steps), :] = arriving_ref[...].astype(F32) / members
        rows = []
        for at, cotangent_ref in enumerate((own, other)):
            part = pl.ds(at * steps, steps)
            mean = mean_ref[part, :]
            weighting = cotangent_ref[:, :1].astype(F32) * factor
            grad_ref[part, :] = (weighting * (predicted_ref[part, :] - mean)).astype(BF16)
            rows.append(lane_sums(mean))
        both = jnp.concatenate(rows, axis=0)
        if previous is not None:
            both += refs[0][...]
        if last is not None:
            both = refs[-4][...] / members - both
        sums_ref[...] = both
        if packed:
            grad_ref[pl.ds(2 * steps, 16), :] = split(both, width)

    shapes = [in_vmem((2 * steps + 16 * packed, width), BF16), in_vmem((2, steps), F32)]
    more = [value for value in (previous, last) if value is not None]
    return call(
        kernel,
        shapes,
        [VMEM] + [VMEM] * (5 + len(more)),
        [pltpu.VMEM((2 * steps, width), F32)],
        work=0.3, name="gradient",
    )(starts, total, arriving, predicted, *cotangents, *more)


def plus(first, second):
    def kernel(first_ref, second_ref, out_ref):
        out_ref[...] = first_ref[...] + second_ref[...]

    return call(kernel, in_vmem(first.shape, F32), [VMEM, VMEM], name="plus")(first, second)


def leave_to_other(grad, rows, before, spread, arriving_spread, steps):
    units = rows.shape[1]
    packed = arriving_spread.shape[0] > 2

    def kernel(grad_ref, rows_ref, before_ref, spread_ref, arriving_ref, out_ref, sum_ref):
        for span in cuts(units, 4):
            term = jnp.dot(
                grad_ref[pl.ds(steps, steps), :], rows_ref[:, span], preferred_element_type=F32
            )
            out_ref[pl.ds(0, steps), span] = (before_ref[:, span] + term).astype(BF16)
        if packed:
            both = spread_ref[...] + joined(arriving_ref[pl.ds(2 * steps, 16), :], steps)
        else:
            both = spread_ref[...] + arriving_ref[...]
        sum_ref[...] = both
        out_ref[pl.ds(steps, 16), :] = split(both, units)

    shapes = [in_vmem((steps + 16, units), BF16), in_vmem((2, steps), F32)]
    return call(kernel, shapes, [VMEM] * 5, work=0.6, name="leave_to_other")(
        grad, rows, before, spread, arriving_spread
    )


def block_rows(grad, hidden, steps, rows):
    total = lax.dot_general(
        grad[pl.ds(0, steps), rows], hidden[0][...], TN, preferred_element_type=F32
    )
    total += lax.dot_general(
        grad[pl.ds(steps, steps), rows], hidden[1][...], TN, preferred_element_type=F32
    )
    return total.astype(BF16)


def write_rows(start, grad, hidden, steps, made, out_ref, sems):
    half = made.shape[0]
    copies = []
    for at, rows in enumerate(cuts(half, 2)):
        made[rows, :] = block_rows(grad, hidden, steps, rows)
        to = pl.ds(pl.multiple_of(start + rows.start, rows.size), rows.size)
        copies.append(start_copy(made.at[rows, :], out_ref.at[to, :], sems.at[at]))
    return copies


def weight_rows(grads, hidden, starts, blocks, features, started=None, back=()):
    half, (steps, units) = grads[0].shape[1], hidden[0].shape
    more = [] if started is None else [started]
    operands, plan = [], []
    for part, pairs, before in back:
        plan.append((part, len(pairs), before is not None))
        operands += [value for pair in pairs for value in pair]
        operands += [] if before is None else [before]

    def kernel(starts_ref, *refs):
        refs = list(refs)
        take = lambda count: [refs.pop(0) for _ in range(count)]
        grad_refs, hidden_refs, operand_refs = take(len(grads)), take(2), take(len(operands))
        take(len(more))
        (out_ref,), sum_refs, (made, sems) = take(1), take(len(back)), take(2)
        copies = []
        for at, (block, grad) in enumerate(zip(blocks, grad_refs)):
            copies += write_rows(
                starts_ref[block, 0],
                grad,
                hidden_refs,
                steps,
                made.at[at],
                out_ref,
                sems.at[at],
            )
        for (part, count, added), sum_ref in zip(plan, sum_refs):
            pairs = [(operand_refs.pop(0), operand_refs.pop(0)) for _ in range(count)]
            before_ref = operand_refs.pop(0) if added else None
            for span in cuts(units, 4):
                out = before_ref[:, span] if added else None
                for grad, rows in pairs:
                    term = jnp.dot(
                        grad[pl.ds(part * steps, steps), :],
                        rows[:, span],
                        preferred_element_type=F32,
                    )
                    out = term if out is None else out + term
                sum_ref[:, span] = out
        for copy in copies:
            copy.wait()

    result = call(
        kernel,
        [in_hbm((features, units), BF16)] + [in_vmem((steps, units), F32)] * len(back),
        [VMEM] * (3 + len(grads) + len(operands)) + [HBM] * len(more),
        [
            pltpu.VMEM((len(grads), half, units), BF16),
            pltpu.SemaphoreType.DMA((len(grads), 2)),
        ],
        aliases={3 + len(grads) + len(operands): 0} if more else None,
        work=2 * len(grads) + len(back), name="weight_rows",
    )(starts, *grads, *hidden, *operands, *more)
    return result


def last_grads(before, arrived, pre_act, spread, model_width):
    steps, units = before.shape
    lanes = -(-steps // 128) * 128

    def kernel(before_ref, arrived_ref, pre, spread_ref, act_ref, reward_ref, act, reward, sems):
        others = joined(arrived_ref[pl.ds(steps, 16), pl.ds(0, lanes)], steps)
        reward[...] = (spread_ref[...][:1] + others[1:]) / model_width
        copies = [start_copy(reward, reward_ref, sems.at[4])]
        for at, span in enumerate(cuts(units, 4)):
            wide = pre[:, span].astype(F32)
            gate = sigmoid(wide)
            slope = gate * (1.0 + wide * (1.0 - gate))
            total = before_ref[:, span] + arrived_ref[pl.ds(0, steps), span].astype(F32)
            act[:, span] = (total * slope).astype(BF16)
            copies.append(start_copy(act.at[:, span], act_ref.at[:, span], sems.at[at]))
        for copy in copies:
            copy.wait()

    return call(
        kernel,
        [in_hbm((steps, units), BF16), in_hbm((1, steps), F32)],
        [VMEM] * 4,
        [
            pltpu.VMEM((steps, units), BF16),
            pltpu.VMEM((1, steps), F32),
            pltpu.SemaphoreType.DMA((5,)),
        ],
        work=1.9, name="last_grads",
    )(before, arrived, pre_act, spread)


class Order:
    def __init__(self):
        self.last = None

    def __call__(self, step, *values):
        if self.last is not None:
            values, _ = lax.optimization_barrier((values, self.last))
        result = step(*values)
        self.last = jax.tree.leaves(result)[0]
        return result


class Piece:
    def __init__(self, order, starts, last, previous):
        self.order, self.starts = order, starts
        self.last, self.previous = last, previous
        self.tensor = lax.axis_index("tensor")

    def leave(self, sent):
        self.arriving = swap(sent, "tensor", shares(lax.axis_size("tensor"))[-1])

    def scatter_rest(self):
        def add(total, arriving):
            return total + arriving.astype(F32)

        for distance in reversed(shares(lax.axis_size("tensor"))[:-1]):
            half = self.total.shape[1] // 2
            high = (self.tensor // distance) % 2
            total = self.order(add, self.total, self.arriving)
            sent = lax.dynamic_slice_in_dim(total, (1 - high) * half, half, 1)
            self.total = lax.dynamic_slice_in_dim(total, high * half, half, 1)
            self.arriving = swap(sent.astype(BF16), "tensor", distance)

    def predict(self):
        steps, width = self.total.shape[0] // 2, self.total.shape[1]
        self.packed = self.last and width >= steps
        before = None if self.previous is None else self.previous.squares
        sent, self.predicted, self.squares = self.order(
            lambda kept, arriving: predicted_of(kept, arriving, self.starts, before, self.packed),
            self.total,
            self.arriving,
        )
        self.sum = self.predicted
        near, *self.far = shares(lax.axis_size("ensemble"))
        self.arriving = swap(sent, "ensemble", near)
        self.exchange_squares(near)

    def exchange_squares(self, distance):
        self.squares_arriving = None
        if self.last and not self.packed:
            self.squares_arriving = swap(self.squares, "ensemble", distance)

    def ensemble_steps(self):
        packed = self.packed
        for distance in self.far + [None]:
            out_packed = self.packed and distance is not None
            sent, self.sum, squares = self.order(
                lambda total, arriving: sum_of(
                    total, arriving, self.starts, self.squares, packed, out_packed
                ),
                self.sum,
                self.arriving,
            )
            if self.squares_arriving is not None:
                squares = self.order(plus, squares, self.squares_arriving)
            self.squares = squares
            if distance is not None:
                self.arriving = swap(sent, "ensemble", distance)
                self.exchange_squares(distance)
                yield
            else:
                self.arriving = swap(sent, "ensemble", 1)

    def gradient(self, cotangents, members, factor):
        def join(share, other, distance):
            high = (self.tensor // distance) % 2
            first = jnp.where(high == 0, share, other)
            second = jnp.where(high == 0, other, share)
            return jnp.concatenate([first, second], axis=1)

        *near, far = shares(lax.axis_size("tensor"))
        packed = self.last and not near and self.sum.shape[1] >= self.sum.shape[0]
        before = (
            self.squares if self.last else None,
            None if self.previous is None else self.previous.sums,
        )
        self.share, self.sums = self.order(
            lambda total, arriving: gradient_of(
                total,
                arriving,
                self.predicted,
                self.starts,
                cotangents,
                before,
                members,
                factor,
                packed,
            ),
            self.sum,
            self.arriving,
        )
        for distance in near:
            other = swap(self.share, "tensor", distance)
            self.share = self.order(functools.partial(join, distance=distance), self.share, other)
        self.other = swap(self.share, "tensor", far)
        if self.last and not packed:
            for distance in near:
                self.sums = self.order(plus, self.sums, swap(self.sums, "tensor", distance))
            self.other_sums = swap(self.sums, "tensor", far)
        else:
            self.other_sums = self.other


def body(pre_act, weights, cotangent):
    pre_act, weights = pre_act[:, 0, :], weights[0]
    steps, features = pre_act.shape[0], weights.shape[0]
    members = lax.axis_size("ensemble")
    model_width = features * lax.axis_size("seq")
    factor = 2.0 / (members * model_width)
    half = features // (2 * PIECES)
    far = shares(lax.axis_size("tensor"))[-1]
    high = (lax.axis_index("tensor") // far) % 2
    starts = []
    for piece in range(PIECES):
        starts += [(2 * piece + 1 - high) * half, (2 * piece + high) * half]
    assert len(starts) < 8
    starts += [0] * (7 - len(starts)) + [lax.axis_index("ensemble") % 2]
    starts = jnp.broadcast_to(jnp.stack(starts).astype(jnp.int32)[:, None], (8, 128))

    pre_other = swap(pre_act, "seq", 1)
    pre_act, starts = lax.optimization_barrier((pre_act, starts))
    order = Order()
    pieces = []
    for at in range(PIECES):
        previous = pieces[-1] if pieces else None
        pieces.append(Piece(order, starts, at == PIECES - 1, previous))
    blocks = [None] * (2 * PIECES)
    own_sent, hidden, blocks[0], pre_act = order(
        lambda p: load_first(p, weights, starts, half), pre_act
    )
    sent, hidden_other, blocks[1] = order(
        lambda p, s: load_second(p, weights, starts, blocks[0], s), pre_other, own_sent
    )
    both = [hidden, hidden_other]
    pieces[0].leave(sent)
    for at in range(1, 2 * PIECES):
        out_type = F32 if at % 2 else BF16
        out = order(
            lambda rows: project(
                both, rows, out_type, weights, starts, at + 1 if at + 1 < 2 * PIECES else None
            ),
            blocks[at],
        )
        if at + 1 < 2 * PIECES:
            blocks[at + 1] = out[1]
        if at % 2:
            pieces[at // 2].total = out[0]
        else:
            pieces[at // 2].leave(out[0])

    wide = order(lambda c: jnp.broadcast_to(c[:, None], (steps, 128)), cotangent)
    cotangents = [wide, swap(wide, "seq", 1)]
    running = []
    for piece in pieces:
        piece.scatter_rest()
        piece.predict()
        running.append(piece.ensemble_steps())
        for other in running[:-1]:
            next(other, None)
    a, b = pieces
    for other in running:
        next(other, None)
    next(running[0], None)
    a.gradient(cotangents, members, factor)
    (weight_grads,) = order(
        lambda g: weight_rows([g], both, starts, [1], features), a.share
    )
    for other in running:
        for _ in other:
            pass
    b.gradient(cotangents, members, factor)

    def middle(a_share, a_other, b_share, weight_grads):
        pairs = [(a_share, blocks[1]), (a_other, blocks[0]), (b_share, blocks[3])]
        back = [(1, pairs, None), (0, pairs, None)]
        return weight_rows(
            [b_share, a_other], both, starts, [3, 0], features, weight_grads, back
        )

    weight_grads, before_other, before = order(middle, a.share, a.other, b.share, weight_grads)
    leaving, spread = order(
        lambda g, s: leave_to_other(g, blocks[2], before_other, b.sums, s, steps),
        b.other,
        b.other_sums,
    )
    arrived = swap(leaving, "seq", 1)
    weight_grads, before = order(
        lambda g, s: weight_rows(
            [g], both, starts, [2], features, s, [(0, [(g, blocks[2])], before)]
        ),
        b.other,
        weight_grads,
    )
    act_grads, reward = order(
        lambda g, s: last_grads(g, s, pre_act, spread, model_width), before, arrived
    )
    return (weight_grads[None], act_grads[:, None, :], reward[0])


def solution(mesh):
    placed = (
        P(("groups", "seq"), "ensemble", "tensor"),
        P("ensemble", "seq", "tensor"),
        P(("groups", "seq")),
    )
    return jax.shard_map(
        body,
        mesh=mesh,
        in_specs=placed,
        out_specs=(
            P(("groups", "ensemble"), "seq", "tensor"),
            P(("groups", "seq"), "ensemble", "tensor"),
            P(("groups", "seq")),
        ),
        check_vma=False,
    )
```

time: 223 us -> 54.4 us (0.24)
  waiting for transfers between devices: 160 us -> 9.12 us
  matrix products: 35.8 us -> 0 us
  Pallas kernels: 0 us -> 24 us
  starting transfers between devices: 0.16 us -> 19.5 us
  between operations: 13.8 us -> 0.97 us
  blocking collectives: 8.98 us -> 0 us
  other arithmetic: 3.04 us -> 0 us
    psum x2 -> x0, waiting for transfers between devices: 123 us -> none  [the longest x1 70.5 us: spread_and_grad(): lax.psum((jnp.sum(predicted, axis=1), jnp.sum(predicted * predicted, axis...]
    dot_general x3 -> x0, matrix products: 35.8 us -> none  [the longest x1 15.1 us: body(): jnp.einsum('smd,mdf->smf', grad_pred, full_weights, preferred_element_typ...]
    all_gather x1 -> x0, waiting for transfers between devices: 34.2 us -> none  [body(): full_weights = lax.all_gather(weights, 'seq', axis=1, tiled=True)]
    pallas_call x0 -> x18, Pallas kernels: none -> 24 us  [placed(): result = run(*operands)]
    ppermute x0 -> x13, starting transfers between devices: none -> 19.5 us  [swap(): return lax.ppermute(value, axis, [(i, i ^ distance) for i in range(size)])]
    ppermute x0 -> x13, waiting for transfers between devices: none -> 9.12 us  [swap(): return lax.ppermute(value, axis, [(i, i ^ distance) for i in range(size)])]
    psum x1 -> x0, blocking collectives: 8.98 us -> none  [spread_and_grad(): lax.psum((jnp.sum(predicted, axis=1), jnp.sum(predicted * predicted, axis...]
    reduce_sum x2 -> x0, other arithmetic: 2.46 us -> none  [the longest x1 2.22 us: spread_and_grad(): jnp.sum(predicted * predicted, axis=(1, 2))]
  transfers between devices with their start and end apart: 4 -> 13, of which waited for: 4 -> 8; matrix products, arithmetic and copies ran while one was open for 7% -> 0% of each run, Pallas kernels for 0% -> 37%
where the time goes in v2:
time: 54.4 us; the launch traced here: 53.9 us
  Pallas kernels  24 us (44%)
  starting transfers between devices  19.5 us (36%)
  waiting for transfers between devices  9.12 us (17%)
  between operations  0.97 us (2%)
    pallas_call x18, Pallas kernels, placed(): result = run(*operands)  24 us
    ppermute x13, starting transfers between devices, swap(): return lax.ppermute(value, axis, [(i, i ^ distance) for i in range(size)])  19.5 us
    ppermute x13, waiting for transfers between devices, swap(): return lax.ppermute(value, axis, [(i, i ^ distance) for i in range(size)])  9.12 us
  transfers between devices with their start and end apart: 13, of which 8 were waited for; matrix products, arithmetic and copies ran while one was open for 0% of the time, Pallas kernels for 37%

profile of v2, /device:TPU:1, one launch (start us, length us, event | category | flops | bytes accessed | tf_op | source)
XLA Modules:
  0.0 53.9 jit_solution(6617972763016789414)
XLA Ops:
  0.6 0.1 collective-permute-start
  0.8 0.1 stack.23
  0.8 0.1 broadcast_in_dim.8.starts_ref
  0.9 3.2 %load_first.1 = (bf16[192,256]{1,0:T(8,128)(2,1)S(1)}, bf16[192,4096]{1,0:T(8,128)(2,1)S(1)}, bf16[256,4096]{1,0:T(8,128)(2,1)S(1)}, bf16[192,4096]{1,0:T(8,128)(2,1)S(1)}) custom-call(s32[8,128]{1,0:T(8,128)S(1)} %broadcast_in_dim.8.starts_ref, bf16[192,4096]{1,0:T(8,128)(2,1)} %bitcast.16, bf16[1024,4096]{1,0:T(8,128)(2,1)} %bitcast.10), custom_call_target="tpu_custom_call" | custom-call | flops 640000000 | bytes 1 | tf_op jit(solution)/shard_map/load_first/pallas_call | solution.py:70
  4.1 0.2 collective-permute-done.source_ref
  4.3 1.6 %load_second.1 = (bf16[384,256]{1,0:T(8,128)(2,1)S(1)}, bf16[192,4096]{1,0:T(8,128)(2,1)S(1)}, bf16[256,4096]{1,0:T(8,128)(2,1)S(1)}) custom-call(s32[8,128]{1,0:T(8,128)S(1)} %broadcast_in_dim.8.starts_ref, bf16[192,4096]{1,0:T(8,128)(2,1)S(1)} %collective-permute-done.source_ref, bf16[1024,4096]{1,0:T(8,128)(2,1)} %bitcast.11, ...), custom_call_target="tpu_custom_call" | custom-call | flops 320000000 | bytes 1 | tf_op jit(solution)/shard_map/load_second/pallas_call | solution.py:70
  6.0 2.6 %collective-permute-start.2 = (bf16[384,256]{1,0:T(8,128)(2,1)S(1)}, bf16[384,256]{1,0:T(8,128)(2,1)S(1)}, u32[]{:S(2)}, u32[]{:S(2)}) collective-permute-start(bf16[384,256]{1,0:T(8,128)(2,1)S(1)} %get-tuple-element.88), channel_id=1, source_target_pairs={{0,2},{2,0},{1,3},{3,1},{4,6},{6,4},{5,7},{7,5},{8,10},{10,8},{9,1... | collective-permute-start | bytes 589832 | tf_op jit(solution)/shard_map/ppermute | solution.py:20
  8.5 1.6 %project.3 = (f32[384,256]{1,0:T(8,128)S(1)}, bf16[256,4096]{1,0:T(8,128)(2,1)S(1)}) custom-call(s32[8,128]{1,0:T(8,128)S(1)} %broadcast_in_dim.8.starts_ref, bf16[1024,4096]{1,0:T(8,128)(2,1)} %bitcast.12, bf16[192,4096]{1,0:T(8,128)(2,1)S(1)} %get-tuple-element.81.first.refs_1_.refs_2_, bf16[192,4096]{1,0:T(8,128)(2,1)S(1)} %get-tuple-element.86.second.refs_2_.refs_3_, ...), custom_call_target="tpu_custom_call" | custom-call | flops 320000000 | bytes 1 | tf_op jit(solution)/shard_map/project/pallas_call | solution.py:70
  10.2 1.8 %project.4 = (bf16[384,256]{1,0:T(8,128)(2,1)S(1)}, bf16[256,4096]{1,0:T(8,128)(2,1)S(1)}) custom-call(s32[8,128]{1,0:T(8,128)S(1)} %broadcast_in_dim.8.starts_ref, bf16[1024,4096]{1,0:T(8,128)(2,1)} %bitcast.13, bf16[192,4096]{1,0:T(8,128)(2,1)S(1)} %get-tuple-element.81.first.refs_1_.refs_2_, ...), custom_call_target="tpu_custom_call" | custom-call | flops 320000000 | bytes 1 | tf_op jit(solution)/shard_map/project/pallas_call | solution.py:70
  11.9 0.1 collective-permute-start.1
  12.0 0.0 copy-start
  12.0 1.5 %project.5.kept_ref = f32[384,256]{1,0:T(8,128)S(1)} custom-call(bf16[192,4096]{1,0:T(8,128)(2,1)S(1)} %get-tuple-element.81.first.refs_1_.refs_2_, bf16[192,4096]{1,0:T(8,128)(2,1)S(1)} %get-tuple-element.86.second.refs_2_.refs_3_, bf16[256,4096]{1,0:T(8,128)(2,1)S(1)} %get-tuple-element.95.rows_ref.refs_9_.refs_15_), custom_call_target="tpu_custom_call" | custom-call | flops 320000000 | bytes 1 | tf_op jit(solution)/shard_map/project/pallas_call | solution.py:70
  13.5 0.1 collective-permute-done.2.arriving_ref
  13.6 0.0 copy-done
  13.6 0.1 broadcast_in_dim.9.own
  13.7 0.2 predicted.2
  13.9 1.5 %collective-permute-start.4 = (bf16[192,256]{1,0:T(8,128)(2,1)S(1)}, bf16[192,256]{1,0:T(8,128)(2,1)S(1)}, u32[]{:S(2)}, u32[]{:S(2)}) collective-permute-start(bf16[192,256]{1,0:T(8,128)(2,1)S(1)} %get-tuple-element.99), channel_id=1, source_target_pairs={{0,4},{4,0},{8,12},{12,8},{1,5},{5,1},{9,13},{13,9},{2,6},{6,2},{1... | collective-permute-start | bytes 294920 | tf_op jit(solution)/shard_map/ppermute | solution.py:20
  15.4 2.5 %collective-permute-done.1.arriving_ref = bf16[384,256]{1,0:T(8,128)(2,1)S(1)} collective-permute-done((bf16[384,256]{1,0:T(8,128)(2,1)S(1)}, bf16[384,256]{1,0:T(8,128)(2,1)S(1)}, u32[]{:S(2)}, u32[]{:S(2)}) %collective-permute-start.1) | collective-permute-done | bytes 196640 | tf_op jit(solution)/shard_map/ppermute | solution.py:20
  17.9 0.2 predicted.3
  18.1 0.0 collective-permute-done.4.arriving_ref
  18.1 0.1 sum_of.4
  18.2 2.4 %collective-permute-start.5 = (bf16[192,256]{1,0:T(8,128)(2,1)S(1)}, bf16[192,256]{1,0:T(8,128)(2,1)S(1)}, u32[]{:S(2)}, u32[]{:S(2)}) collective-permute-start(bf16[192,256]{1,0:T(8,128)(2,1)S(1)} %get-tuple-element.109), channel_id=1, source_target_pairs={{0,8},{4,12},{8,0},{12,4},{1,9},{5,13},{9,1},{13,5},{2,10},{6,14},... | collective-permute-start | bytes 294920 | tf_op jit(solution)/shard_map/ppermute | solution.py:20
  20.6 1.3 %collective-permute-start.3 = (bf16[208,256]{1,0:T(8,128)(2,1)S(1)}, bf16[208,256]{1,0:T(8,128)(2,1)S(1)}, u32[]{:S(2)}, u32[]{:S(2)}) collective-permute-start(bf16[208,256]{1,0:T(8,128)(2,1)S(1)} %get-tuple-element.104), channel_id=1, source_target_pairs={{0,4},{4,0},{8,12},{12,8},{1,5},{5,1},{9,13},{13,9},{2,6},{6,2},{1... | collective-permute-start | bytes 319496 | tf_op jit(solution)/shard_map/ppermute | solution.py:20
  21.9 0.8 %collective-permute-done.5.arriving_ref = bf16[192,256]{1,0:T(8,128)(2,1)S(1)} collective-permute-done((bf16[192,256]{1,0:T(8,128)(2,1)S(1)}, bf16[192,256]{1,0:T(8,128)(2,1)S(1)}, u32[]{:S(2)}, u32[]{:S(2)}) %collective-permute-start.5) | collective-permute-done | bytes 98336 | tf_op jit(solution)/shard_map/ppermute | solution.py:20
  22.6 0.6 %sum_of.5 = (bf16[192,256]{1,0:T(8,128)(2,1)S(1)}, f32[192,256]{1,0:T(8,128)S(1)}, f32[2,192]{1,0:T(2,128)}) custom-call(s32[8,128]{1,0:T(8,128)S(1)} %broadcast_in_dim.8.starts_ref, f32[192,256]{1,0:T(8,128)S(1)} %get-tuple-element.110.total_ref, bf16[192,256]{1,0:T(8,128)(2,1)S(1)} %collective-permute-done.5.arriving_ref, ...), custom_call_target="tpu_custom_call" | custom-call | flops 20000000 | bytes 1 | tf_op jit(solution)/shard_map/sum_of/pallas_call | solution.py:70
  23.2 1.7 %collective-permute-start.7 = (bf16[192,256]{1,0:T(8,128)(2,1)S(1)}, bf16[192,256]{1,0:T(8,128)(2,1)S(1)}, u32[]{:S(2)}, u32[]{:S(2)}) collective-permute-start(bf16[192,256]{1,0:T(8,128)(2,1)S(1)} %get-tuple-element.113), channel_id=1, source_target_pairs={{0,4},{4,0},{8,12},{12,8},{1,5},{5,1},{9,13},{13,9},{2,6},{6,2},{1... | collective-permute-start | bytes 294920 | tf_op jit(solution)/shard_map/ppermute | solution.py:20
  25.0 0.2 collective-permute-done.3.arriving_ref
  25.2 0.1 sum_of.6
  25.3 3.2 %collective-permute-start.6 = (bf16[208,256]{1,0:T(8,128)(2,1)S(1)}, bf16[208,256]{1,0:T(8,128)(2,1)S(1)}, u32[]{:S(2)}, u32[]{:S(2)}) collective-permute-start(bf16[208,256]{1,0:T(8,128)(2,1)S(1)} %get-tuple-element.118), channel_id=1, source_target_pairs={{0,8},{4,12},{8,0},{12,4},{1,9},{5,13},{9,1},{13,5},{2,10},{6,14},... | collective-permute-start | bytes 319496 | tf_op jit(solution)/shard_map/ppermute | solution.py:20
  28.5 2.8 %collective-permute-start.8 = (bf16[192,128]{1,0:T(8,128)(2,1)S(1)}, bf16[192,128]{1,0:T(8,128)(2,1)S(1)}, u32[]{:S(2)}, u32[]{:S(2)}) collective-permute-start(bf16[192,128]{1,0:T(8,128)(2,1)S(1)} %broadcast_in_dim.9.own), channel_id=1, source_target_pairs={{0,1},{1,0},{2,3},{3,2},{4,5},{5,4},{6,7},{7,6},{8,9},{9,8},{10,11... | collective-permute-start | bytes 147464 | tf_op jit(solution)/shard_map/ppermute | solution.py:20
  31.3 0.0 collective-permute-done.7.arriving_ref
  31.3 0.9 %collective-permute-done.8.other = bf16[192,128]{1,0:T(8,128)(2,1)S(1)} collective-permute-done((bf16[192,128]{1,0:T(8,128)(2,1)S(1)}, bf16[192,128]{1,0:T(8,128)(2,1)S(1)}, u32[]{:S(2)}, u32[]{:S(2)}) %collective-permute-start.8) | collective-permute-done | bytes 49184 | tf_op jit(solution)/shard_map/ppermute | solution.py:20
  32.2 0.3 gradient.2
  32.5 1.5 %collective-permute-start.11 = (bf16[384,256]{1,0:T(8,128)(2,1)S(1)}, bf16[384,256]{1,0:T(8,128)(2,1)S(1)}, u32[]{:S(2)}, u32[]{:S(2)}) collective-permute-start(bf16[384,256]{1,0:T(8,128)(2,1)S(1)} %get-tuple-element.136.refs_0_.refs_4_.refs_10_), channel_id=1, source_target_pairs={{0,2},{2,0},{1,3},{3,1},{4,6},{6,4},{5,7},{7,5},{8,10},{10,8},{9,1... | collective-permute-start | bytes 589832 | tf_op jit(solution)/shard_map/ppermute | solution.py:20
  34.0 2.3 %weight_rows.3.refs_16_ = bf16[1024,4096]{1,0:T(8,128)(2,1)} custom-call(s32[8,128]{1,0:T(8,128)S(1)} %broadcast_in_dim.8.starts_ref, bf16[384,256]{1,0:T(8,128)(2,1)S(1)} %get-tuple-element.136.refs_0_.refs_4_.refs_10_, bf16[192,4096]{1,0:T(8,128)(2,1)S(1)} %get-tuple-element.81.first.refs_1_.refs_2_, ...), custom_call_target="tpu_custom_call" | custom-call | flops 400000000 | bytes 1 | tf_op jit(solution)/shard_map/weight_rows/pallas_call | solution.py:70
  36.3 0.0 collective-permute-done.6.arriving_ref
  36.3 0.1 collective-permute-start.9
  36.4 3.5 %collective-permute-done.9.arriving_ref = bf16[192,256]{1,0:T(8,128)(2,1)S(1)} collective-permute-done((bf16[192,256]{1,0:T(8,128)(2,1)S(1)}, bf16[192,256]{1,0:T(8,128)(2,1)S(1)}, u32[]{:S(2)}, u32[]{:S(2)}) %collective-permute-start.9) | collective-permute-done | bytes 98336 | tf_op jit(solution)/shard_map/ppermute | solution.py:20
  39.9 0.3 gradient.3
  40.2 0.4 collective-permute-start.10
  40.6 0.0 collective-permute-done.11.refs_1_.refs_6_.refs_12_
  40.6 5.5 %weight_rows.4 = (bf16[1024,4096]{1,0:T(8,128)(2,1)}, f32[192,4096]{1,0:T(8,128)S(1)}, f32[192,4096]{1,0:T(8,128)S(1)}) custom-call(s32[8,128]{1,0:T(8,128)S(1)} %broadcast_in_dim.8.starts_ref, bf16[400,256]{1,0:T(8,128)(2,1)S(1)} %get-tuple-element.134.refs_0_.refs_8_.refs_14_, ...), custom_call_target="tpu_custom_call", output_to_operand_aliasing={{0}: (17, {})} | custom-call | flops 1200000000 | bytes 1 | tf_op jit(solution)/shard_map/weight_rows/pallas_call | solution.py:70
  46.1 0.0 collective-permute-done.10.grad_ref.arriving_ref.refs_0_.refs_3_
  46.1 0.6 %leave_to_other.1 = (bf16[208,4096]{1,0:T(8,128)(2,1)S(1)}, f32[2,192]{1,0:T(2,128)S(1)}) custom-call(bf16[400,256]{1,0:T(8,128)(2,1)S(1)} %collective-permute-done.10.grad_ref.arriving_ref.refs_0_.refs_3_, bf16[256,4096]{1,0:T(8,128)(2,1)S(1)} %get-tuple-element.92.rows_ref.refs_4_, f32[192,4096]{1,0:T(8,128)S(1)} %get-tuple-element.140.before_ref, ...), custom_call_target="tpu_custom_call" | custom-call | flops 120000000 | bytes 1 | tf_op jit(solution)/shard_map/leave_to_other/pallas_call | solution.py:70
  46.7 1.8 %collective-permute-start.12 = (bf16[208,4096]{1,0:T(8,128)(2,1)S(1)}, bf16[208,4096]{1,0:T(8,128)(2,1)S(1)}, u32[]{:S(2)}, u32[]{:S(2)}) collective-permute-start(bf16[208,4096]{1,0:T(8,128)(2,1)S(1)} %get-tuple-element.143), channel_id=1, source_target_pairs={{0,1},{1,0},{2,3},{3,2},{4,5},{5,4},{6,7},{7,6},{8,9},{9,8},{10,11... | collective-permute-start | bytes 5111816 | tf_op jit(solution)/shard_map/ppermute | solution.py:20
  48.6 2.3 %weight_rows.5 = (bf16[1024,4096]{1,0:T(8,128)(2,1)}, f32[192,4096]{1,0:T(8,128)S(1)}) custom-call(s32[8,128]{1,0:T(8,128)S(1)} %broadcast_in_dim.8.starts_ref, bf16[400,256]{1,0:T(8,128)(2,1)S(1)} %collective-permute-done.10.grad_ref.arriving_ref.refs_0_.refs_3_, ...), custom_call_target="tpu_custom_call", output_to_operand_aliasing={{0}: (7, {})} | custom-call | flops 600000000 | bytes 1 | tf_op jit(solution)/shard_map/weight_rows/pallas_call | solution.py:70
  50.9 0.9 %collective-permute-done.12.arrived_ref = bf16[208,4096]{1,0:T(8,128)(2,1)S(1)} collective-permute-done((bf16[208,4096]{1,0:T(8,128)(2,1)S(1)}, bf16[208,4096]{1,0:T(8,128)(2,1)S(1)}, u32[]{:S(2)}, u32[]{:S(2)}) %collective-permute-start.12) | collective-permute-done | bytes 1703968 | tf_op jit(solution)/shard_map/ppermute | solution.py:20
  51.8 1.9 %last_grads.1 = (bf16[192,4096]{1,0:T(8,128)(2,1)}, f32[1,192]{1,0:T(1,128)}) custom-call(f32[192,4096]{1,0:T(8,128)S(1)} %get-tuple-element.149.before_ref, bf16[208,4096]{1,0:T(8,128)(2,1)S(1)} %collective-permute-done.12.arrived_ref, bf16[192,4096]{1,0:T(8,128)(2,1)S(1)} %get-tuple-element.151.pre, f32[2,192]{1,0:T(2,128)S(1)} %get-tuple-element.152.spread_ref), custom_call_target="tpu_custom_call" | custom-call | flops 380000000 | bytes 1 | tf_op jit(solution)/shard_map/last_grads/pallas_call | solution.py:70
  (2 shorter events, 0.0 us)
Async XLA Ops:
  0.6 3.7 %collective-permute-start = (bf16[192,4096]{1,0:T(8,128)(2,1)}, bf16[192,4096]{1,0:T(8,128)(2,1)S(1)}, u32[]{:S(2)}, u32[]{:S(2)}) collective-permute-start(bf16[192,4096]{1,0:T(8,128)(2,1)} %bitcast.15), channel_id=1, source_target_pairs={{0,1},{1,0},{2,3},{3,2},{4,5},{5,4},{6,7},{7,6},{8,9},{9,8},{10,11... | collective-permute-start | bytes 4718600 | tf_op jit(solution)/shard_map/ppermute | solution.py:20
  6.0 7.7 %collective-permute-start.2 = (bf16[384,256]{1,0:T(8,128)(2,1)S(1)}, bf16[384,256]{1,0:T(8,128)(2,1)S(1)}, u32[]{:S(2)}, u32[]{:S(2)}) collective-permute-start(bf16[384,256]{1,0:T(8,128)(2,1)S(1)} %get-tuple-element.88), channel_id=1, source_target_pairs={{0,2},{2,0},{1,3},{3,1},{4,6},{6,4},{5,7},{7,5},{8,10},{10,8},{9,1... | collective-permute-start | bytes 589832 | tf_op jit(solution)/shard_map/ppermute | solution.py:20
  11.9 6.0 %collective-permute-start.1 = (bf16[384,256]{1,0:T(8,128)(2,1)S(1)}, bf16[384,256]{1,0:T(8,128)(2,1)S(1)}, u32[]{:S(2)}, u32[]{:S(2)}) collective-permute-start(bf16[384,256]{1,0:T(8,128)(2,1)S(1)} %get-tuple-element.94), channel_id=1, source_target_pairs={{0,2},{2,0},{1,3},{3,1},{4,6},{6,4},{5,7},{7,5},{8,10},{10,8},{9,1... | collective-permute-start | bytes 589832 | tf_op jit(solution)/shard_map/ppermute | solution.py:20
  12.0 1.7 %copy-start = (bf16[192]{0:T(256)(128)(2,1)S(1)}, bf16[192]{0:T(256)(128)(2,1)}, u32[]{:S(2)}) copy-start(bf16[192]{0:T(256)(128)(2,1)} %param.5) | copy-start | bytes 1156
  13.9 4.2 %collective-permute-start.4 = (bf16[192,256]{1,0:T(8,128)(2,1)S(1)}, bf16[192,256]{1,0:T(8,128)(2,1)S(1)}, u32[]{:S(2)}, u32[]{:S(2)}) collective-permute-start(bf16[192,256]{1,0:T(8,128)(2,1)S(1)} %get-tuple-element.99), channel_id=1, source_target_pairs={{0,4},{4,0},{8,12},{12,8},{1,5},{5,1},{9,13},{13,9},{2,6},{6,2},{1... | collective-permute-start | bytes 294920 | tf_op jit(solution)/shard_map/ppermute | solution.py:20
  18.2 4.4 %collective-permute-start.5 = (bf16[192,256]{1,0:T(8,128)(2,1)S(1)}, bf16[192,256]{1,0:T(8,128)(2,1)S(1)}, u32[]{:S(2)}, u32[]{:S(2)}) collective-permute-start(bf16[192,256]{1,0:T(8,128)(2,1)S(1)} %get-tuple-element.109), channel_id=1, source_target_pairs={{0,8},{4,12},{8,0},{12,4},{1,9},{5,13},{9,1},{13,5},{2,10},{6,14},... | collective-permute-start | bytes 294920 | tf_op jit(solution)/shard_map/ppermute | solution.py:20
  20.6 4.6 %collective-permute-start.3 = (bf16[208,256]{1,0:T(8,128)(2,1)S(1)}, bf16[208,256]{1,0:T(8,128)(2,1)S(1)}, u32[]{:S(2)}, u32[]{:S(2)}) collective-permute-start(bf16[208,256]{1,0:T(8,128)(2,1)S(1)} %get-tuple-element.104), channel_id=1, source_target_pairs={{0,4},{4,0},{8,12},{12,8},{1,5},{5,1},{9,13},{13,9},{2,6},{6,2},{1... | collective-permute-start | bytes 319496 | tf_op jit(solution)/shard_map/ppermute | solution.py:20
  23.2 8.1 %collective-permute-start.7 = (bf16[192,256]{1,0:T(8,128)(2,1)S(1)}, bf16[192,256]{1,0:T(8,128)(2,1)S(1)}, u32[]{:S(2)}, u32[]{:S(2)}) collective-permute-start(bf16[192,256]{1,0:T(8,128)(2,1)S(1)} %get-tuple-element.113), channel_id=1, source_target_pairs={{0,4},{4,0},{8,12},{12,8},{1,5},{5,1},{9,13},{13,9},{2,6},{6,2},{1... | collective-permute-start | bytes 294920 | tf_op jit(solution)/shard_map/ppermute | solution.py:20
  25.3 11.0 %collective-permute-start.6 = (bf16[208,256]{1,0:T(8,128)(2,1)S(1)}, bf16[208,256]{1,0:T(8,128)(2,1)S(1)}, u32[]{:S(2)}, u32[]{:S(2)}) collective-permute-start(bf16[208,256]{1,0:T(8,128)(2,1)S(1)} %get-tuple-element.118), channel_id=1, source_target_pairs={{0,8},{4,12},{8,0},{12,4},{1,9},{5,13},{9,1},{13,5},{2,10},{6,14},... | collective-permute-start | bytes 319496 | tf_op jit(solution)/shard_map/ppermute | solution.py:20
  28.5 3.7 %collective-permute-start.8 = (bf16[192,128]{1,0:T(8,128)(2,1)S(1)}, bf16[192,128]{1,0:T(8,128)(2,1)S(1)}, u32[]{:S(2)}, u32[]{:S(2)}) collective-permute-start(bf16[192,128]{1,0:T(8,128)(2,1)S(1)} %broadcast_in_dim.9.own), channel_id=1, source_target_pairs={{0,1},{1,0},{2,3},{3,2},{4,5},{5,4},{6,7},{7,6},{8,9},{9,8},{10,11... | collective-permute-start | bytes 147464 | tf_op jit(solution)/shard_map/ppermute | solution.py:20
  32.5 8.1 %collective-permute-start.11 = (bf16[384,256]{1,0:T(8,128)(2,1)S(1)}, bf16[384,256]{1,0:T(8,128)(2,1)S(1)}, u32[]{:S(2)}, u32[]{:S(2)}) collective-permute-start(bf16[384,256]{1,0:T(8,128)(2,1)S(1)} %get-tuple-element.136.refs_0_.refs_4_.refs_10_), channel_id=1, source_target_pairs={{0,2},{2,0},{1,3},{3,1},{4,6},{6,4},{5,7},{7,5},{8,10},{10,8},{9,1... | collective-permute-start | bytes 589832 | tf_op jit(solution)/shard_map/ppermute | solution.py:20
  36.3 3.5 %collective-permute-start.9 = (bf16[192,256]{1,0:T(8,128)(2,1)S(1)}, bf16[192,256]{1,0:T(8,128)(2,1)S(1)}, u32[]{:S(2)}, u32[]{:S(2)}) collective-permute-start(bf16[192,256]{1,0:T(8,128)(2,1)S(1)} %get-tuple-element.128), channel_id=1, source_target_pairs={{0,4},{4,0},{8,12},{12,8},{1,5},{5,1},{9,13},{13,9},{2,6},{6,2},{1... | collective-permute-start | bytes 294920 | tf_op jit(solution)/shard_map/ppermute | solution.py:20
  40.2 5.9 %collective-permute-start.10 = (bf16[400,256]{1,0:T(8,128)(2,1)S(1)}, bf16[400,256]{1,0:T(8,128)(2,1)S(1)}, u32[]{:S(2)}, u32[]{:S(2)}) collective-permute-start(bf16[400,256]{1,0:T(8,128)(2,1)S(1)} %get-tuple-element.134.refs_0_.refs_8_.refs_14_), channel_id=1, source_target_pairs={{0,2},{2,0},{1,3},{3,1},{4,6},{6,4},{5,7},{7,5},{8,10},{10,8},{9,1... | collective-permute-start | bytes 614408 | tf_op jit(solution)/shard_map/ppermute | solution.py:20
  46.7 5.0 %collective-permute-start.12 = (bf16[208,4096]{1,0:T(8,128)(2,1)S(1)}, bf16[208,4096]{1,0:T(8,128)(2,1)S(1)}, u32[]{:S(2)}, u32[]{:S(2)}) collective-permute-start(bf16[208,4096]{1,0:T(8,128)(2,1)S(1)} %get-tuple-element.143), channel_id=1, source_target_pairs={{0,1},{1,0},{2,3},{3,2},{4,5},{5,4},{6,7},{7,6},{8,9},{9,8},{10,11... | collective-permute-start | bytes 5111816 | tf_op jit(solution)/shard_map/ppermute | solution.py:20

commit v3 on v2

v3 whole, which is shorter than its diff:
```python
import functools

import jax
import jax.numpy as jnp
from jax import lax
from jax.experimental import pallas as pl
from jax.experimental.pallas import tpu as pltpu
from jax.sharding import PartitionSpec as P

F32, BF16 = jnp.float32, jnp.bfloat16
NT = (((1,), (1,)), ((), ()))
TN = (((0,), (0,)), ((), ()))
PIECES = 2
WORK = 0.6
VMEM_LIMIT = 16 * 2**20


def swap(value, axis, distance):
    size = lax.axis_size(axis)
    return lax.ppermute(value, axis, [(i, i ^ distance) for i in range(size)])


def shares(size):
    return [1 << bit for bit in range(size.bit_length() - 1)]


def sigmoid(wide):
    return jax.nn.sigmoid(wide)


def silu(value):
    wide = value.astype(F32)
    return (wide * sigmoid(wide)).astype(BF16)


VMEM = pl.BlockSpec(memory_space=pltpu.VMEM)
HBM = pl.BlockSpec(memory_space=pltpu.HBM)


def in_vmem(shape, dtype):
    return pltpu.VMEM(shape, dtype)


def in_hbm(shape, dtype):
    return pltpu.HBM(shape, dtype)


def call(kernel, out_shape, in_specs, scratch=(), aliases=None, name=None):
    outs = out_shape if isinstance(out_shape, list) else [out_shape]
    out_specs = [pl.BlockSpec(memory_space=out.memory_space) for out in outs]
    run = pl.pallas_call(
        kernel,
        out_shape=outs,
        in_specs=in_specs,
        out_specs=out_specs,
        scratch_shapes=list(scratch),
        input_output_aliases=aliases or {},
        compiler_params=pltpu.CompilerParams(vmem_limit_bytes=VMEM_LIMIT),
        cost_estimate=pl.CostEstimate(
            flops=int(WORK * 1e9), bytes_accessed=1, transcendentals=0
        ),
        name=name,
    )

    def placed(*operands):
        operands = [
            pltpu.with_memory_space_constraint(value, spec.memory_space)
            for value, spec in zip(operands, in_specs)
        ]
        result = run(*operands)
        return result if isinstance(out_shape, list) else result[0]

    return placed


def cuts(whole, parts):
    return [pl.ds(at * (whole // parts), whole // parts) for at in range(parts)]


def number(numbers_ref, at, step):
    return pl.multiple_of(numbers_ref[at, 0], step)


def start_copy(source, target, sem):
    copy = pltpu.make_async_copy(source, target, sem)
    copy.start()
    return copy


def split(rows, width):
    count, steps = rows.shape
    parts = []
    for _ in range(3):
        part = rows.astype(BF16).astype(F32)
        parts.append(part)
        rows = rows - part
    parts.append(jnp.zeros((16 - 3 * count, steps), F32))
    out = jnp.concatenate(parts, axis=0)
    if width > steps:
        out = jnp.concatenate([out, jnp.zeros((16, width - steps), F32)], axis=1)
    return out.astype(BF16)


def joined(parts, steps):
    wide = parts[:, :steps].astype(F32)
    return wide[:2] + wide[2:4] + wide[4:6]


def load_first(source, weights, starts, half):
    steps, units = source.shape
    spans = 4
    width = units // spans

    def kernel(starts_ref, source_ref, weights_ref, sent_ref, hidden_ref, held, pre, total, sems):
        rows = pl.ds(number(starts_ref, 0, half), half)

        def copies(at):
            span = pl.ds(pl.multiple_of(at * width, width), width)
            return span, (
                pltpu.make_async_copy(source_ref.at[:, span], pre.at[:, span], sems.at[0, at]),
                pltpu.make_async_copy(
                    weights_ref.at[rows, span], held.at[:, span], sems.at[1, at]
                ),
            )

        def start(at):
            for copy in copies(at)[1]:
                copy.start()

        start(0)
        start(1)
        total[...] = jnp.zeros_like(total)

        def step(at, carry):
            @pl.when(at + 2 < spans)
            def _():
                start(at + 2)

            span, pair = copies(at)
            for copy in pair:
                copy.wait()
            hidden = silu(pre[:, span])
            hidden_ref[:, span] = hidden
            total[...] += lax.dot_general(
                hidden, held[:, span], NT, preferred_element_type=F32
            )
            return carry

        lax.fori_loop(0, spans, step, 0)
        sent_ref[...] = total[...].astype(BF16)

    return call(
        kernel,
        [
            in_vmem((steps, half), BF16),
            in_vmem((steps, units), BF16),
            in_vmem((half, units), BF16),
            in_vmem((steps, units), BF16),
        ],
        [VMEM, HBM, HBM],
        [pltpu.VMEM((steps, half), F32), pltpu.SemaphoreType.DMA((2, spans))],
        name="load_first",
    )(starts, source, weights)


def load_second(source, weights, starts, held, following):
    steps, units = source.shape
    half = held.shape[0]

    def kernel(starts_ref, source_ref, weights_ref, held_ref, out_ref, hidden_ref, block, sem):
        first = number(starts_ref, following, half)
        copy = start_copy(weights_ref.at[pl.ds(first, half), :], block, sem)

        @pl.when(first >= 0)
        def _():
            total = None
            for span in cuts(units, 4):
                hidden = silu(source_ref[:, span])
                hidden_ref[:, span] = hidden
                term = lax.dot_general(hidden, held_ref[:, span], NT, preferred_element_type=F32)
                total = term if total is None else total + term
            out_ref[...] = total.astype(BF16)

        copy.wait()

    return call(
        kernel,
        [
            in_vmem((steps, half), BF16),
            in_vmem((steps, units), BF16),
            in_vmem((half, units), BF16),
        ],
        [VMEM, VMEM, HBM, VMEM],
        [pltpu.SemaphoreType.DMA],
        name="load_second",
    )(starts, source, weights, held)


def project(hidden, rows, out_type, weights, starts, following):
    steps, units = hidden[0].shape
    half = rows.shape[0]
    more = following is not None

    def products(hidden_refs, rows_ref, out_ref):
        for at, hidden_ref in enumerate(hidden_refs):
            total = lax.dot_general(
                hidden_ref[...], rows_ref[...], NT, preferred_element_type=F32
            )
            out_ref[pl.ds(at * steps, steps), :] = total.astype(out_type)

    def kernel(first, second, rows_ref, out_ref):
        products((first, second), rows_ref, out_ref)

    def loading(starts_ref, weights_ref, first, second, rows_ref, out_ref, block, sem):
        start = number(starts_ref, following, half)
        copy = start_copy(weights_ref.at[pl.ds(start, half), :], block, sem)

        @pl.when(start >= 0)
        def _():
            products((first, second), rows_ref, out_ref)

        copy.wait()

    out_shape = in_vmem((2 * steps, half), out_type)
    if not more:
        return [call(kernel, out_shape, [VMEM] * 3, name="project")(*hidden, rows)]
    return call(
        loading,
        [out_shape, in_vmem((half, units), BF16)],
        [VMEM, HBM, VMEM, VMEM, VMEM],
        [pltpu.SemaphoreType.DMA],
        name="project",
    )(starts, weights, *hidden, rows)


def lane_sums(value):
    width = value.shape[1]
    if width % 128 == 0:
        squares = value * value
        squares = sum(squares[:, at : at + 128] for at in range(0, width, 128))
        return jnp.sum(squares.T, axis=0, keepdims=True)
    ones = jnp.ones((8, value.shape[1]), F32)
    sums = lax.dot_general(
        ones, value * value, NT, precision=lax.Precision.HIGHEST, preferred_element_type=F32
    )
    return sums[:1]


def half_of(place, steps):
    return pl.ds(pl.multiple_of(place * steps, steps), steps)


def predicted_of(kept, arriving, starts, squares, packed):
    steps, width = kept.shape[0] // 2, kept.shape[1]

    def kernel(starts_ref, kept_ref, *refs):
        sent_ref, total_ref, squares_ref = refs[-3:]
        rows = []
        for at in range(2):
            part = pl.ds(at * steps, steps)
            arrived = refs[0][part, :] if len(arriving) == 1 else refs[at][...]
            total = kept_ref[part, :] + arrived.astype(F32)
            total_ref[part, :] = total
            rows.append(lane_sums(total))
        sent_ref[pl.ds(0, steps), :] = total_ref[half_of(1 - starts_ref[7, 0], steps), :].astype(BF16)
        both = jnp.concatenate(rows, axis=0)
        if squares is not None:
            both += refs[len(arriving)][...]
        squares_ref[...] = both
        if packed:
            sent_ref[pl.ds(steps, 16), :] = split(both, width)

    shapes = [
        in_vmem((steps + 16 * packed, width), BF16),
        in_vmem((2 * steps, width), F32),
        in_vmem((2, steps), F32),
    ]
    more = [] if squares is None else [squares]
    operands = [starts, kept, *arriving, *more]
    return call(kernel, shapes, [VMEM] * len(operands), name="predicted")(*operands)


def sum_of(total, arriving, starts, squares, packed, out_packed):
    steps, width = arriving.shape[0] - 16 * packed, arriving.shape[1]

    def kernel(starts_ref, total_ref, arriving_ref, *refs):
        sent_ref, out_ref = refs[-2:] if squares is None else refs[1:3]
        held = total_ref[half_of(starts_ref[7, 0], steps), :] if total.shape[0] > steps else total_ref[...]
        out = held + arriving_ref[pl.ds(0, steps), :].astype(F32)
        sent_ref[pl.ds(0, steps), :] = out.astype(BF16)
        out_ref[...] = out
        if squares is None:
            return
        both = refs[0][...]
        if packed:
            both += joined(arriving_ref[pl.ds(steps, 16), :], both.shape[1])
        refs[3][...] = both
        if out_packed:
            sent_ref[pl.ds(steps, 16), :] = split(both, width)

    shapes = [
        in_vmem((steps + 16 * out_packed, width), BF16),
        in_vmem((steps, width), F32),
    ]
    more = [] if squares is None else [squares]
    shapes += [in_vmem(value.shape, F32) for value in more]
    return call(kernel, shapes, [VMEM] * (3 + len(more)), name="sum_of")(
        starts, total, arriving, *more
    )


def kept_gradient(total, predicted, starts, cotangents, members, factor):
    steps, width = total.shape

    def kernel(starts_ref, total_ref, predicted_ref, own, other, grad_ref):
        first = starts_ref[7, 0] == 0
        weighting = jnp.where(first, own[:, :1], other[:, :1]).astype(F32) * factor
        predicted_rows = predicted_ref[half_of(starts_ref[7, 0], steps), :]
        grad_ref[...] = (weighting * (predicted_rows - total_ref[...] / members)).astype(BF16)

    operands = [starts, total, predicted, *cotangents]
    return call(
        kernel,
        in_vmem((steps, width), BF16),
        [VMEM] * len(operands),
        name="kept_gradient",
    )(*operands)


def gradient_of(total, arriving, predicted, starts, cotangents, members, factor, sums):
    steps, width = total.shape
    squares, previous, packed = sums

    def kernel(starts_ref, total_ref, arriving_ref, predicted_ref, own, other, *refs):
        refs, mean_ref = list(refs[:-1]), refs[-1]
        previous_ref = refs.pop(0) if previous is not None else None
        squares_ref = refs.pop(0) if squares is not None else None
        sent_ref, grad_ref, sums_ref = refs
        mean_ref[half_of(starts_ref[7, 0], steps), :] = total_ref[...] / members
        mean_ref[half_of(1 - starts_ref[7, 0], steps), :] = arriving_ref[...].astype(F32) / members
        rows = []
        for at, cotangent_ref in enumerate((own, other)):
            part = pl.ds(at * steps, steps)
            mean = mean_ref[part, :]
            weighting = cotangent_ref[:, :1].astype(F32) * factor
            grad_ref[part, :] = (weighting * (predicted_ref[part, :] - mean)).astype(BF16)
            rows.append(lane_sums(mean))
        sent_ref[pl.ds(0, steps), :] = grad_ref[half_of(1 - starts_ref[7, 0], steps), :]
        both = jnp.concatenate(rows, axis=0)
        if previous is not None:
            both += previous_ref[...]
        if squares is not None:
            both = squares_ref[...] / members - both
        sums_ref[...] = both
        if packed:
            sent_ref[pl.ds(steps, 16), :] = split(both, width)

    operands = [starts, total, arriving, predicted, *cotangents]
    operands += [value for value in (previous, squares) if value is not None]
    return call(
        kernel,
        [
            in_vmem((steps + 16 * packed, width), BF16),
            in_vmem((2 * steps, width), BF16),
            in_vmem((2, steps), F32),
        ],
        [VMEM] * len(operands),
        [pltpu.VMEM((2 * steps, width), F32)],
        name="gradient",
    )(*operands)


def in_place(kept, rest, starts, steps):
    def kernel(starts_ref, kept_ref, rest_ref, out_ref):
        out_ref[half_of(starts_ref[7, 0], steps), :] = kept_ref[...]
        out_ref[half_of(1 - starts_ref[7, 0], steps), :] = rest_ref[pl.ds(0, steps), :]

    out_shape = in_vmem((2 * steps, kept.shape[1]), BF16)
    return call(kernel, out_shape, [VMEM] * 3, name="in_place")(starts, kept, rest)


def plus(first, second):
    def kernel(first_ref, second_ref, out_ref):
        out_ref[...] = first_ref[...] + second_ref[...]

    return call(kernel, in_vmem(first.shape, F32), [VMEM, VMEM], name="plus")(first, second)


def leave_to_other(first, second, before, spread, arriving_spread, steps):
    units = before.shape[1]
    packed = arriving_spread.shape[0] > 2

    def kernel(g0, rows0, g1, rows1, before_ref, spread_ref, arriving_ref, out_ref, sum_ref):
        for span in cuts(units, 4):
            total = before_ref[:, span]
            for grad, rows in ((g0, rows0), (g1, rows1)):
                total += jnp.dot(
                    grad[pl.ds(steps, steps), :], rows[:, span], preferred_element_type=F32
                )
            out_ref[pl.ds(0, steps), span] = total.astype(BF16)
        if packed:
            both = spread_ref[...] + joined(arriving_ref[pl.ds(steps, 16), :], steps)
        else:
            both = spread_ref[...] + arriving_ref[...]
        sum_ref[...] = both
        out_ref[pl.ds(steps, 16), :] = split(both, units)

    shapes = [in_vmem((steps + 16, units), BF16), in_vmem((2, steps), F32)]
    return call(kernel, shapes, [VMEM] * 7, name="leave_to_other")(
        *first, *second, before, spread, arriving_spread
    )


def block_rows(grad, hidden, steps, rows):
    total = None
    for at, held in enumerate(hidden):
        term = lax.dot_general(
            grad[pl.ds(at * steps, steps), rows], held[...], TN, preferred_element_type=F32
        )
        total = term if total is None else total + term
    return total.astype(BF16)


def write_rows(start, grad, hidden, steps, made, out_ref, sems):
    copies = []
    for at, rows in enumerate(cuts(made.shape[0], 2)):
        made[rows, :] = block_rows(grad, hidden, steps, rows)
        to = pl.ds(pl.multiple_of(start + rows.start, rows.size), rows.size)
        copies.append(start_copy(made.at[rows, :], out_ref.at[to, :], sems.at[at]))
    return copies


def add_back(refs, pairs, added, sum_ref, part):
    steps, units = sum_ref.shape
    for span in cuts(units, 4):
        out = refs[2 * pairs][:, span] if added else None
        for at in range(pairs):
            grad, rows = refs[2 * at : 2 * at + 2]
            term = jnp.dot(
                grad[pl.ds(part * steps, steps), :], rows[:, span], preferred_element_type=F32
            )
            out = term if out is None else out + term
        sum_ref[:, span] = out


def weight_rows(grads, hidden, starts, blocks, features, started=None, back=()):
    half, (steps, units) = grads[0].shape[1], hidden[0].shape
    started = [] if started is None else [started]
    operands = []
    for _, pairs, before in back:
        operands += [value for pair in pairs for value in pair]
        operands += [] if before is None else [before]
    count = len(grads)

    def kernel(starts_ref, *refs):
        grad_refs, held, refs = refs[:count], refs[count : count + 2], refs[count + 2 :]
        out_ref, *sum_refs, made, sems = refs[len(operands) + len(started) :]
        copies = []
        for at, (grad, block) in enumerate(zip(grad_refs, blocks)):
            copies += write_rows(
                starts_ref[block, 0], grad, held, steps, made.at[at], out_ref, sems.at[at]
            )
        for (part, pairs, before), sum_ref in zip(back, sum_refs):
            add_back(refs, len(pairs), before is not None, sum_ref, part)
            refs = refs[2 * len(pairs) + (before is not None) :]
        for copy in copies:
            copy.wait()

    return call(
        kernel,
        [in_hbm((features, units), BF16)] + [in_vmem((steps, units), F32)] * len(back),
        [VMEM] * (3 + count + len(operands)) + [HBM] * len(started),
        [pltpu.VMEM((count, half, units), BF16), pltpu.SemaphoreType.DMA((count, 2))],
        aliases={3 + count + len(operands): 0} if started else None,
        name="weight_rows",
    )(starts, *grads, *hidden, *operands, *started)


def slope_of(pre_act):
    def kernel(pre, slope_ref):
        for span in cuts(pre_act.shape[1], 4):
            wide = pre[:, span].astype(F32)
            gate = sigmoid(wide)
            slope_ref[:, span] = gate * (1.0 + wide * (1.0 - gate))

    return call(kernel, in_vmem(pre_act.shape, F32), [VMEM], name="slope_of")(pre_act)


def last_grads(before, arrived, slope, spread, model_width):
    steps, units = before.shape
    lanes = -(-steps // 128) * 128

    def kernel(
        before_ref, arrived_ref, slope, spread_ref, act_ref, reward_ref, act, reward, sems
    ):
        others = joined(arrived_ref[pl.ds(steps, 16), pl.ds(0, lanes)], steps)
        reward[...] = (spread_ref[...][:1] + others[1:]) / model_width
        copies = [start_copy(reward, reward_ref, sems.at[4])]
        for at, span in enumerate(cuts(units, 4)):
            total = before_ref[:, span] + arrived_ref[pl.ds(0, steps), span].astype(F32)
            act[:, span] = (total * slope[:, span]).astype(BF16)
            copies.append(start_copy(act.at[:, span], act_ref.at[:, span], sems.at[at]))
        for copy in copies:
            copy.wait()

    return call(
        kernel,
        [in_hbm((steps, units), BF16), in_hbm((1, steps), F32)],
        [VMEM] * 4,
        [
            pltpu.VMEM((steps, units), BF16),
            pltpu.VMEM((1, steps), F32),
            pltpu.SemaphoreType.DMA((5,)),
        ],
        name="last_grads",
    )(before, arrived, slope, spread)


class Order:
    def __init__(self):
        self.last = None

    def __call__(self, step, *values):
        if self.last is not None:
            values, _ = lax.optimization_barrier((values, self.last))
        result = step(*values)
        self.last = jax.tree.leaves(result)[0]
        return result


class Piece:
    def __init__(self, order, starts, last, previous):
        self.order, self.starts = order, starts
        self.last, self.previous = last, previous
        self.tensor = lax.axis_index("tensor")
        self.arriving = []

    def leave(self, sent):
        self.arriving.append(swap(sent, "tensor", shares(lax.axis_size("tensor"))[-1]))

    def scatter_rest(self):
        def add(total, arriving):
            return total + arriving.astype(F32)

        for distance in reversed(shares(lax.axis_size("tensor"))[:-1]):
            half = self.total.shape[1] // 2
            high = (self.tensor // distance) % 2
            total = self.order(add, self.total, jnp.concatenate(self.arriving))
            sent = lax.dynamic_slice_in_dim(total, (1 - high) * half, half, 1)
            self.total = lax.dynamic_slice_in_dim(total, high * half, half, 1)
            self.arriving = [swap(sent.astype(BF16), "tensor", distance)]

    def predict(self):
        steps, width = self.total.shape[0] // 2, self.total.shape[1]
        self.packed = self.last and width >= steps
        before = None if self.previous is None else self.previous.squares
        sent, self.predicted, self.squares = self.order(
            lambda kept, *arriving: predicted_of(
                kept, arriving, self.starts, before, self.packed
            ),
            self.total,
            *self.arriving,
        )
        self.sum = self.predicted
        near, *self.far = shares(lax.axis_size("ensemble"))
        self.arriving = swap(sent, "ensemble", near)
        self.exchange_squares(near)

    def exchange_squares(self, distance):
        self.squares_arriving = None
        if self.last and not self.packed:
            self.squares_arriving = swap(self.squares, "ensemble", distance)

    def ensemble_steps(self):
        packed = self.packed
        for distance in self.far + [None]:
            out_packed = self.packed and distance is not None
            before = self.squares if self.last else None
            sent, self.sum, *squares = self.order(
                lambda total, arriving: sum_of(
                    total, arriving, self.starts, before, packed, out_packed
                ),
                self.sum,
                self.arriving,
            )
            if self.last:
                self.squares = squares[0]
            if self.squares_arriving is not None:
                self.squares = self.order(plus, self.squares, self.squares_arriving)
            if distance is not None:
                self.arriving = swap(sent, "ensemble", distance)
                self.exchange_squares(distance)
                yield
            else:
                self.arriving = swap(sent, "ensemble", 1)

    def gather(self, share):
        def join(share, other, distance):
            high = (self.tensor // distance) % 2
            first = jnp.where(high == 0, share, other)
            second = jnp.where(high == 0, other, share)
            return jnp.concatenate([first, second], axis=1)

        *near, far = shares(lax.axis_size("tensor"))
        for distance in near:
            other = swap(share, "tensor", distance)
            share = self.order(functools.partial(join, distance=distance), share, other)
        return share, swap(share, "tensor", far)

    def early_gradient(self, cotangents, members, factor):
        grad = self.order(
            lambda total: kept_gradient(
                total, self.predicted, self.starts, cotangents, members, factor
            ),
            self.sum,
        )
        self.kept = self.gather(grad)

    def gradient(self, cotangents, members, factor):
        *near, far = shares(lax.axis_size("tensor"))
        packed = self.last and not near and self.sum.shape[1] >= self.sum.shape[0]
        sums = (
            self.squares if self.last else None,
            None if self.previous is None else self.previous.sums,
            packed,
        )
        sent, self.share, self.sums = self.order(
            lambda total, arriving: gradient_of(
                total,
                arriving,
                self.predicted,
                self.starts,
                cotangents,
                members,
                factor,
                sums,
            ),
            self.sum,
            self.arriving,
        )
        self.rest = self.gather(sent)
        self.other_sums = self.rest[1]
        if self.last and not packed:
            for distance in near:
                self.sums = self.order(plus, self.sums, swap(self.sums, "tensor", distance))
            self.other_sums = swap(self.sums, "tensor", far)
        if near:
            self.share = self.together(0)

    def together(self, which):
        steps = self.sum.shape[0]
        return self.order(
            lambda kept, rest: in_place(kept, rest, self.starts, steps),
            self.kept[which],
            self.rest[which],
        )


def body(pre_act, weights, cotangent):
    pre_act, weights = pre_act[:, 0, :], weights[0]
    steps, features = pre_act.shape[0], weights.shape[0]
    members = lax.axis_size("ensemble")
    model_width = features * lax.axis_size("seq")
    factor = 2.0 / (members * model_width)
    half = features // (2 * PIECES)
    far = shares(lax.axis_size("tensor"))[-1]
    high = (lax.axis_index("tensor") // far) % 2
    starts = []
    for piece in range(PIECES):
        starts += [(2 * piece + 1 - high) * half, (2 * piece + high) * half]
    assert len(starts) < 8
    starts += [0] * (7 - len(starts)) + [lax.axis_index("ensemble") % 2]
    starts = jnp.broadcast_to(jnp.stack(starts).astype(jnp.int32)[:, None], (8, 128))

    pre_other = swap(pre_act, "seq", 1)
    cot_other = swap(cotangent, "seq", 1)
    pre_act, starts = lax.optimization_barrier((pre_act, starts))
    order = Order()
    pieces = []
    for at in range(PIECES):
        previous = pieces[-1] if pieces else None
        pieces.append(Piece(order, starts, at == PIECES - 1, previous))
    blocks = [None] * (2 * PIECES)
    sent, hidden, blocks[0], pre_act = order(
        lambda p: load_first(p, weights, starts, half), pre_act
    )
    pieces[0].leave(sent)
    sent, hidden_other, blocks[2] = order(
        lambda p: load_second(p, weights, starts, blocks[0], 2), pre_other
    )
    pieces[0].leave(sent)
    both = [hidden, hidden_other]

    def products(at, following):
        out = order(
            lambda rows: project(
                both, rows, F32 if at % 2 else BF16, weights, starts, following
            ),
            blocks[at],
        )
        if following is not None:
            blocks[following] = out[1]
        return out[0]

    a, b = pieces
    b.leave(products(2, 1))
    a.total = products(1, 3)
    a.scatter_rest()
    a.predict()
    b.total = products(3, None)
    slope = order(slope_of, pre_act)
    cotangents = [
        order(lambda c: jnp.broadcast_to(c[:, None], (steps, 128)), value)
        for value in (cotangent, cot_other)
    ]
    b.scatter_rest()
    b.predict()
    a_steps, b_steps = a.ensemble_steps(), b.ensemble_steps()
    next(a_steps)
    for _ in b.far:
        next(b_steps)
        next(a_steps, None)
    a.early_gradient(cotangents, members, factor)
    next(b_steps, None)
    b.early_gradient(cotangents, members, factor)
    a.gradient(cotangents, members, factor)

    def rows_of(shares, at, started, back):
        return order(
            lambda started, *shares: weight_rows(
                shares,
                both,
                starts,
                at,
                features,
                started,
                [
                    (part, [(shares[n], blocks[at[n]]) for n in range(len(at))], before)
                    for part, before in back
                ],
            ),
            started,
            *shares,
        )

    sides = [(1, None), (0, None)]
    weight_grads, before_other, before = rows_of([a.share], [1], None, sides)
    b.gradient(cotangents, members, factor)
    sides = [(1, before_other), (0, before)]
    weight_grads, before_other, before = rows_of([b.share], [3], weight_grads, sides)
    a_other = a.together(1)
    b_other = b.together(1)
    leaving, spread = order(
        lambda x, y, z: leave_to_other(
            (x, blocks[0]), (y, blocks[2]), before_other, b.sums, z, steps
        ),
        a_other,
        b_other,
        b.other_sums,
    )
    arrived = swap(leaving, "seq", 1)
    weight_grads, before = rows_of([a_other, b_other], [0, 2], weight_grads, [(0, before)])
    act_grads, reward = order(
        lambda g, s: last_grads(g, s, slope, spread, model_width), before, arrived
    )
    return (weight_grads[None], act_grads[:, None, :], reward[0])


def solution(mesh):
    placed = (
        P(("groups", "seq"), "ensemble", "tensor"),
        P("ensemble", "seq", "tensor"),
        P(("groups", "seq")),
    )
    return jax.shard_map(
        body,
        mesh=mesh,
        in_specs=placed,
        out_specs=(
            P(("groups", "ensemble"), "seq", "tensor"),
            P(("groups", "seq"), "ensemble", "tensor"),
            P(("groups", "seq")),
        ),
        check_vma=False,
    )
```

time: 54.4 us -> 50 us (0.919)
  waiting for transfers between devices: 9.12 us -> 6.9 us
  starting transfers between devices: 19.5 us -> 18.4 us
  Pallas kernels: 24 us -> 23.1 us
    ppermute x13 -> x16, waiting for transfers between devices: 9.12 us -> 6.9 us  [swap(): return lax.ppermute(value, axis, [(i, i ^ distance) for i in range(size)])]
    ppermute x13 -> x16, starting transfers between devices: 19.5 us -> 18.4 us  [swap(): return lax.ppermute(value, axis, [(i, i ^ distance) for i in range(size)])]
    pallas_call x18 -> x23, Pallas kernels: 24 us -> 23.1 us  [placed(): result = run(*operands)]
  transfers between devices with their start and end apart: 13 -> 16, of which waited for: 8 -> 4; matrix products, arithmetic and copies ran while one was open for 0% -> 1% of each run, Pallas kernels for 37% -> 42%
where the time goes in v3:
time: 50 us; the launch traced here: 49.8 us
  Pallas kernels  23.1 us (46%)
  starting transfers between devices  18.4 us (37%)
  waiting for transfers between devices  6.9 us (14%)
  between operations  1.05 us (2%)
    pallas_call x23, Pallas kernels, placed(): result = run(*operands)  23.1 us
    ppermute x16, starting transfers between devices, swap(): return lax.ppermute(value, axis, [(i, i ^ distance) for i in range(size)])  18.4 us
    ppermute x16, waiting for transfers between devices, swap(): return lax.ppermute(value, axis, [(i, i ^ distance) for i in range(size)])  6.9 us
  transfers between devices with their start and end apart: 16, of which 4 were waited for; matrix products, arithmetic and copies ran while one was open for 1% of the time, Pallas kernels for 42%

profile of v3, /device:TPU:1, one launch (start us, length us, event | category | flops | bytes accessed | tf_op | source)
XLA Modules:
  0.0 49.8 jit_solution(18232699056001258873)
XLA Ops:
  0.6 0.1 collective-permute-start
  0.8 0.5 collective-permute-start.5
  1.2 0.1 stack.23
  1.3 0.1 broadcast_in_dim.10.starts_ref
  1.4 3.2 %load_first.1 = (bf16[192,256]{1,0:T(8,128)(2,1)S(1)}, bf16[192,4096]{1,0:T(8,128)(2,1)S(1)}, bf16[256,4096]{1,0:T(8,128)(2,1)S(1)}, bf16[192,4096]{1,0:T(8,128)(2,1)S(1)}) custom-call(s32[8,128]{1,0:T(8,128)S(1)} %broadcast_in_dim.10.starts_ref, bf16[192,4096]{1,0:T(8,128)(2,1)} %bitcast.16, bf16[1024,4096]{1,0:T(8,128)(2,1)} %bitcast.10), custom_call_target="tpu_custom_call" | custom-call | flops 600000000 | bytes 1 | tf_op jit(solution)/shard_map/load_first/pallas_call | solution.py:70
  4.6 2.4 %collective-permute-start.1 = (bf16[192,256]{1,0:T(8,128)(2,1)S(1)}, bf16[192,256]{1,0:T(8,128)(2,1)S(1)}, u32[]{:S(2)}, u32[]{:S(2)}) collective-permute-start(bf16[192,256]{1,0:T(8,128)(2,1)S(1)} %get-tuple-element.94), channel_id=1, source_target_pairs={{0,2},{2,0},{1,3},{3,1},{4,6},{6,4},{5,7},{7,5},{8,10},{10,8},{9,1... | collective-permute-start | bytes 294920 | tf_op jit(solution)/shard_map/ppermute | solution.py:20
  6.9 0.0 collective-permute-done.source_ref
  6.9 1.6 %load_second.1 = (bf16[192,256]{1,0:T(8,128)(2,1)S(1)}, bf16[192,4096]{1,0:T(8,128)(2,1)S(1)}, bf16[256,4096]{1,0:T(8,128)(2,1)S(1)}) custom-call(s32[8,128]{1,0:T(8,128)S(1)} %broadcast_in_dim.10.starts_ref, bf16[192,4096]{1,0:T(8,128)(2,1)S(1)} %collective-permute-done.source_ref, bf16[1024,4096]{1,0:T(8,128)(2,1)} %bitcast.11, ...), custom_call_target="tpu_custom_call" | custom-call | flops 600000000 | bytes 1 | tf_op jit(solution)/shard_map/load_second/pallas_call | solution.py:70
  8.6 0.1 collective-permute-start.2
  8.7 1.6 %project.3 = (bf16[384,256]{1,0:T(8,128)(2,1)S(1)}, bf16[256,4096]{1,0:T(8,128)(2,1)S(1)}) custom-call(s32[8,128]{1,0:T(8,128)S(1)} %broadcast_in_dim.10.starts_ref, bf16[1024,4096]{1,0:T(8,128)(2,1)} %bitcast.12, bf16[192,4096]{1,0:T(8,128)(2,1)S(1)} %get-tuple-element.93.first.refs_1_.refs_2_, ...), custom_call_target="tpu_custom_call" | custom-call | flops 600000000 | bytes 1 | tf_op jit(solution)/shard_map/project/pallas_call | solution.py:70
  10.3 1.5 %collective-permute-start.4 = (bf16[384,256]{1,0:T(8,128)(2,1)S(1)}, bf16[384,256]{1,0:T(8,128)(2,1)S(1)}, u32[]{:S(2)}, u32[]{:S(2)}) collective-permute-start(bf16[384,256]{1,0:T(8,128)(2,1)S(1)} %get-tuple-element.102), channel_id=1, source_target_pairs={{0,2},{2,0},{1,3},{3,1},{4,6},{6,4},{5,7},{7,5},{8,10},{10,8},{9,1... | collective-permute-start | bytes 589832 | tf_op jit(solution)/shard_map/ppermute | solution.py:20
  11.8 1.7 %project.4 = (f32[384,256]{1,0:T(8,128)S(1)}, bf16[256,4096]{1,0:T(8,128)(2,1)S(1)}) custom-call(s32[8,128]{1,0:T(8,128)S(1)} %broadcast_in_dim.10.starts_ref, bf16[1024,4096]{1,0:T(8,128)(2,1)} %bitcast.13, bf16[192,4096]{1,0:T(8,128)(2,1)S(1)} %get-tuple-element.93.first.refs_1_.refs_2_, bf16[192,4096]{1,0:T(8,128)(2,1)S(1)} %get-tuple-element.97.second.refs_2_.refs_3_, ...), custom_call_target="tpu_custom_call" | custom-call | flops 600000000 | bytes 1 | tf_op jit(solution)/shard_map/project/pallas_call | solution.py:70
  13.6 0.0 collective-permute-done.1.refs_0_
  13.6 0.0 collective-permute-done.2.refs_1_
  13.6 0.2 predicted.2
  13.8 1.4 %collective-permute-start.3 = (bf16[192,256]{1,0:T(8,128)(2,1)S(1)}, bf16[192,256]{1,0:T(8,128)(2,1)S(1)}, u32[]{:S(2)}, u32[]{:S(2)}) collective-permute-start(bf16[192,256]{1,0:T(8,128)(2,1)S(1)} %get-tuple-element.109), channel_id=1, source_target_pairs={{0,4},{4,0},{8,12},{12,8},{1,5},{5,1},{9,13},{13,9},{2,6},{6,2},{1... | collective-permute-start | bytes 294920 | tf_op jit(solution)/shard_map/ppermute | solution.py:20
  15.1 1.5 %project.5.kept_ref = f32[384,256]{1,0:T(8,128)S(1)} custom-call(bf16[192,4096]{1,0:T(8,128)(2,1)S(1)} %get-tuple-element.93.first.refs_1_.refs_2_, bf16[192,4096]{1,0:T(8,128)(2,1)S(1)} %get-tuple-element.97.second.refs_2_.refs_3_, bf16[256,4096]{1,0:T(8,128)(2,1)S(1)} %get-tuple-element.111.rows_ref.refs_4_.refs_7_), custom_call_target="tpu_custom_call" | custom-call | flops 600000000 | bytes 1 | tf_op jit(solution)/shard_map/project/pallas_call | solution.py:70
  16.6 0.0 copy-start
  16.7 0.8 %slope_of.1.slope = f32[192,4096]{1,0:T(8,128)S(1)} custom-call(bf16[192,4096]{1,0:T(8,128)(2,1)S(1)} %get-tuple-element.113.pre), custom_call_target="tpu_custom_call" | custom-call | flops 600000000 | bytes 1 | tf_op jit(solution)/shard_map/slope_of/pallas_call | solution.py:70
  17.4 0.0 collective-permute-done.5
  17.4 0.0 copy-done
  17.5 0.1 broadcast_in_dim.11.own
  17.6 0.0 collective-permute-done.4.refs_0_
  17.6 0.1 broadcast_in_dim.12.other
  17.7 0.2 predicted.3
  17.8 0.3 collective-permute-start.7
  18.2 0.0 collective-permute-done.3.arriving_ref
  18.2 0.1 sum_of.4
  18.2 2.4 %collective-permute-start.6 = (bf16[192,256]{1,0:T(8,128)(2,1)S(1)}, bf16[192,256]{1,0:T(8,128)(2,1)S(1)}, u32[]{:S(2)}, u32[]{:S(2)}) collective-permute-start(bf16[192,256]{1,0:T(8,128)(2,1)S(1)} %get-tuple-element.123), channel_id=1, source_target_pairs={{0,8},{4,12},{8,0},{12,4},{1,9},{5,13},{9,1},{13,5},{2,10},{6,14},... | collective-permute-start | bytes 294920 | tf_op jit(solution)/shard_map/ppermute | solution.py:20
  20.6 0.8 %collective-permute-done.7.arriving_ref = bf16[208,256]{1,0:T(8,128)(2,1)S(1)} collective-permute-done((bf16[208,256]{1,0:T(8,128)(2,1)S(1)}, bf16[208,256]{1,0:T(8,128)(2,1)S(1)}, u32[]{:S(2)}, u32[]{:S(2)}) %collective-permute-start.7) | collective-permute-done | bytes 106528 | tf_op jit(solution)/shard_map/ppermute | solution.py:20
  21.5 0.1 sum_of.5
  21.5 2.4 %collective-permute-start.9 = (bf16[208,256]{1,0:T(8,128)(2,1)S(1)}, bf16[208,256]{1,0:T(8,128)(2,1)S(1)}, u32[]{:S(2)}, u32[]{:S(2)}) collective-permute-start(bf16[208,256]{1,0:T(8,128)(2,1)S(1)} %get-tuple-element.128), channel_id=1, source_target_pairs={{0,8},{4,12},{8,0},{12,4},{1,9},{5,13},{9,1},{13,5},{2,10},{6,14},... | collective-permute-start | bytes 319496 | tf_op jit(solution)/shard_map/ppermute | solution.py:20
  23.9 0.0 collective-permute-done.6.arriving_ref
  23.9 1.1 %collective-permute-start.8 = (bf16[192,256]{1,0:T(8,128)(2,1)S(1)}, bf16[192,256]{1,0:T(8,128)(2,1)S(1)}, u32[]{:S(2)}, u32[]{:S(2)}) collective-permute-start(bf16[192,256]{1,0:T(8,128)(2,1)S(1)} %get-tuple-element.132), channel_id=1, source_target_pairs={{0,4},{4,0},{8,12},{12,8},{1,5},{5,1},{9,13},{13,9},{2,6},{6,2},{1... | collective-permute-start | bytes 294920 | tf_op jit(solution)/shard_map/ppermute | solution.py:20
  25.0 0.1 kept_gradient.2
  25.2 0.3 collective-permute-start.11
  25.5 4.1 %collective-permute-done.9.arriving_ref = bf16[208,256]{1,0:T(8,128)(2,1)S(1)} collective-permute-done((bf16[208,256]{1,0:T(8,128)(2,1)S(1)}, bf16[208,256]{1,0:T(8,128)(2,1)S(1)}, u32[]{:S(2)}, u32[]{:S(2)}) %collective-permute-start.9) | collective-permute-done | bytes 106528 | tf_op jit(solution)/shard_map/ppermute | solution.py:20
  29.6 0.1 collective-permute-start.10
  29.7 0.1 kept_gradient.3
  29.8 0.3 collective-permute-start.13
  30.1 0.0 collective-permute-done.8.arriving_ref
  30.1 0.3 gradient.2
  30.5 1.3 %collective-permute-start.12 = (bf16[192,256]{1,0:T(8,128)(2,1)S(1)}, bf16[192,256]{1,0:T(8,128)(2,1)S(1)}, u32[]{:S(2)}, u32[]{:S(2)}) collective-permute-start(bf16[192,256]{1,0:T(8,128)(2,1)S(1)} %get-tuple-element.144), channel_id=1, source_target_pairs={{0,2},{2,0},{1,3},{3,1},{4,6},{6,4},{5,7},{7,5},{8,10},{10,8},{9,1... | collective-permute-start | bytes 294920 | tf_op jit(solution)/shard_map/ppermute | solution.py:20
  31.8 2.3 %weight_rows.3 = (bf16[1024,4096]{1,0:T(8,128)(2,1)}, f32[192,4096]{1,0:T(8,128)S(1)}, f32[192,4096]{1,0:T(8,128)S(1)}) custom-call(s32[8,128]{1,0:T(8,128)S(1)} %broadcast_in_dim.10.starts_ref, bf16[384,256]{1,0:T(8,128)(2,1)S(1)} %get-tuple-element.145.refs_0_.refs_3_.refs_5_, bf16[192,4096]{1,0:T(8,128)(2,1)S(1)} %get-tuple-element.93.first.refs_1_.refs_2_, ...), custom_call_target="tpu_custom_call" | custom-call | flops 600000000 | bytes 1 | tf_op jit(solution)/shard_map/weight_rows/pallas_call | solution.py:70
  34.0 0.4 collective-permute-done.10.arriving_ref
  34.5 0.3 gradient.3
  34.8 0.1 collective-permute-start.14
  34.9 2.5 %weight_rows.4 = (bf16[1024,4096]{1,0:T(8,128)(2,1)}, f32[192,4096]{1,0:T(8,128)S(1)}, f32[192,4096]{1,0:T(8,128)S(1)}) custom-call(s32[8,128]{1,0:T(8,128)S(1)} %broadcast_in_dim.10.starts_ref, bf16[384,256]{1,0:T(8,128)(2,1)S(1)} %get-tuple-element.153.refs_0_.refs_3_.refs_6_, ...), custom_call_target="tpu_custom_call", output_to_operand_aliasing={{0}: (10, {})} | custom-call | flops 600000000 | bytes 1 | tf_op jit(solution)/shard_map/weight_rows/pallas_call | solution.py:70
  37.4 0.0 collective-permute-done.11.kept_ref
  37.4 0.0 collective-permute-done.12.rest_ref
  37.4 0.1 in_place.2.g0.refs_0_.refs_4_
  37.4 0.0 collective-permute-done.13.kept_ref
  37.5 1.5 %collective-permute-done.14.rest_ref.arriving_ref = bf16[208,256]{1,0:T(8,128)(2,1)S(1)} collective-permute-done((bf16[208,256]{1,0:T(8,128)(2,1)S(1)}, bf16[208,256]{1,0:T(8,128)(2,1)S(1)}, u32[]{:S(2)}, u32[]{:S(2)}) %collective-permute-start.14) | collective-permute-done | bytes 106528 | tf_op jit(solution)/shard_map/ppermute | solution.py:20
  39.0 1.0 %leave_to_other.1 = (bf16[208,4096]{1,0:T(8,128)(2,1)S(1)}, f32[2,192]{1,0:T(2,128)S(1)}) custom-call(bf16[384,256]{1,0:T(8,128)(2,1)S(1)} %in_place.2.g0.refs_0_.refs_4_, bf16[256,4096]{1,0:T(8,128)(2,1)S(1)} %get-tuple-element.96.held_ref.rows0.refs_5_, bf16[384,256]{1,0:T(8,128)(2,1)S(1)} %in_place.3.g1.refs_1_.refs_6_, ...), custom_call_target="tpu_custom_call" | custom-call | flops 600000000 | bytes 1 | tf_op jit(solution)/shard_map/leave_to_other/pallas_call | solution.py:70
  40.0 4.3 %collective-permute-start.15 = (bf16[208,4096]{1,0:T(8,128)(2,1)S(1)}, bf16[208,4096]{1,0:T(8,128)(2,1)S(1)}, u32[]{:S(2)}, u32[]{:S(2)}) collective-permute-start(bf16[208,4096]{1,0:T(8,128)(2,1)S(1)} %get-tuple-element.167), channel_id=1, source_target_pairs={{0,1},{1,0},{2,3},{3,2},{4,5},{5,4},{6,7},{7,6},{8,9},{9,8},{10,11... | collective-permute-start | bytes 5111816 | tf_op jit(solution)/shard_map/ppermute | solution.py:20
  44.3 4.0 %weight_rows.5 = (bf16[1024,4096]{1,0:T(8,128)(2,1)}, f32[192,4096]{1,0:T(8,128)S(1)}) custom-call(s32[8,128]{1,0:T(8,128)S(1)} %broadcast_in_dim.10.starts_ref, bf16[384,256]{1,0:T(8,128)(2,1)S(1)} %in_place.2.g0.refs_0_.refs_4_, bf16[384,256]{1,0:T(8,128)(2,1)S(1)} %in_place.3.g1.refs_1_.refs_6_, ...), custom_call_target="tpu_custom_call", output_to_operand_aliasing={{0}: (10, {})} | custom-call | flops 600000000 | bytes 1 | tf_op jit(solution)/shard_map/weight_rows/pallas_call | solution.py:70
  48.3 0.0 collective-permute-done.15.arrived_ref
  48.3 1.3 %last_grads.1 = (bf16[192,4096]{1,0:T(8,128)(2,1)}, f32[1,192]{1,0:T(1,128)}) custom-call(f32[192,4096]{1,0:T(8,128)S(1)} %get-tuple-element.174.before_ref, bf16[208,4096]{1,0:T(8,128)(2,1)S(1)} %collective-permute-done.15.arrived_ref, f32[192,4096]{1,0:T(8,128)S(1)} %slope_of.1.slope, f32[2,192]{1,0:T(2,128)S(1)} %get-tuple-element.176.spread_ref), custom_call_target="tpu_custom_call" | custom-call | flops 600000000 | bytes 1 | tf_op jit(solution)/shard_map/last_grads/pallas_call | solution.py:70
  (4 shorter events, 0.1 us)
Async XLA Ops:
  0.6 6.3 %collective-permute-start = (bf16[192,4096]{1,0:T(8,128)(2,1)}, bf16[192,4096]{1,0:T(8,128)(2,1)S(1)}, u32[]{:S(2)}, u32[]{:S(2)}) collective-permute-start(bf16[192,4096]{1,0:T(8,128)(2,1)} %bitcast.15), channel_id=1, source_target_pairs={{0,1},{1,0},{2,3},{3,2},{4,5},{5,4},{6,7},{7,6},{8,9},{9,8},{10,11... | collective-permute-start | bytes 4718600 | tf_op jit(solution)/shard_map/ppermute | solution.py:20
  0.8 16.7 %collective-permute-start.5 = (bf16[192]{0:T(256)(128)(2,1)}, bf16[192]{0:T(256)(128)(2,1)S(1)}, u32[]{:S(2)}, u32[]{:S(2)}) collective-permute-start(bf16[192]{0:T(256)(128)(2,1)} %param.5), channel_id=1, source_target_pairs={{0,1},{1,0},{2,3},{3,2},{4,5},{5,4},{6,7},{7,6},{8,9},{9,8},{10,11... | collective-permute-start | bytes 1160 | tf_op jit(solution)/shard_map/ppermute | solution.py:20
  4.6 9.0 %collective-permute-start.1 = (bf16[192,256]{1,0:T(8,128)(2,1)S(1)}, bf16[192,256]{1,0:T(8,128)(2,1)S(1)}, u32[]{:S(2)}, u32[]{:S(2)}) collective-permute-start(bf16[192,256]{1,0:T(8,128)(2,1)S(1)} %get-tuple-element.94), channel_id=1, source_target_pairs={{0,2},{2,0},{1,3},{3,1},{4,6},{6,4},{5,7},{7,5},{8,10},{10,8},{9,1... | collective-permute-start | bytes 294920 | tf_op jit(solution)/shard_map/ppermute | solution.py:20
  8.6 5.0 %collective-permute-start.2 = (bf16[192,256]{1,0:T(8,128)(2,1)S(1)}, bf16[192,256]{1,0:T(8,128)(2,1)S(1)}, u32[]{:S(2)}, u32[]{:S(2)}) collective-permute-start(bf16[192,256]{1,0:T(8,128)(2,1)S(1)} %get-tuple-element.99), channel_id=1, source_target_pairs={{0,2},{2,0},{1,3},{3,1},{4,6},{6,4},{5,7},{7,5},{8,10},{10,8},{9,1... | collective-permute-start | bytes 294920 | tf_op jit(solution)/shard_map/ppermute | solution.py:20
  10.3 7.2 %collective-permute-start.4 = (bf16[384,256]{1,0:T(8,128)(2,1)S(1)}, bf16[384,256]{1,0:T(8,128)(2,1)S(1)}, u32[]{:S(2)}, u32[]{:S(2)}) collective-permute-start(bf16[384,256]{1,0:T(8,128)(2,1)S(1)} %get-tuple-element.102), channel_id=1, source_target_pairs={{0,2},{2,0},{1,3},{3,1},{4,6},{6,4},{5,7},{7,5},{8,10},{10,8},{9,1... | collective-permute-start | bytes 589832 | tf_op jit(solution)/shard_map/ppermute | solution.py:20
  13.8 4.4 %collective-permute-start.3 = (bf16[192,256]{1,0:T(8,128)(2,1)S(1)}, bf16[192,256]{1,0:T(8,128)(2,1)S(1)}, u32[]{:S(2)}, u32[]{:S(2)}) collective-permute-start(bf16[192,256]{1,0:T(8,128)(2,1)S(1)} %get-tuple-element.109), channel_id=1, source_target_pairs={{0,4},{4,0},{8,12},{12,8},{1,5},{5,1},{9,13},{13,9},{2,6},{6,2},{1... | collective-permute-start | bytes 294920 | tf_op jit(solution)/shard_map/ppermute | solution.py:20
  16.6 0.8 %copy-start = (bf16[192]{0:T(256)(128)(2,1)S(1)}, bf16[192]{0:T(256)(128)(2,1)}, u32[]{:S(2)}) copy-start(bf16[192]{0:T(256)(128)(2,1)} %param.5) | copy-start | bytes 1156
  17.8 3.6 %collective-permute-start.7 = (bf16[208,256]{1,0:T(8,128)(2,1)S(1)}, bf16[208,256]{1,0:T(8,128)(2,1)S(1)}, u32[]{:S(2)}, u32[]{:S(2)}) collective-permute-start(bf16[208,256]{1,0:T(8,128)(2,1)S(1)} %get-tuple-element.119), channel_id=1, source_target_pairs={{0,4},{4,0},{8,12},{12,8},{1,5},{5,1},{9,13},{13,9},{2,6},{6,2},{1... | collective-permute-start | bytes 319496 | tf_op jit(solution)/shard_map/ppermute | solution.py:20
  18.2 5.7 %collective-permute-start.6 = (bf16[192,256]{1,0:T(8,128)(2,1)S(1)}, bf16[192,256]{1,0:T(8,128)(2,1)S(1)}, u32[]{:S(2)}, u32[]{:S(2)}) collective-permute-start(bf16[192,256]{1,0:T(8,128)(2,1)S(1)} %get-tuple-element.123), channel_id=1, source_target_pairs={{0,8},{4,12},{8,0},{12,4},{1,9},{5,13},{9,1},{13,5},{2,10},{6,14},... | collective-permute-start | bytes 294920 | tf_op jit(solution)/shard_map/ppermute | solution.py:20
  21.5 8.1 %collective-permute-start.9 = (bf16[208,256]{1,0:T(8,128)(2,1)S(1)}, bf16[208,256]{1,0:T(8,128)(2,1)S(1)}, u32[]{:S(2)}, u32[]{:S(2)}) collective-permute-start(bf16[208,256]{1,0:T(8,128)(2,1)S(1)} %get-tuple-element.128), channel_id=1, source_target_pairs={{0,8},{4,12},{8,0},{12,4},{1,9},{5,13},{9,1},{13,5},{2,10},{6,14},... | collective-permute-start | bytes 319496 | tf_op jit(solution)/shard_map/ppermute | solution.py:20
  23.9 6.2 %collective-permute-start.8 = (bf16[192,256]{1,0:T(8,128)(2,1)S(1)}, bf16[192,256]{1,0:T(8,128)(2,1)S(1)}, u32[]{:S(2)}, u32[]{:S(2)}) collective-permute-start(bf16[192,256]{1,0:T(8,128)(2,1)S(1)} %get-tuple-element.132), channel_id=1, source_target_pairs={{0,4},{4,0},{8,12},{12,8},{1,5},{5,1},{9,13},{13,9},{2,6},{6,2},{1... | collective-permute-start | bytes 294920 | tf_op jit(solution)/shard_map/ppermute | solution.py:20
  25.2 12.2 %collective-permute-start.11 = (bf16[192,256]{1,0:T(8,128)(2,1)S(1)}, bf16[192,256]{1,0:T(8,128)(2,1)S(1)}, u32[]{:S(2)}, u32[]{:S(2)}) collective-permute-start(bf16[192,256]{1,0:T(8,128)(2,1)S(1)} %kept_gradient.2), channel_id=1, source_target_pairs={{0,2},{2,0},{1,3},{3,1},{4,6},{6,4},{5,7},{7,5},{8,10},{10,8},{9,1... | collective-permute-start | bytes 294920 | tf_op jit(solution)/shard_map/ppermute | solution.py:20
  29.6 4.8 %collective-permute-start.10 = (bf16[192,256]{1,0:T(8,128)(2,1)S(1)}, bf16[192,256]{1,0:T(8,128)(2,1)S(1)}, u32[]{:S(2)}, u32[]{:S(2)}) collective-permute-start(bf16[192,256]{1,0:T(8,128)(2,1)S(1)} %get-tuple-element.139), channel_id=1, source_target_pairs={{0,4},{4,0},{8,12},{12,8},{1,5},{5,1},{9,13},{13,9},{2,6},{6,2},{1... | collective-permute-start | bytes 294920 | tf_op jit(solution)/shard_map/ppermute | solution.py:20
  29.8 7.6 %collective-permute-start.13 = (bf16[192,256]{1,0:T(8,128)(2,1)S(1)}, bf16[192,256]{1,0:T(8,128)(2,1)S(1)}, u32[]{:S(2)}, u32[]{:S(2)}) collective-permute-start(bf16[192,256]{1,0:T(8,128)(2,1)S(1)} %kept_gradient.3), channel_id=1, source_target_pairs={{0,2},{2,0},{1,3},{3,1},{4,6},{6,4},{5,7},{7,5},{8,10},{10,8},{9,1... | collective-permute-start | bytes 294920 | tf_op jit(solution)/shard_map/ppermute | solution.py:20
  30.5 6.9 %collective-permute-start.12 = (bf16[192,256]{1,0:T(8,128)(2,1)S(1)}, bf16[192,256]{1,0:T(8,128)(2,1)S(1)}, u32[]{:S(2)}, u32[]{:S(2)}) collective-permute-start(bf16[192,256]{1,0:T(8,128)(2,1)S(1)} %get-tuple-element.144), channel_id=1, source_target_pairs={{0,2},{2,0},{1,3},{3,1},{4,6},{6,4},{5,7},{7,5},{8,10},{10,8},{9,1... | collective-permute-start | bytes 294920 | tf_op jit(solution)/shard_map/ppermute | solution.py:20
  34.8 4.2 %collective-permute-start.14 = (bf16[208,256]{1,0:T(8,128)(2,1)S(1)}, bf16[208,256]{1,0:T(8,128)(2,1)S(1)}, u32[]{:S(2)}, u32[]{:S(2)}) collective-permute-start(bf16[208,256]{1,0:T(8,128)(2,1)S(1)} %get-tuple-element.152), channel_id=1, source_target_pairs={{0,2},{2,0},{1,3},{3,1},{4,6},{6,4},{5,7},{7,5},{8,10},{10,8},{9,1... | collective-permute-start | bytes 319496 | tf_op jit(solution)/shard_map/ppermute | solution.py:20
  40.0 8.3 %collective-permute-start.15 = (bf16[208,4096]{1,0:T(8,128)(2,1)S(1)}, bf16[208,4096]{1,0:T(8,128)(2,1)S(1)}, u32[]{:S(2)}, u32[]{:S(2)}) collective-permute-start(bf16[208,4096]{1,0:T(8,128)(2,1)S(1)} %get-tuple-element.167), channel_id=1, source_target_pairs={{0,1},{1,0},{2,3},{3,2},{4,5},{5,4},{6,7},{7,6},{8,9},{9,8},{10,11... | collective-permute-start | bytes 5111816 | tf_op jit(solution)/shard_map/ppermute | solution.py:20

commit v4 on v3

--- a/solution.py
+++ b/solution.py
@@ -11,7 +11,7 @@
 NT = (((1,), (1,)), ((), ()))
 TN = (((0,), (0,)), ((), ()))
 PIECES = 2
-WORK = 0.6
+WORK = 0.45
 VMEM_LIMIT = 16 * 2**20
 
 
@@ -111,8 +111,10 @@
     spans = 4
     width = units // spans
 
-    def kernel(starts_ref, source_ref, weights_ref, sent_ref, hidden_ref, held, pre, total, sems):
+    def kernel(starts_ref, source_ref, weights_ref, sent_ref, hidden_ref, *refs):
+        held, following, pre, total, sems, sem = refs
         rows = pl.ds(number(starts_ref, 0, half), half)
+        later = pl.ds(number(starts_ref, 2, half), half)
 
         def copies(at):
             span = pl.ds(pl.multiple_of(at * width, width), width)
@@ -127,20 +129,17 @@
             for copy in copies(at)[1]:
                 copy.start()
 
-        start(0)
-        start(1)
+        for at in range(spans):
+            start(at)
+        copy = start_copy(weights_ref.at[later, :], following, sem)
         total[...] = jnp.zeros_like(total)
 
         def step(at, carry):
-            @pl.when(at + 2 < spans)
-            def _():
-                start(at + 2)
-
             span, pair = copies(at)
             for copy in pair:
                 copy.wait()
             hidden = silu(pre[:, span])
-            hidden_ref[:, span] = hidden
+            hidden_ref[pl.ds(0, steps), span] = hidden
             total[...] += lax.dot_general(
                 hidden, held[:, span], NT, preferred_element_type=F32
             )
@@ -148,26 +147,34 @@
 
         lax.fori_loop(0, spans, step, 0)
         sent_ref[...] = total[...].astype(BF16)
+        copy.wait()
 
     return call(
         kernel,
         [
             in_vmem((steps, half), BF16),
-            in_vmem((steps, units), BF16),
+            in_vmem((2 * steps, units), BF16),
+            in_vmem((half, units), BF16),
             in_vmem((half, units), BF16),
             in_vmem((steps, units), BF16),
         ],
         [VMEM, HBM, HBM],
-        [pltpu.VMEM((steps, half), F32), pltpu.SemaphoreType.DMA((2, spans))],
+        [
+            pltpu.VMEM((steps, half), F32),
+            pltpu.SemaphoreType.DMA((2, spans)),
+            pltpu.SemaphoreType.DMA,
+        ],
         name="load_first",
     )(starts, source, weights)
 
 
-def load_second(source, weights, starts, held, following):
+def load_second(source, weights, starts, held, hidden, following):
     steps, units = source.shape
     half = held.shape[0]
 
-    def kernel(starts_ref, source_ref, weights_ref, held_ref, out_ref, hidden_ref, block, sem):
+    def kernel(
+        starts_ref, source_ref, weights_ref, held_ref, _, out_ref, hidden_ref, block, sem
+    ):
         first = number(starts_ref, following, half)
         copy = start_copy(weights_ref.at[pl.ds(first, half), :], block, sem)
 
@@ -176,7 +183,7 @@
             total = None
             for span in cuts(units, 4):
                 hidden = silu(source_ref[:, span])
-                hidden_ref[:, span] = hidden
+                hidden_ref[pl.ds(steps, steps), span] = hidden
                 term = lax.dot_general(hidden, held_ref[:, span], NT, preferred_element_type=F32)
                 total = term if total is None else total + term
             out_ref[...] = total.astype(BF16)
@@ -187,50 +194,44 @@
         kernel,
         [
             in_vmem((steps, half), BF16),
-            in_vmem((steps, units), BF16),
+            in_vmem((2 * steps, units), BF16),
             in_vmem((half, units), BF16),
         ],
-        [VMEM, VMEM, HBM, VMEM],
+        [VMEM, VMEM, HBM, VMEM, VMEM],
         [pltpu.SemaphoreType.DMA],
+        aliases={4: 1},
         name="load_second",
-    )(starts, source, weights, held)
+    )(starts, source, weights, held, hidden)
 
 
 def project(hidden, rows, out_type, weights, starts, following):
-    steps, units = hidden[0].shape
+    steps, units = hidden.shape
     half = rows.shape[0]
-    more = following is not None
-
-    def products(hidden_refs, rows_ref, out_ref):
-        for at, hidden_ref in enumerate(hidden_refs):
-            total = lax.dot_general(
-                hidden_ref[...], rows_ref[...], NT, preferred_element_type=F32
-            )
-            out_ref[pl.ds(at * steps, steps), :] = total.astype(out_type)
-
-    def kernel(first, second, rows_ref, out_ref):
-        products((first, second), rows_ref, out_ref)
-
-    def loading(starts_ref, weights_ref, first, second, rows_ref, out_ref, block, sem):
+
+    def product(hidden_ref, rows_ref, out_ref):
+        total = lax.dot_general(hidden_ref[...], rows_ref[...], NT, preferred_element_type=F32)
+        out_ref[...] = total.astype(out_type)
+
+    def loading(starts_ref, weights_ref, hidden_ref, rows_ref, out_ref, block, sem):
         start = number(starts_ref, following, half)
         copy = start_copy(weights_ref.at[pl.ds(start, half), :], block, sem)
 
         @pl.when(start >= 0)
         def _():
-            products((first, second), rows_ref, out_ref)
+            product(hidden_ref, rows_ref, out_ref)
 
         copy.wait()
 
-    out_shape = in_vmem((2 * steps, half), out_type)
-    if not more:
-        return [call(kernel, out_shape, [VMEM] * 3, name="project")(*hidden, rows)]
+    out_shape = in_vmem((steps, half), out_type)
+    if following is None:
+        return [call(product, out_shape, [VMEM] * 2, name="project")(hidden, rows)]
     return call(
         loading,
         [out_shape, in_vmem((half, units), BF16)],
-        [VMEM, HBM, VMEM, VMEM, VMEM],
+        [VMEM, HBM, VMEM, VMEM],
         [pltpu.SemaphoreType.DMA],
         name="project",
-    )(starts, weights, *hidden, rows)
+    )(starts, weights, hidden, rows)
 
 
 def lane_sums(value):
@@ -327,7 +328,7 @@
     )(*operands)
 
 
-def gradient_of(total, arriving, predicted, starts, cotangents, members, factor, sums):
+def gradient_of(total, arriving, predicted, starts, cotangents, members, factor, sums, passed):
     steps, width = total.shape
     squares, previous, packed = sums
 
@@ -335,6 +336,9 @@
         refs, mean_ref = list(refs[:-1]), refs[-1]
         previous_ref = refs.pop(0) if previous is not None else None
         squares_ref = refs.pop(0) if squares is not None else None
+        if passed is not None:
+            passed_ref = refs.pop(0)
+            refs[0][pl.ds(steps, steps), :] = passed_ref[...]
         sent_ref, grad_ref, sums_ref = refs
         mean_ref[half_of(starts_ref[7, 0], steps), :] = total_ref[...] / members
         mean_ref[half_of(1 - starts_ref[7, 0], steps), :] = arriving_ref[...].astype(F32) / members
@@ -356,11 +360,12 @@
             sent_ref[pl.ds(steps, 16), :] = split(both, width)
 
     operands = [starts, total, arriving, predicted, *cotangents]
-    operands += [value for value in (previous, squares) if value is not None]
+    operands += [value for value in (previous, squares, passed) if value is not None]
+    below = 16 * packed if passed is None else steps
     return call(
         kernel,
         [
-            in_vmem((steps + 16 * packed, width), BF16),
+            in_vmem((steps + below, width), BF16),
             in_vmem((2 * steps, width), BF16),
             in_vmem((2, steps), F32),
         ],
@@ -370,9 +375,9 @@
     )(*operands)
 
 
-def in_place(kept, rest, starts, steps):
+def in_place(kept, rest, starts, steps, offset):
     def kernel(starts_ref, kept_ref, rest_ref, out_ref):
-        out_ref[half_of(starts_ref[7, 0], steps), :] = kept_ref[...]
+        out_ref[half_of(starts_ref[7, 0], steps), :] = kept_ref[pl.ds(offset, steps), :]
         out_ref[half_of(1 - starts_ref[7, 0], steps), :] = rest_ref[pl.ds(0, steps), :]
 
     out_shape = in_vmem((2 * steps, kept.shape[1]), BF16)
@@ -392,7 +397,7 @@
 
     def kernel(g0, rows0, g1, rows1, before_ref, spread_ref, arriving_ref, out_ref, sum_ref):
         for span in cuts(units, 4):
-            total = before_ref[:, span]
+            total = before_ref[pl.ds(steps, steps), span]
             for grad, rows in ((g0, rows0), (g1, rows1)):
                 total += jnp.dot(
                     grad[pl.ds(steps, steps), :], rows[:, span], preferred_element_type=F32
@@ -411,69 +416,97 @@
     )
 
 
-def block_rows(grad, hidden, steps, rows):
-    total = None
-    for at, held in enumerate(hidden):
-        term = lax.dot_general(
-            grad[pl.ds(at * steps, steps), rows], held[...], TN, preferred_element_type=F32
-        )
-        total = term if total is None else total + term
-    return total.astype(BF16)
-
-
-def write_rows(start, grad, hidden, steps, made, out_ref, sems):
-    copies = []
-    for at, rows in enumerate(cuts(made.shape[0], 2)):
-        made[rows, :] = block_rows(grad, hidden, steps, rows)
-        to = pl.ds(pl.multiple_of(start + rows.start, rows.size), rows.size)
-        copies.append(start_copy(made.at[rows, :], out_ref.at[to, :], sems.at[at]))
-    return copies
-
-
-def add_back(refs, pairs, added, sum_ref, part):
-    steps, units = sum_ref.shape
-    for span in cuts(units, 4):
-        out = refs[2 * pairs][:, span] if added else None
-        for at in range(pairs):
-            grad, rows = refs[2 * at : 2 * at + 2]
-            term = jnp.dot(
-                grad[pl.ds(part * steps, steps), :], rows[:, span], preferred_element_type=F32
+def send_block(made, at, span, starts_ref, block, out_ref, sem):
+    half = made.shape[1]
+    to = pl.ds(number(starts_ref, block, half), half)
+    return start_copy(made.at[at, :, span], out_ref.at[to, span], sem)
+
+
+def kept_products(kept, hidden, rows, starts):
+    (steps, half), units = kept.shape, rows.shape[1]
+
+    def kernel(starts_ref, kept_ref, h, rows_ref, term_ref, back_ref):
+        part = half_of(starts_ref[7, 0], steps)
+        for span in cuts(units, 4):
+            term = lax.dot_general(kept_ref[...], h[part, span], TN, preferred_element_type=F32)
+            term_ref[:, span] = term.astype(BF16)
+            back_ref[:, span] = jnp.dot(
+                kept_ref[...], rows_ref[:, span], preferred_element_type=F32
             )
-            out = term if out is None else out + term
-        sum_ref[:, span] = out
-
-
-def weight_rows(grads, hidden, starts, blocks, features, started=None, back=()):
-    half, (steps, units) = grads[0].shape[1], hidden[0].shape
-    started = [] if started is None else [started]
-    operands = []
-    for _, pairs, before in back:
-        operands += [value for pair in pairs for value in pair]
-        operands += [] if before is None else [before]
-    count = len(grads)
-
-    def kernel(starts_ref, *refs):
-        grad_refs, held, refs = refs[:count], refs[count : count + 2], refs[count + 2 :]
-        out_ref, *sum_refs, made, sems = refs[len(operands) + len(started) :]
+
+    shapes = [in_vmem((half, units), BF16), in_vmem((steps, units), F32)]
+    return call(kernel, shapes, [VMEM] * 4, name="kept_products")(starts, kept, hidden, rows)
+
+
+def first_blocks(first, second, term, hidden, starts, blocks, features, rows, kept_back):
+    half, (steps, units) = first.shape[1], kept_back.shape
+
+    def kernel(starts_ref, g0, g1, term_ref, h, w0, w1, kept_ref, out_ref, sum_ref, made, sems):
+        kept, rest = half_of(starts_ref[7, 0], steps), half_of(1 - starts_ref[7, 0], steps)
         copies = []
-        for at, (grad, block) in enumerate(zip(grad_refs, blocks)):
-            copies += write_rows(
-                starts_ref[block, 0], grad, held, steps, made.at[at], out_ref, sems.at[at]
+        for at, span in enumerate(cuts(units, 4)):
+            total = lax.dot_general(g1[...], h[:, span], TN, preferred_element_type=F32)
+            made[1, :, span] = total.astype(BF16)
+            copies.append(
+                send_block(made, 1, span, starts_ref, blocks[1], out_ref, sems.at[1, at])
             )
-        for (part, pairs, before), sum_ref in zip(back, sum_refs):
-            add_back(refs, len(pairs), before is not None, sum_ref, part)
-            refs = refs[2 * len(pairs) + (before is not None) :]
+        for at, span in enumerate(cuts(units, 4)):
+            total = lax.dot_general(g0[rest, :], h[rest, span], TN, preferred_element_type=F32)
+            made[0, :, span] = (total + term_ref[:, span].astype(F32)).astype(BF16)
+            copies.append(
+                send_block(made, 0, span, starts_ref, blocks[0], out_ref, sems.at[0, at])
+            )
+        for span in cuts(units, 4):
+            for part, more in ((kept, kept_ref), (rest, None)):
+                total = jnp.dot(g1[part, :], w1[:, span], preferred_element_type=F32)
+                if more is None:
+                    total += jnp.dot(g0[part, :], w0[:, span], preferred_element_type=F32)
+                else:
+                    total += more[:, span]
+                sum_ref[part, span] = total
         for copy in copies:
             copy.wait()
 
     return call(
         kernel,
-        [in_hbm((features, units), BF16)] + [in_vmem((steps, units), F32)] * len(back),
-        [VMEM] * (3 + count + len(operands)) + [HBM] * len(started),
-        [pltpu.VMEM((count, half, units), BF16), pltpu.SemaphoreType.DMA((count, 2))],
-        aliases={3 + count + len(operands): 0} if started else None,
-        name="weight_rows",
-    )(starts, *grads, *hidden, *operands, *started)
+        [in_hbm((features, units), BF16), in_vmem((2 * steps, units), F32)],
+        [VMEM] * 8,
+        [pltpu.VMEM((2, half, units), BF16), pltpu.SemaphoreType.DMA((2, 4))],
+        name="first_blocks",
+    )(starts, first, second, term, hidden, *rows, kept_back)
+
+
+def last_blocks(grads, hidden, starts, blocks, started, rows, before):
+    (features, units), half = started.shape, grads[0].shape[1]
+    steps = before.shape[0] // 2
+
+    def kernel(starts_ref, g0, g1, h, w0, w1, before_ref, _, out_ref, sum_ref, made, sems):
+        copies = []
+        for block, grad in enumerate((g0, g1)):
+            for at, span in enumerate(cuts(units, 4)):
+                total = lax.dot_general(grad[...], h[:, span], TN, preferred_element_type=F32)
+                made[block, :, span] = total.astype(BF16)
+                copies.append(
+                    send_block(
+                        made, block, span, starts_ref, blocks[block], out_ref, sems.at[block, at]
+                    )
+                )
+        own = pl.ds(0, steps)
+        for span in cuts(units, 4):
+            total = jnp.dot(g0[own, :], w0[:, span], preferred_element_type=F32)
+            total += jnp.dot(g1[own, :], w1[:, span], preferred_element_type=F32)
+            sum_ref[:, span] = total + before_ref[own, span]
+        for copy in copies:
+            copy.wait()
+
+    return call(
+        kernel,
+        [in_hbm((features, units), BF16), in_vmem((steps, units), F32)],
+        [VMEM] * 7 + [HBM],
+        [pltpu.VMEM((2, half, units), BF16), pltpu.SemaphoreType.DMA((2, 4))],
+        aliases={7: 0},
+        name="last_blocks",
+    )(starts, *grads, hidden, *rows, before, started)
 
 
 def slope_of(pre_act):
@@ -608,15 +641,14 @@
         return share, swap(share, "tensor", far)
 
     def early_gradient(self, cotangents, members, factor):
-        grad = self.order(
+        return self.order(
             lambda total: kept_gradient(
                 total, self.predicted, self.starts, cotangents, members, factor
             ),
             self.sum,
         )
-        self.kept = self.gather(grad)
-
-    def gradient(self, cotangents, members, factor):
+
+    def gradient(self, cotangents, members, factor, passed=None):
         *near, far = shares(lax.axis_size("tensor"))
         packed = self.last and not near and self.sum.shape[1] >= self.sum.shape[0]
         sums = (
@@ -634,6 +666,7 @@
                 members,
                 factor,
                 sums,
+                passed,
             ),
             self.sum,
             self.arriving,
@@ -650,7 +683,7 @@
     def together(self, which):
         steps = self.sum.shape[0]
         return self.order(
-            lambda kept, rest: in_place(kept, rest, self.starts, steps),
+            lambda kept, rest: in_place(kept, rest, self.starts, steps, self.offset),
             self.kept[which],
             self.rest[which],
         )
@@ -673,7 +706,6 @@
     starts = jnp.broadcast_to(jnp.stack(starts).astype(jnp.int32)[:, None], (8, 128))
 
     pre_other = swap(pre_act, "seq", 1)
-    cot_other = swap(cotangent, "seq", 1)
     pre_act, starts = lax.optimization_barrier((pre_act, starts))
     order = Order()
     pieces = []
@@ -681,20 +713,19 @@
         previous = pieces[-1] if pieces else None
         pieces.append(Piece(order, starts, at == PIECES - 1, previous))
     blocks = [None] * (2 * PIECES)
-    sent, hidden, blocks[0], pre_act = order(
+    sent, hidden, blocks[0], blocks[2], pre_act = order(
         lambda p: load_first(p, weights, starts, half), pre_act
     )
     pieces[0].leave(sent)
-    sent, hidden_other, blocks[2] = order(
-        lambda p: load_second(p, weights, starts, blocks[0], 2), pre_other
+    sent, hidden, blocks[1] = order(
+        lambda p, h: load_second(p, weights, starts, blocks[0], h, 1), pre_other, hidden
     )
     pieces[0].leave(sent)
-    both = [hidden, hidden_other]
 
     def products(at, following):
         out = order(
             lambda rows: project(
-                both, rows, F32 if at % 2 else BF16, weights, starts, following
+                hidden, rows, F32 if at % 2 else BF16, weights, starts, following
             ),
             blocks[at],
         )
@@ -703,16 +734,13 @@
         return out[0]
 
     a, b = pieces
-    b.leave(products(2, 1))
-    a.total = products(1, 3)
+    b.leave(products(2, 3))
+    a.total = products(1, None)
     a.scatter_rest()
     a.predict()
     b.total = products(3, None)
     slope = order(slope_of, pre_act)
-    cotangents = [
-        order(lambda c: jnp.broadcast_to(c[:, None], (steps, 128)), value)
-        for value in (cotangent, cot_other)
-    ]
+    cot_other = swap(order(lambda c: c, cotangent), "seq", 1)
     b.scatter_rest()
     b.predict()
     a_steps, b_steps = a.ensemble_steps(), b.ensemble_steps()
@@ -720,46 +748,46 @@
     for _ in b.far:
         next(b_steps)
         next(a_steps, None)
-    a.early_gradient(cotangents, members, factor)
+    cotangents = [
+        order(lambda c: jnp.broadcast_to(c[:, None], (steps, 128)), value)
+        for value in (cotangent, cot_other)
+    ]
+    kept = a.early_gradient(cotangents, members, factor)
+    a.kept, a.offset = a.gather(kept), 0
+    rows_early, rows_late = [blocks[1], blocks[3]], [blocks[0], blocks[2]]
     next(b_steps, None)
-    b.early_gradient(cotangents, members, factor)
-    a.gradient(cotangents, members, factor)
-
-    def rows_of(shares, at, started, back):
-        return order(
-            lambda started, *shares: weight_rows(
-                shares,
-                both,
-                starts,
-                at,
-                features,
-                started,
-                [
-                    (part, [(shares[n], blocks[at[n]]) for n in range(len(at))], before)
-                    for part, before in back
-                ],
-            ),
-            started,
-            *shares,
-        )
-
-    sides = [(1, None), (0, None)]
-    weight_grads, before_other, before = rows_of([a.share], [1], None, sides)
+    term, kept_back = order(
+        lambda g: kept_products(g, hidden, blocks[1], starts), a.kept[0]
+    )
+    kept = b.early_gradient(cotangents, members, factor)
+    a.kept = a.kept[0], order(lambda x: x, a.kept[1])
+    a.gradient(cotangents, members, factor, kept)
+    b.kept, b.offset = a.rest, steps
     b.gradient(cotangents, members, factor)
-    sides = [(1, before_other), (0, before)]
-    weight_grads, before_other, before = rows_of([b.share], [3], weight_grads, sides)
+    weight_grads, before = order(
+        lambda x, y: first_blocks(
+            x, y, term, hidden, starts, [1, 3], features, rows_early, kept_back
+        ),
+        a.share,
+        b.share,
+    )
     a_other = a.together(1)
     b_other = b.together(1)
     leaving, spread = order(
         lambda x, y, z: leave_to_other(
-            (x, blocks[0]), (y, blocks[2]), before_other, b.sums, z, steps
+            (x, blocks[0]), (y, blocks[2]), before, b.sums, z, steps
         ),
         a_other,
         b_other,
         b.other_sums,
     )
     arrived = swap(leaving, "seq", 1)
-    weight_grads, before = rows_of([a_other, b_other], [0, 2], weight_grads, [(0, before)])
+    weight_grads, before = order(
+        lambda x, y, s: last_blocks([x, y], hidden, starts, [0, 2], s, rows_late, before),
+        a_other,
+        b_other,
+        weight_grads,
+    )
     act_grads, reward = order(
         lambda g, s: last_grads(g, s, slope, spread, model_width), before, arrived
     )

time: 50 us -> 47.6 us (0.952)
  waiting for transfers between devices: 6.9 us -> 2.56 us
  starting transfers between devices: 18.4 us -> 22 us
  Pallas kernels: 23.1 us -> 21.7 us
    ppermute x16 -> x15, waiting for transfers between devices: 6.9 us -> 2.56 us  [swap(): return lax.ppermute(value, axis, [(i, i ^ distance) for i in range(size)])]
    ppermute x16 -> x15, starting transfers between devices: 18.4 us -> 22 us  [swap(): return lax.ppermute(value, axis, [(i, i ^ distance) for i in range(size)])]
    pallas_call x23, Pallas kernels: 23.1 us -> 21.7 us  [placed(): result = run(*operands)]
  transfers between devices with their start and end apart: 16 -> 15, of which waited for: 4 -> 4; matrix products, arithmetic and copies ran while one was open for 1% -> 1% of each run, Pallas kernels for 42% -> 41%
where the time goes in v4:
time: 47.6 us; the launch traced here: 47.5 us
  starting transfers between devices  22 us (46%)
  Pallas kernels  21.7 us (46%)
  waiting for transfers between devices  2.56 us (5%)
  between operations  0.83 us (2%)
    ppermute x15, starting transfers between devices, swap(): return lax.ppermute(value, axis, [(i, i ^ distance) for i in range(size)])  22 us
    pallas_call x23, Pallas kernels, placed(): result = run(*operands)  21.7 us
    ppermute x15, waiting for transfers between devices, swap(): return lax.ppermute(value, axis, [(i, i ^ distance) for i in range(size)])  2.56 us
  transfers between devices with their start and end apart: 15, of which 4 were waited for; matrix products, arithmetic and copies ran while one was open for 1% of the time, Pallas kernels for 41%

profile of v4, /device:TPU:1, one launch (start us, length us, event | category | flops | bytes accessed | tf_op | source)
XLA Modules:
  0.0 47.5 jit_solution(13641084390121142443)
XLA Ops:
  0.6 0.1 collective-permute-start
  0.8 0.1 stack.23
  0.8 0.1 broadcast_in_dim.10.starts_ref
  0.9 2.8 %load_first.1 = (bf16[192,256]{1,0:T(8,128)(2,1)S(1)}, bf16[384,4096]{1,0:T(8,128)(2,1)S(1)}, bf16[256,4096]{1,0:T(8,128)(2,1)S(1)}, bf16[256,4096]{1,0:T(8,128)(2,1)S(1)}, bf16[192,4096]{1,0:T(8,128)(2,1)S(1)}) custom-call(s32[8,128]{1,0:T(8,128)S(1)} %broadcast_in_dim.10.starts_ref, bf16[192,4096]{1,0:T(8,128)(2,1)} %bitcast.15, bf16[1024,4096]{1,0:T(8,128)(2,1)} %bitcast.10), custom_call_target="tpu_custom_call" | custom-call | flops 450000000 | bytes 1 | tf_op jit(solution)/shard_map/load_first/pallas_call | solution.py:70
  3.7 2.7 %collective-permute-start.1 = (bf16[192,256]{1,0:T(8,128)(2,1)S(1)}, bf16[192,256]{1,0:T(8,128)(2,1)S(1)}, u32[]{:S(2)}, u32[]{:S(2)}) collective-permute-start(bf16[192,256]{1,0:T(8,128)(2,1)S(1)} %get-tuple-element.94), channel_id=1, source_target_pairs={{0,2},{2,0},{1,3},{3,1},{4,6},{6,4},{5,7},{7,5},{8,10},{10,8},{9,1... | collective-permute-start | bytes 294920 | tf_op jit(solution)/shard_map/ppermute | solution.py:20
  6.5 0.0 collective-permute-done.source_ref
  6.5 1.6 %load_second.1 = (bf16[192,256]{1,0:T(8,128)(2,1)S(1)}, bf16[384,4096]{1,0:T(8,128)(2,1)S(1)}, bf16[256,4096]{1,0:T(8,128)(2,1)S(1)}) custom-call(s32[8,128]{1,0:T(8,128)S(1)} %broadcast_in_dim.10.starts_ref, bf16[192,4096]{1,0:T(8,128)(2,1)S(1)} %collective-permute-done.source_ref, bf16[1024,4096]{1,0:T(8,128)(2,1)} %bitcast.11, ...), custom_call_target="tpu_custom_call", output_to_operand_aliasing={{1}: (4, {})} | custom-call | flops 450000000 | bytes 1 | tf_op jit(solution)/shard_map/load_second/pallas_call | solution.py:70
  8.1 0.2 collective-permute-start.2
  8.4 1.6 %project.3 = (bf16[384,256]{1,0:T(8,128)(2,1)S(1)}, bf16[256,4096]{1,0:T(8,128)(2,1)S(1)}) custom-call(s32[8,128]{1,0:T(8,128)S(1)} %broadcast_in_dim.10.starts_ref, bf16[1024,4096]{1,0:T(8,128)(2,1)} %bitcast.12, bf16[384,4096]{1,0:T(8,128)(2,1)S(1)} %get-tuple-element.98.hidden_ref.h, bf16[256,4096]{1,0:T(8,128)(2,1)S(1)} %get-tuple-element.102.rows_ref.rows1.w1), custom_call_target="tpu_custom_call" | custom-call | flops 450000000 | bytes 1 | tf_op jit(solution)/shard_map/project/pallas_call | solution.py:70
  10.0 1.3 %collective-permute-start.4 = (bf16[384,256]{1,0:T(8,128)(2,1)S(1)}, bf16[384,256]{1,0:T(8,128)(2,1)S(1)}, u32[]{:S(2)}, u32[]{:S(2)}) collective-permute-start(bf16[384,256]{1,0:T(8,128)(2,1)S(1)} %get-tuple-element.103), channel_id=1, source_target_pairs={{0,2},{2,0},{1,3},{3,1},{4,6},{6,4},{5,7},{7,5},{8,10},{10,8},{9,1... | collective-permute-start | bytes 589832 | tf_op jit(solution)/shard_map/ppermute | solution.py:20
  11.4 1.0 %project.4.kept_ref = f32[384,256]{1,0:T(8,128)S(1)} custom-call(bf16[384,4096]{1,0:T(8,128)(2,1)S(1)} %get-tuple-element.98.hidden_ref.h, bf16[256,4096]{1,0:T(8,128)(2,1)S(1)} %get-tuple-element.104.rows_ref.w0), custom_call_target="tpu_custom_call" | custom-call | flops 450000000 | bytes 1 | tf_op jit(solution)/shard_map/project/pallas_call | solution.py:70
  12.4 0.0 collective-permute-done.1.refs_0_
  12.4 0.0 collective-permute-done.2.refs_1_
  12.4 0.2 predicted.2
  12.6 1.4 %collective-permute-start.3 = (bf16[192,256]{1,0:T(8,128)(2,1)S(1)}, bf16[192,256]{1,0:T(8,128)(2,1)S(1)}, u32[]{:S(2)}, u32[]{:S(2)}) collective-permute-start(bf16[192,256]{1,0:T(8,128)(2,1)S(1)} %get-tuple-element.109), channel_id=1, source_target_pairs={{0,4},{4,0},{8,12},{12,8},{1,5},{5,1},{9,13},{13,9},{2,6},{6,2},{1... | collective-permute-start | bytes 294920 | tf_op jit(solution)/shard_map/ppermute | solution.py:20
  13.9 1.0 %project.5.kept_ref = f32[384,256]{1,0:T(8,128)S(1)} custom-call(bf16[384,4096]{1,0:T(8,128)(2,1)S(1)} %get-tuple-element.98.hidden_ref.h, bf16[256,4096]{1,0:T(8,128)(2,1)S(1)} %get-tuple-element.111.rows_ref.w1), custom_call_target="tpu_custom_call" | custom-call | flops 450000000 | bytes 1 | tf_op jit(solution)/shard_map/project/pallas_call | solution.py:70
  14.9 0.8 %slope_of.1.slope = f32[192,4096]{1,0:T(8,128)S(1)} custom-call(bf16[192,4096]{1,0:T(8,128)(2,1)S(1)} %get-tuple-element.113.pre), custom_call_target="tpu_custom_call" | custom-call | flops 450000000 | bytes 1 | tf_op jit(solution)/shard_map/slope_of/pallas_call | solution.py:70
  15.7 0.6 %collective-permute-done.4.refs_0_ = bf16[384,256]{1,0:T(8,128)(2,1)S(1)} collective-permute-done((bf16[384,256]{1,0:T(8,128)(2,1)S(1)}, bf16[384,256]{1,0:T(8,128)(2,1)S(1)}, u32[]{:S(2)}, u32[]{:S(2)}) %collective-permute-start.4) | collective-permute-done | bytes 196640 | tf_op jit(solution)/shard_map/ppermute | solution.py:20
  16.3 0.0 copy-start
  16.3 0.2 predicted.3
  16.5 1.3 %collective-permute-start.6 = (bf16[208,256]{1,0:T(8,128)(2,1)S(1)}, bf16[208,256]{1,0:T(8,128)(2,1)S(1)}, u32[]{:S(2)}, u32[]{:S(2)}) collective-permute-start(bf16[208,256]{1,0:T(8,128)(2,1)S(1)} %get-tuple-element.118), channel_id=1, source_target_pairs={{0,4},{4,0},{8,12},{12,8},{1,5},{5,1},{9,13},{13,9},{2,6},{6,2},{1... | collective-permute-start | bytes 319496 | tf_op jit(solution)/shard_map/ppermute | solution.py:20
  17.8 0.0 collective-permute-done.3.arriving_ref
  17.8 0.1 sum_of.4
  17.9 2.4 %collective-permute-start.5 = (bf16[192,256]{1,0:T(8,128)(2,1)S(1)}, bf16[192,256]{1,0:T(8,128)(2,1)S(1)}, u32[]{:S(2)}, u32[]{:S(2)}) collective-permute-start(bf16[192,256]{1,0:T(8,128)(2,1)S(1)} %get-tuple-element.122), channel_id=1, source_target_pairs={{0,8},{4,12},{8,0},{12,4},{1,9},{5,13},{9,1},{13,5},{2,10},{6,14},... | collective-permute-start | bytes 294920 | tf_op jit(solution)/shard_map/ppermute | solution.py:20
  20.3 0.0 collective-permute-done.6.arriving_ref
  20.3 0.1 sum_of.5
  20.3 2.2 %collective-permute-start.9 = (bf16[208,256]{1,0:T(8,128)(2,1)S(1)}, bf16[208,256]{1,0:T(8,128)(2,1)S(1)}, u32[]{:S(2)}, u32[]{:S(2)}) collective-permute-start(bf16[208,256]{1,0:T(8,128)(2,1)S(1)} %get-tuple-element.127), channel_id=1, source_target_pairs={{0,8},{4,12},{8,0},{12,4},{1,9},{5,13},{9,1},{13,5},{2,10},{6,14},... | collective-permute-start | bytes 319496 | tf_op jit(solution)/shard_map/ppermute | solution.py:20
  22.5 0.0 copy-done
  22.5 3.2 %collective-permute-start.7 = (bf16[192]{0:T(256)(128)(2,1)S(1)}, bf16[192]{0:T(256)(128)(2,1)S(1)}, u32[]{:S(2)}, u32[]{:S(2)}) collective-permute-start(bf16[192]{0:T(256)(128)(2,1)S(1)} %copy-done), channel_id=1, source_target_pairs={{0,1},{1,0},{2,3},{3,2},{4,5},{5,4},{6,7},{7,6},{8,9},{9,8},{10,11... | collective-permute-start | bytes 1160 | tf_op jit(solution)/shard_map/ppermute | solution.py:20
  25.7 0.0 collective-permute-done.5.arriving_ref
  25.7 1.4 %collective-permute-start.10 = (bf16[192,256]{1,0:T(8,128)(2,1)S(1)}, bf16[192,256]{1,0:T(8,128)(2,1)S(1)}, u32[]{:S(2)}, u32[]{:S(2)}) collective-permute-start(bf16[192,256]{1,0:T(8,128)(2,1)S(1)} %get-tuple-element.131), channel_id=1, source_target_pairs={{0,4},{4,0},{8,12},{12,8},{1,5},{5,1},{9,13},{13,9},{2,6},{6,2},{1... | collective-permute-start | bytes 294920 | tf_op jit(solution)/shard_map/ppermute | solution.py:20
  27.1 0.0 collective-permute-done.7
  27.1 0.1 broadcast_in_dim.11.own
  27.2 0.1 broadcast_in_dim.12.other
  27.3 0.1 kept_gradient.2.kept_ref
  27.5 1.0 %collective-permute-start.8 = (bf16[192,256]{1,0:T(8,128)(2,1)S(1)}, bf16[192,256]{1,0:T(8,128)(2,1)S(1)}, u32[]{:S(2)}, u32[]{:S(2)}) collective-permute-start(bf16[192,256]{1,0:T(8,128)(2,1)S(1)} %kept_gradient.2.kept_ref), channel_id=1, source_target_pairs={{0,2},{2,0},{1,3},{3,1},{4,6},{6,4},{5,7},{7,5},{8,10},{10,8},{9,1... | collective-permute-start | bytes 294920 | tf_op jit(solution)/shard_map/ppermute | solution.py:20
  28.5 0.6 %collective-permute-done.9.arriving_ref = bf16[208,256]{1,0:T(8,128)(2,1)S(1)} collective-permute-done((bf16[208,256]{1,0:T(8,128)(2,1)S(1)}, bf16[208,256]{1,0:T(8,128)(2,1)S(1)}, u32[]{:S(2)}, u32[]{:S(2)}) %collective-permute-start.9) | collective-permute-done | bytes 106528 | tf_op jit(solution)/shard_map/ppermute | solution.py:20
  29.1 0.2 collective-permute-start.12
  29.3 1.1 %kept_products.1 = (bf16[256,4096]{1,0:T(8,128)(2,1)S(1)}, f32[192,4096]{1,0:T(8,128)S(1)}) custom-call(s32[8,128]{1,0:T(8,128)S(1)} %broadcast_in_dim.10.starts_ref, bf16[192,256]{1,0:T(8,128)(2,1)S(1)} %kept_gradient.2.kept_ref, bf16[384,4096]{1,0:T(8,128)(2,1)S(1)} %get-tuple-element.98.hidden_ref.h, bf16[256,4096]{1,0:T(8,128)(2,1)S(1)} %get-tuple-element.104.rows_ref.w0), custom_call_target="tpu_custom_call" | custom-call | flops 450000000 | bytes 1 | tf_op jit(solution)/shard_map/kept_products/pallas_call | solution.py:70
  30.4 0.1 kept_gradient.3.refs_0_
  30.6 0.4 collective-permute-done.8.kept_ref
  31.0 0.0 collective-permute-done.10.arriving_ref
  31.0 0.3 gradient.2
  31.3 1.0 %collective-permute-start.11 = (bf16[384,256]{1,0:T(8,128)(2,1)S(1)}, bf16[384,256]{1,0:T(8,128)(2,1)S(1)}, u32[]{:S(2)}, u32[]{:S(2)}) collective-permute-start(bf16[384,256]{1,0:T(8,128)(2,1)S(1)} %get-tuple-element.147), channel_id=1, source_target_pairs={{0,2},{2,0},{1,3},{3,1},{4,6},{6,4},{5,7},{7,5},{8,10},{10,8},{9,1... | collective-permute-start | bytes 589832 | tf_op jit(solution)/shard_map/ppermute | solution.py:20
  32.3 0.9 %collective-permute-done.12.arriving_ref = bf16[192,256]{1,0:T(8,128)(2,1)S(1)} collective-permute-done((bf16[192,256]{1,0:T(8,128)(2,1)S(1)}, bf16[192,256]{1,0:T(8,128)(2,1)S(1)}, u32[]{:S(2)}, u32[]{:S(2)}) %collective-permute-start.12) | collective-permute-done | bytes 98336 | tf_op jit(solution)/shard_map/ppermute | solution.py:20
  33.2 0.3 gradient.3
  33.5 1.0 %collective-permute-start.13 = (bf16[208,256]{1,0:T(8,128)(2,1)S(1)}, bf16[208,256]{1,0:T(8,128)(2,1)S(1)}, u32[]{:S(2)}, u32[]{:S(2)}) collective-permute-start(bf16[208,256]{1,0:T(8,128)(2,1)S(1)} %get-tuple-element.154), channel_id=1, source_target_pairs={{0,2},{2,0},{1,3},{3,1},{4,6},{6,4},{5,7},{7,5},{8,10},{10,8},{9,1... | collective-permute-start | bytes 319496 | tf_op jit(solution)/shard_map/ppermute | solution.py:20
  34.5 3.9 %first_blocks.1 = (bf16[1024,4096]{1,0:T(8,128)(2,1)}, f32[384,4096]{1,0:T(8,128)S(1)}) custom-call(s32[8,128]{1,0:T(8,128)S(1)} %broadcast_in_dim.10.starts_ref, bf16[384,256]{1,0:T(8,128)(2,1)S(1)} %get-tuple-element.155.g0, bf16[384,256]{1,0:T(8,128)(2,1)S(1)} %get-tuple-element.156.g1, bf16[256,4096]{1,0:T(8,128)(2,1)S(1)} %get-tuple-element.142.term_ref, ...), custom_call_target="tpu_custom_call" | custom-call | flops 450000000 | bytes 1 | tf_op jit(solution)/shard_map/first_blocks/pallas_call | solution.py:70
  38.4 0.0 collective-permute-done.11.rest_ref.kept_ref
  38.4 0.1 in_place.2.g0
  38.5 0.0 collective-permute-done.13.rest_ref.arriving_ref
  38.5 0.1 in_place.3.g1
  38.5 1.0 %leave_to_other.1 = (bf16[208,4096]{1,0:T(8,128)(2,1)S(1)}, f32[2,192]{1,0:T(2,128)S(1)}) custom-call(bf16[384,256]{1,0:T(8,128)(2,1)S(1)} %in_place.2.g0, bf16[256,4096]{1,0:T(8,128)(2,1)S(1)} %get-tuple-element.96.held_ref.rows0.w0, bf16[384,256]{1,0:T(8,128)(2,1)S(1)} %in_place.3.g1, bf16[256,4096]{1,0:T(8,128)(2,1)S(1)} %get-tuple-element.102.rows_ref.rows1.w1, ...), custom_call_target="tpu_custom_call" | custom-call | flops 450000000 | bytes 1 | tf_op jit(solution)/shard_map/leave_to_other/pallas_call | solution.py:70
  39.6 2.6 %collective-permute-start.14 = (bf16[208,4096]{1,0:T(8,128)(2,1)S(1)}, bf16[208,4096]{1,0:T(8,128)(2,1)S(1)}, u32[]{:S(2)}, u32[]{:S(2)}) collective-permute-start(bf16[208,4096]{1,0:T(8,128)(2,1)S(1)} %get-tuple-element.168), channel_id=1, source_target_pairs={{0,1},{1,0},{2,3},{3,2},{4,5},{5,4},{6,7},{7,6},{8,9},{9,8},{10,11... | collective-permute-start | bytes 5111816 | tf_op jit(solution)/shard_map/ppermute | solution.py:20
  42.2 4.0 %last_blocks.1 = (bf16[1024,4096]{1,0:T(8,128)(2,1)}, f32[192,4096]{1,0:T(8,128)S(1)}) custom-call(s32[8,128]{1,0:T(8,128)S(1)} %broadcast_in_dim.10.starts_ref, bf16[384,256]{1,0:T(8,128)(2,1)S(1)} %in_place.2.g0, bf16[384,256]{1,0:T(8,128)(2,1)S(1)} %in_place.3.g1, ...), custom_call_target="tpu_custom_call", output_to_operand_aliasing={{0}: (7, {})} | custom-call | flops 450000000 | bytes 1 | tf_op jit(solution)/shard_map/last_blocks/pallas_call | solution.py:70
  46.2 0.0 collective-permute-done.14.arrived_ref
  46.2 1.3 %last_grads.1 = (bf16[192,4096]{1,0:T(8,128)(2,1)}, f32[1,192]{1,0:T(1,128)}) custom-call(f32[192,4096]{1,0:T(8,128)S(1)} %get-tuple-element.174.before_ref, bf16[208,4096]{1,0:T(8,128)(2,1)S(1)} %collective-permute-done.14.arrived_ref, f32[192,4096]{1,0:T(8,128)S(1)} %slope_of.1.slope, f32[2,192]{1,0:T(2,128)S(1)} %get-tuple-element.176.spread_ref), custom_call_target="tpu_custom_call" | custom-call | flops 450000000 | bytes 1 | tf_op jit(solution)/shard_map/last_grads/pallas_call | solution.py:70
  (3 shorter events, 0.1 us)
Async XLA Ops:
  0.6 5.8 %collective-permute-start = (bf16[192,4096]{1,0:T(8,128)(2,1)}, bf16[192,4096]{1,0:T(8,128)(2,1)S(1)}, u32[]{:S(2)}, u32[]{:S(2)}) collective-permute-start(bf16[192,4096]{1,0:T(8,128)(2,1)} %bitcast.14), channel_id=1, source_target_pairs={{0,1},{1,0},{2,3},{3,2},{4,5},{5,4},{6,7},{7,6},{8,9},{9,8},{10,11... | collective-permute-start | bytes 4718600 | tf_op jit(solution)/shard_map/ppermute | solution.py:20
  3.7 8.6 %collective-permute-start.1 = (bf16[192,256]{1,0:T(8,128)(2,1)S(1)}, bf16[192,256]{1,0:T(8,128)(2,1)S(1)}, u32[]{:S(2)}, u32[]{:S(2)}) collective-permute-start(bf16[192,256]{1,0:T(8,128)(2,1)S(1)} %get-tuple-element.94), channel_id=1, source_target_pairs={{0,2},{2,0},{1,3},{3,1},{4,6},{6,4},{5,7},{7,5},{8,10},{10,8},{9,1... | collective-permute-start | bytes 294920 | tf_op jit(solution)/shard_map/ppermute | solution.py:20
  8.1 4.3 %collective-permute-start.2 = (bf16[192,256]{1,0:T(8,128)(2,1)S(1)}, bf16[192,256]{1,0:T(8,128)(2,1)S(1)}, u32[]{:S(2)}, u32[]{:S(2)}) collective-permute-start(bf16[192,256]{1,0:T(8,128)(2,1)S(1)} %get-tuple-element.101), channel_id=1, source_target_pairs={{0,2},{2,0},{1,3},{3,1},{4,6},{6,4},{5,7},{7,5},{8,10},{10,8},{9,1... | collective-permute-start | bytes 294920 | tf_op jit(solution)/shard_map/ppermute | solution.py:20
  10.0 6.3 %collective-permute-start.4 = (bf16[384,256]{1,0:T(8,128)(2,1)S(1)}, bf16[384,256]{1,0:T(8,128)(2,1)S(1)}, u32[]{:S(2)}, u32[]{:S(2)}) collective-permute-start(bf16[384,256]{1,0:T(8,128)(2,1)S(1)} %get-tuple-element.103), channel_id=1, source_target_pairs={{0,2},{2,0},{1,3},{3,1},{4,6},{6,4},{5,7},{7,5},{8,10},{10,8},{9,1... | collective-permute-start | bytes 589832 | tf_op jit(solution)/shard_map/ppermute | solution.py:20
  12.6 5.3 %collective-permute-start.3 = (bf16[192,256]{1,0:T(8,128)(2,1)S(1)}, bf16[192,256]{1,0:T(8,128)(2,1)S(1)}, u32[]{:S(2)}, u32[]{:S(2)}) collective-permute-start(bf16[192,256]{1,0:T(8,128)(2,1)S(1)} %get-tuple-element.109), channel_id=1, source_target_pairs={{0,4},{4,0},{8,12},{12,8},{1,5},{5,1},{9,13},{13,9},{2,6},{6,2},{1... | collective-permute-start | bytes 294920 | tf_op jit(solution)/shard_map/ppermute | solution.py:20
  16.3 6.2 %copy-start = (bf16[192]{0:T(256)(128)(2,1)S(1)}, bf16[192]{0:T(256)(128)(2,1)}, u32[]{:S(2)}) copy-start(bf16[192]{0:T(256)(128)(2,1)} %param.5) | copy-start | bytes 1156
  16.5 3.8 %collective-permute-start.6 = (bf16[208,256]{1,0:T(8,128)(2,1)S(1)}, bf16[208,256]{1,0:T(8,128)(2,1)S(1)}, u32[]{:S(2)}, u32[]{:S(2)}) collective-permute-start(bf16[208,256]{1,0:T(8,128)(2,1)S(1)} %get-tuple-element.118), channel_id=1, source_target_pairs={{0,4},{4,0},{8,12},{12,8},{1,5},{5,1},{9,13},{13,9},{2,6},{6,2},{1... | collective-permute-start | bytes 319496 | tf_op jit(solution)/shard_map/ppermute | solution.py:20
  17.9 7.8 %collective-permute-start.5 = (bf16[192,256]{1,0:T(8,128)(2,1)S(1)}, bf16[192,256]{1,0:T(8,128)(2,1)S(1)}, u32[]{:S(2)}, u32[]{:S(2)}) collective-permute-start(bf16[192,256]{1,0:T(8,128)(2,1)S(1)} %get-tuple-element.122), channel_id=1, source_target_pairs={{0,8},{4,12},{8,0},{12,4},{1,9},{5,13},{9,1},{13,5},{2,10},{6,14},... | collective-permute-start | bytes 294920 | tf_op jit(solution)/shard_map/ppermute | solution.py:20
  20.3 8.7 %collective-permute-start.9 = (bf16[208,256]{1,0:T(8,128)(2,1)S(1)}, bf16[208,256]{1,0:T(8,128)(2,1)S(1)}, u32[]{:S(2)}, u32[]{:S(2)}) collective-permute-start(bf16[208,256]{1,0:T(8,128)(2,1)S(1)} %get-tuple-element.127), channel_id=1, source_target_pairs={{0,8},{4,12},{8,0},{12,4},{1,9},{5,13},{9,1},{13,5},{2,10},{6,14},... | collective-permute-start | bytes 319496 | tf_op jit(solution)/shard_map/ppermute | solution.py:20
  22.5 4.6 %collective-permute-start.7 = (bf16[192]{0:T(256)(128)(2,1)S(1)}, bf16[192]{0:T(256)(128)(2,1)S(1)}, u32[]{:S(2)}, u32[]{:S(2)}) collective-permute-start(bf16[192]{0:T(256)(128)(2,1)S(1)} %copy-done), channel_id=1, source_target_pairs={{0,1},{1,0},{2,3},{3,2},{4,5},{5,4},{6,7},{7,6},{8,9},{9,8},{10,11... | collective-permute-start | bytes 1160 | tf_op jit(solution)/shard_map/ppermute | solution.py:20
  25.7 5.3 %collective-permute-start.10 = (bf16[192,256]{1,0:T(8,128)(2,1)S(1)}, bf16[192,256]{1,0:T(8,128)(2,1)S(1)}, u32[]{:S(2)}, u32[]{:S(2)}) collective-permute-start(bf16[192,256]{1,0:T(8,128)(2,1)S(1)} %get-tuple-element.131), channel_id=1, source_target_pairs={{0,4},{4,0},{8,12},{12,8},{1,5},{5,1},{9,13},{13,9},{2,6},{6,2},{1... | collective-permute-start | bytes 294920 | tf_op jit(solution)/shard_map/ppermute | solution.py:20
  27.5 3.5 %collective-permute-start.8 = (bf16[192,256]{1,0:T(8,128)(2,1)S(1)}, bf16[192,256]{1,0:T(8,128)(2,1)S(1)}, u32[]{:S(2)}, u32[]{:S(2)}) collective-permute-start(bf16[192,256]{1,0:T(8,128)(2,1)S(1)} %kept_gradient.2.kept_ref), channel_id=1, source_target_pairs={{0,2},{2,0},{1,3},{3,1},{4,6},{6,4},{5,7},{7,5},{8,10},{10,8},{9,1... | collective-permute-start | bytes 294920 | tf_op jit(solution)/shard_map/ppermute | solution.py:20
  29.1 4.1 %collective-permute-start.12 = (bf16[192,256]{1,0:T(8,128)(2,1)S(1)}, bf16[192,256]{1,0:T(8,128)(2,1)S(1)}, u32[]{:S(2)}, u32[]{:S(2)}) collective-permute-start(bf16[192,256]{1,0:T(8,128)(2,1)S(1)} %get-tuple-element.140), channel_id=1, source_target_pairs={{0,4},{4,0},{8,12},{12,8},{1,5},{5,1},{9,13},{13,9},{2,6},{6,2},{1... | collective-permute-start | bytes 294920 | tf_op jit(solution)/shard_map/ppermute | solution.py:20
  31.3 7.1 %collective-permute-start.11 = (bf16[384,256]{1,0:T(8,128)(2,1)S(1)}, bf16[384,256]{1,0:T(8,128)(2,1)S(1)}, u32[]{:S(2)}, u32[]{:S(2)}) collective-permute-start(bf16[384,256]{1,0:T(8,128)(2,1)S(1)} %get-tuple-element.147), channel_id=1, source_target_pairs={{0,2},{2,0},{1,3},{3,1},{4,6},{6,4},{5,7},{7,5},{8,10},{10,8},{9,1... | collective-permute-start | bytes 589832 | tf_op jit(solution)/shard_map/ppermute | solution.py:20
  33.5 5.0 %collective-permute-start.13 = (bf16[208,256]{1,0:T(8,128)(2,1)S(1)}, bf16[208,256]{1,0:T(8,128)(2,1)S(1)}, u32[]{:S(2)}, u32[]{:S(2)}) collective-permute-start(bf16[208,256]{1,0:T(8,128)(2,1)S(1)} %get-tuple-element.154), channel_id=1, source_target_pairs={{0,2},{2,0},{1,3},{3,1},{4,6},{6,4},{5,7},{7,5},{8,10},{10,8},{9,1... | collective-permute-start | bytes 319496 | tf_op jit(solution)/shard_map/ppermute | solution.py:20
  39.6 6.6 %collective-permute-start.14 = (bf16[208,4096]{1,0:T(8,128)(2,1)S(1)}, bf16[208,4096]{1,0:T(8,128)(2,1)S(1)}, u32[]{:S(2)}, u32[]{:S(2)}) collective-permute-start(bf16[208,4096]{1,0:T(8,128)(2,1)S(1)} %get-tuple-element.168), channel_id=1, source_target_pairs={{0,1},{1,0},{2,3},{3,2},{4,5},{5,4},{6,7},{7,6},{8,9},{9,8},{10,11... | collective-permute-start | bytes 5111816 | tf_op jit(solution)/shard_map/ppermute | solution.py:20

commit v5 on v4

--- a/solution.py
+++ b/solution.py
@@ -11,7 +11,7 @@
 NT = (((1,), (1,)), ((), ()))
 TN = (((0,), (0,)), ((), ()))
 PIECES = 2
-WORK = 0.45
+WORK = 0.4
 VMEM_LIMIT = 16 * 2**20
 
 
@@ -45,7 +45,7 @@
     return pltpu.HBM(shape, dtype)
 
 
-def call(kernel, out_shape, in_specs, scratch=(), aliases=None, name=None):
+def call(kernel, out_shape, in_specs, scratch=(), aliases=None, work=WORK, name=None):
     outs = out_shape if isinstance(out_shape, list) else [out_shape]
     out_specs = [pl.BlockSpec(memory_space=out.memory_space) for out in outs]
     run = pl.pallas_call(
@@ -57,7 +57,7 @@
         input_output_aliases=aliases or {},
         compiler_params=pltpu.CompilerParams(vmem_limit_bytes=VMEM_LIMIT),
         cost_estimate=pl.CostEstimate(
-            flops=int(WORK * 1e9), bytes_accessed=1, transcendentals=0
+            flops=int(work * 1e9), bytes_accessed=1, transcendentals=0
         ),
         name=name,
     )
@@ -224,7 +224,7 @@
 
     out_shape = in_vmem((steps, half), out_type)
     if following is None:
-        return [call(product, out_shape, [VMEM] * 2, name="project")(hidden, rows)]
+        return [call(product, out_shape, [VMEM] * 2, work=2 * WORK, name="project")(hidden, rows)]
     return call(
         loading,
         [out_shape, in_vmem((half, units), BF16)],
@@ -416,10 +416,10 @@
     )
 
 
-def send_block(made, at, span, starts_ref, block, out_ref, sem):
+def send_block(made, at, starts_ref, block, out_ref, sems):
     half = made.shape[1]
     to = pl.ds(number(starts_ref, block, half), half)
-    return start_copy(made.at[at, :, span], out_ref.at[to, span], sem)
+    return start_copy(made.at[at], out_ref.at[to, :], sems.at[at])
 
 
 def kept_products(kept, hidden, rows, starts):
@@ -443,27 +443,26 @@
 
     def kernel(starts_ref, g0, g1, term_ref, h, w0, w1, kept_ref, out_ref, sum_ref, made, sems):
         kept, rest = half_of(starts_ref[7, 0], steps), half_of(1 - starts_ref[7, 0], steps)
-        copies = []
-        for at, span in enumerate(cuts(units, 4)):
+        for span in cuts(units, 4):
             total = lax.dot_general(g1[...], h[:, span], TN, preferred_element_type=F32)
             made[1, :, span] = total.astype(BF16)
-            copies.append(
-                send_block(made, 1, span, starts_ref, blocks[1], out_ref, sems.at[1, at])
-            )
-        for at, span in enumerate(cuts(units, 4)):
+        copies = [send_block(made, 1, starts_ref, blocks[1], out_ref, sems)]
+        for span in cuts(units, 4):
             total = lax.dot_general(g0[rest, :], h[rest, span], TN, preferred_element_type=F32)
             made[0, :, span] = (total + term_ref[:, span].astype(F32)).astype(BF16)
-            copies.append(
-                send_block(made, 0, span, starts_ref, blocks[0], out_ref, sems.at[0, at])
-            )
-        for span in cuts(units, 4):
-            for part, more in ((kept, kept_ref), (rest, None)):
-                total = jnp.dot(g1[part, :], w1[:, span], preferred_element_type=F32)
-                if more is None:
-                    total += jnp.dot(g0[part, :], w0[:, span], preferred_element_type=F32)
-                else:
-                    total += more[:, span]
-                sum_ref[part, span] = total
+        copies.append(send_block(made, 0, starts_ref, blocks[0], out_ref, sems))
+
+        @pl.when(starts_ref[7, 0] >= 0)
+        def _():
+            for span in cuts(units, 4):
+                for part, more in ((kept, kept_ref), (rest, None)):
+                    total = jnp.dot(g1[part, :], w1[:, span], preferred_element_type=F32)
+                    if more is None:
+                        total += jnp.dot(g0[part, :], w0[:, span], preferred_element_type=F32)
+                    else:
+                        total += more[:, span]
+                    sum_ref[part, span] = total
+
         for copy in copies:
             copy.wait()
 
@@ -471,7 +470,7 @@
         kernel,
         [in_hbm((features, units), BF16), in_vmem((2 * steps, units), F32)],
         [VMEM] * 8,
-        [pltpu.VMEM((2, half, units), BF16), pltpu.SemaphoreType.DMA((2, 4))],
+        [pltpu.VMEM((2, half, units), BF16), pltpu.SemaphoreType.DMA((2,))],
         name="first_blocks",
     )(starts, first, second, term, hidden, *rows, kept_back)
 
@@ -482,20 +481,20 @@
 
     def kernel(starts_ref, g0, g1, h, w0, w1, before_ref, _, out_ref, sum_ref, made, sems):
         copies = []
-        for block, grad in enumerate((g0, g1)):
-            for at, span in enumerate(cuts(units, 4)):
+        for at, grad in enumerate((g0, g1)):
+            for span in cuts(units, 4):
                 total = lax.dot_general(grad[...], h[:, span], TN, preferred_element_type=F32)
-                made[block, :, span] = total.astype(BF16)
-                copies.append(
-                    send_block(
-                        made, block, span, starts_ref, blocks[block], out_ref, sems.at[block, at]
-                    )
-                )
-        own = pl.ds(0, steps)
-        for span in cuts(units, 4):
-            total = jnp.dot(g0[own, :], w0[:, span], preferred_element_type=F32)
-            total += jnp.dot(g1[own, :], w1[:, span], preferred_element_type=F32)
-            sum_ref[:, span] = total + before_ref[own, span]
+                made[at, :, span] = total.astype(BF16)
+            copies.append(send_block(made, at, starts_ref, blocks[at], out_ref, sems))
+
+        @pl.when(starts_ref[7, 0] >= 0)
+        def _():
+            own = pl.ds(0, steps)
+            for span in cuts(units, 4):
+                total = jnp.dot(g0[own, :], w0[:, span], preferred_element_type=F32)
+                total += jnp.dot(g1[own, :], w1[:, span], preferred_element_type=F32)
+                sum_ref[:, span] = total + before_ref[own, span]
+
         for copy in copies:
             copy.wait()
 
@@ -503,7 +502,7 @@
         kernel,
         [in_hbm((features, units), BF16), in_vmem((steps, units), F32)],
         [VMEM] * 7 + [HBM],
-        [pltpu.VMEM((2, half, units), BF16), pltpu.SemaphoreType.DMA((2, 4))],
+        [pltpu.VMEM((2, half, units), BF16), pltpu.SemaphoreType.DMA((2,))],
         aliases={7: 0},
         name="last_blocks",
     )(starts, *grads, hidden, *rows, before, started)
@@ -739,7 +738,6 @@
     a.scatter_rest()
     a.predict()
     b.total = products(3, None)
-    slope = order(slope_of, pre_act)
     cot_other = swap(order(lambda c: c, cotangent), "seq", 1)
     b.scatter_rest()
     b.predict()
@@ -747,6 +745,7 @@
     next(a_steps)
     for _ in b.far:
         next(b_steps)
+        slope = order(slope_of, pre_act)
         next(a_steps, None)
     cotangents = [
         order(lambda c: jnp.broadcast_to(c[:, None], (steps, 128)), value)

time: 47.6 us -> 47.4 us (level)
  waiting for transfers between devices: 2.56 us -> 4.84 us
  starting transfers between devices: 22 us -> 20 us
  Pallas kernels: 21.7 us -> 21 us
    ppermute x15, waiting for transfers between devices: 2.56 us -> 4.84 us  [swap(): return lax.ppermute(value, axis, [(i, i ^ distance) for i in range(size)])]
    ppermute x15, starting transfers between devices: 22 us -> 20 us  [swap(): return lax.ppermute(value, axis, [(i, i ^ distance) for i in range(size)])]
    pallas_call x23, Pallas kernels: 21.7 us -> 21 us  [placed(): result = run(*operands)]
  transfers between devices with their start and end apart: 15 -> 15, of which waited for: 4 -> 3; matrix products, arithmetic and copies ran while one was open for 1% -> 1% of each run, Pallas kernels for 41% -> 40%
where the time goes in v5:
time: 47.4 us; the launch traced here: 47.2 us
  Pallas kernels  21 us (44%)
  starting transfers between devices  20 us (42%)
  waiting for transfers between devices  4.84 us (10%)
  between operations  1.02 us (2%)
    pallas_call x23, Pallas kernels, placed(): result = run(*operands)  21 us
    ppermute x15, starting transfers between devices, swap(): return lax.ppermute(value, axis, [(i, i ^ distance) for i in range(size)])  20 us
    ppermute x15, waiting for transfers between devices, swap(): return lax.ppermute(value, axis, [(i, i ^ distance) for i in range(size)])  4.84 us
  transfers between devices with their start and end apart: 15, of which 3 were waited for; matrix products, arithmetic and copies ran while one was open for 1% of the time, Pallas kernels for 40%

profile of v5, /device:TPU:1, one launch (start us, length us, event | category | flops | bytes accessed | tf_op | source)
XLA Modules:
  0.0 47.2 jit_solution(11807169815183785428)
XLA Ops:
  0.6 0.1 collective-permute-start
  0.8 0.1 stack.23
  0.8 0.1 broadcast_in_dim.10.starts_ref
  0.9 2.8 %load_first.1 = (bf16[192,256]{1,0:T(8,128)(2,1)S(1)}, bf16[384,4096]{1,0:T(8,128)(2,1)S(1)}, bf16[256,4096]{1,0:T(8,128)(2,1)S(1)}, bf16[256,4096]{1,0:T(8,128)(2,1)S(1)}, bf16[192,4096]{1,0:T(8,128)(2,1)S(1)}) custom-call(s32[8,128]{1,0:T(8,128)S(1)} %broadcast_in_dim.10.starts_ref, bf16[192,4096]{1,0:T(8,128)(2,1)} %bitcast.15, bf16[1024,4096]{1,0:T(8,128)(2,1)} %bitcast.10), custom_call_target="tpu_custom_call" | custom-call | flops 400000000 | bytes 1 | tf_op jit(solution)/shard_map/load_first/pallas_call | solution.py:70
  3.7 2.7 %collective-permute-start.1 = (bf16[192,256]{1,0:T(8,128)(2,1)S(1)}, bf16[192,256]{1,0:T(8,128)(2,1)S(1)}, u32[]{:S(2)}, u32[]{:S(2)}) collective-permute-start(bf16[192,256]{1,0:T(8,128)(2,1)S(1)} %get-tuple-element.94), channel_id=1, source_target_pairs={{0,2},{2,0},{1,3},{3,1},{4,6},{6,4},{5,7},{7,5},{8,10},{10,8},{9,1... | collective-permute-start | bytes 294920 | tf_op jit(solution)/shard_map/ppermute | solution.py:20
  6.5 0.0 collective-permute-done.source_ref
  6.5 1.6 %load_second.1 = (bf16[192,256]{1,0:T(8,128)(2,1)S(1)}, bf16[384,4096]{1,0:T(8,128)(2,1)S(1)}, bf16[256,4096]{1,0:T(8,128)(2,1)S(1)}) custom-call(s32[8,128]{1,0:T(8,128)S(1)} %broadcast_in_dim.10.starts_ref, bf16[192,4096]{1,0:T(8,128)(2,1)S(1)} %collective-permute-done.source_ref, bf16[1024,4096]{1,0:T(8,128)(2,1)} %bitcast.11, ...), custom_call_target="tpu_custom_call", output_to_operand_aliasing={{1}: (4, {})} | custom-call | flops 400000000 | bytes 1 | tf_op jit(solution)/shard_map/load_second/pallas_call | solution.py:70
  8.1 0.2 collective-permute-start.2
  8.4 1.6 %project.3 = (bf16[384,256]{1,0:T(8,128)(2,1)S(1)}, bf16[256,4096]{1,0:T(8,128)(2,1)S(1)}) custom-call(s32[8,128]{1,0:T(8,128)S(1)} %broadcast_in_dim.10.starts_ref, bf16[1024,4096]{1,0:T(8,128)(2,1)} %bitcast.12, bf16[384,4096]{1,0:T(8,128)(2,1)S(1)} %get-tuple-element.98.hidden_ref.h, bf16[256,4096]{1,0:T(8,128)(2,1)S(1)} %get-tuple-element.102.rows_ref.rows1.w1), custom_call_target="tpu_custom_call" | custom-call | flops 400000000 | bytes 1 | tf_op jit(solution)/shard_map/project/pallas_call | solution.py:70
  10.0 1.3 %collective-permute-start.4 = (bf16[384,256]{1,0:T(8,128)(2,1)S(1)}, bf16[384,256]{1,0:T(8,128)(2,1)S(1)}, u32[]{:S(2)}, u32[]{:S(2)}) collective-permute-start(bf16[384,256]{1,0:T(8,128)(2,1)S(1)} %get-tuple-element.103), channel_id=1, source_target_pairs={{0,2},{2,0},{1,3},{3,1},{4,6},{6,4},{5,7},{7,5},{8,10},{10,8},{9,1... | collective-permute-start | bytes 589832 | tf_op jit(solution)/shard_map/ppermute | solution.py:20
  11.4 1.0 %project.4.kept_ref = f32[384,256]{1,0:T(8,128)S(1)} custom-call(bf16[384,4096]{1,0:T(8,128)(2,1)S(1)} %get-tuple-element.98.hidden_ref.h, bf16[256,4096]{1,0:T(8,128)(2,1)S(1)} %get-tuple-element.104.rows_ref.w0), custom_call_target="tpu_custom_call" | custom-call | flops 800000000 | bytes 1 | tf_op jit(solution)/shard_map/project/pallas_call | solution.py:70
  12.4 0.0 collective-permute-done.1.refs_0_
  12.4 0.0 collective-permute-done.2.refs_1_
  12.4 0.2 predicted.2
  12.6 1.4 %collective-permute-start.3 = (bf16[192,256]{1,0:T(8,128)(2,1)S(1)}, bf16[192,256]{1,0:T(8,128)(2,1)S(1)}, u32[]{:S(2)}, u32[]{:S(2)}) collective-permute-start(bf16[192,256]{1,0:T(8,128)(2,1)S(1)} %get-tuple-element.109), channel_id=1, source_target_pairs={{0,4},{4,0},{8,12},{12,8},{1,5},{5,1},{9,13},{13,9},{2,6},{6,2},{1... | collective-permute-start | bytes 294920 | tf_op jit(solution)/shard_map/ppermute | solution.py:20
  13.9 1.0 %project.5.kept_ref = f32[384,256]{1,0:T(8,128)S(1)} custom-call(bf16[384,4096]{1,0:T(8,128)(2,1)S(1)} %get-tuple-element.98.hidden_ref.h, bf16[256,4096]{1,0:T(8,128)(2,1)S(1)} %get-tuple-element.111.rows_ref.w1), custom_call_target="tpu_custom_call" | custom-call | flops 800000000 | bytes 1 | tf_op jit(solution)/shard_map/project/pallas_call | solution.py:70
  14.9 0.0 copy-start
  14.9 1.4 %collective-permute-done.4.refs_0_ = bf16[384,256]{1,0:T(8,128)(2,1)S(1)} collective-permute-done((bf16[384,256]{1,0:T(8,128)(2,1)S(1)}, bf16[384,256]{1,0:T(8,128)(2,1)S(1)}, u32[]{:S(2)}, u32[]{:S(2)}) %collective-permute-start.4) | collective-permute-done | bytes 196640 | tf_op jit(solution)/shard_map/ppermute | solution.py:20
  16.3 0.2 predicted.3
  16.5 1.3 %collective-permute-start.6 = (bf16[208,256]{1,0:T(8,128)(2,1)S(1)}, bf16[208,256]{1,0:T(8,128)(2,1)S(1)}, u32[]{:S(2)}, u32[]{:S(2)}) collective-permute-start(bf16[208,256]{1,0:T(8,128)(2,1)S(1)} %get-tuple-element.116), channel_id=1, source_target_pairs={{0,4},{4,0},{8,12},{12,8},{1,5},{5,1},{9,13},{13,9},{2,6},{6,2},{1... | collective-permute-start | bytes 319496 | tf_op jit(solution)/shard_map/ppermute | solution.py:20
  17.8 0.0 collective-permute-done.3.arriving_ref
  17.8 0.1 sum_of.4
  17.9 2.4 %collective-permute-start.5 = (bf16[192,256]{1,0:T(8,128)(2,1)S(1)}, bf16[192,256]{1,0:T(8,128)(2,1)S(1)}, u32[]{:S(2)}, u32[]{:S(2)}) collective-permute-start(bf16[192,256]{1,0:T(8,128)(2,1)S(1)} %get-tuple-element.120), channel_id=1, source_target_pairs={{0,8},{4,12},{8,0},{12,4},{1,9},{5,13},{9,1},{13,5},{2,10},{6,14},... | collective-permute-start | bytes 294920 | tf_op jit(solution)/shard_map/ppermute | solution.py:20
  20.3 0.0 copy-done
  20.3 1.9 %collective-permute-start.7 = (bf16[192]{0:T(256)(128)(2,1)S(1)}, bf16[192]{0:T(256)(128)(2,1)S(1)}, u32[]{:S(2)}, u32[]{:S(2)}) collective-permute-start(bf16[192]{0:T(256)(128)(2,1)S(1)} %copy-done), channel_id=1, source_target_pairs={{0,1},{1,0},{2,3},{3,2},{4,5},{5,4},{6,7},{7,6},{8,9},{9,8},{10,11... | collective-permute-start | bytes 1160 | tf_op jit(solution)/shard_map/ppermute | solution.py:20
  22.2 0.0 collective-permute-done.6.arriving_ref
  22.2 0.1 sum_of.5
  22.2 0.3 collective-permute-start.9
  22.5 0.8 %slope_of.1.slope = f32[192,4096]{1,0:T(8,128)S(1)} custom-call(bf16[192,4096]{1,0:T(8,128)(2,1)S(1)} %get-tuple-element.127.pre), custom_call_target="tpu_custom_call" | custom-call | flops 400000000 | bytes 1 | tf_op jit(solution)/shard_map/slope_of/pallas_call | solution.py:70
  23.3 0.0 collective-permute-done.5.arriving_ref
  23.3 1.4 %collective-permute-start.10 = (bf16[192,256]{1,0:T(8,128)(2,1)S(1)}, bf16[192,256]{1,0:T(8,128)(2,1)S(1)}, u32[]{:S(2)}, u32[]{:S(2)}) collective-permute-start(bf16[192,256]{1,0:T(8,128)(2,1)S(1)} %get-tuple-element.131), channel_id=1, source_target_pairs={{0,4},{4,0},{8,12},{12,8},{1,5},{5,1},{9,13},{13,9},{2,6},{6,2},{1... | collective-permute-start | bytes 294920 | tf_op jit(solution)/shard_map/ppermute | solution.py:20
  24.7 0.0 collective-permute-done.7
  24.7 0.1 broadcast_in_dim.11.own
  24.8 0.1 broadcast_in_dim.12.other
  24.9 0.1 kept_gradient.2.kept_ref
  25.0 1.0 %collective-permute-start.8 = (bf16[192,256]{1,0:T(8,128)(2,1)S(1)}, bf16[192,256]{1,0:T(8,128)(2,1)S(1)}, u32[]{:S(2)}, u32[]{:S(2)}) collective-permute-start(bf16[192,256]{1,0:T(8,128)(2,1)S(1)} %kept_gradient.2.kept_ref), channel_id=1, source_target_pairs={{0,2},{2,0},{1,3},{3,1},{4,6},{6,4},{5,7},{7,5},{8,10},{10,8},{9,1... | collective-permute-start | bytes 294920 | tf_op jit(solution)/shard_map/ppermute | solution.py:20
  26.0 2.7 %collective-permute-done.9.arriving_ref = bf16[208,256]{1,0:T(8,128)(2,1)S(1)} collective-permute-done((bf16[208,256]{1,0:T(8,128)(2,1)S(1)}, bf16[208,256]{1,0:T(8,128)(2,1)S(1)}, u32[]{:S(2)}, u32[]{:S(2)}) %collective-permute-start.9) | collective-permute-done | bytes 106528 | tf_op jit(solution)/shard_map/ppermute | solution.py:20
  28.8 0.4 collective-permute-start.12
  29.2 1.1 %kept_products.1 = (bf16[256,4096]{1,0:T(8,128)(2,1)S(1)}, f32[192,4096]{1,0:T(8,128)S(1)}) custom-call(s32[8,128]{1,0:T(8,128)S(1)} %broadcast_in_dim.10.starts_ref, bf16[192,256]{1,0:T(8,128)(2,1)S(1)} %kept_gradient.2.kept_ref, bf16[384,4096]{1,0:T(8,128)(2,1)S(1)} %get-tuple-element.98.hidden_ref.h, bf16[256,4096]{1,0:T(8,128)(2,1)S(1)} %get-tuple-element.104.rows_ref.w0), custom_call_target="tpu_custom_call" | custom-call | flops 400000000 | bytes 1 | tf_op jit(solution)/shard_map/kept_products/pallas_call | solution.py:70
  30.3 0.1 kept_gradient.3.refs_0_
  30.5 0.0 collective-permute-done.8.kept_ref
  30.5 0.0 collective-permute-done.10.arriving_ref
  30.5 0.3 gradient.2
  30.8 1.1 %collective-permute-start.11 = (bf16[384,256]{1,0:T(8,128)(2,1)S(1)}, bf16[384,256]{1,0:T(8,128)(2,1)S(1)}, u32[]{:S(2)}, u32[]{:S(2)}) collective-permute-start(bf16[384,256]{1,0:T(8,128)(2,1)S(1)} %get-tuple-element.147), channel_id=1, source_target_pairs={{0,2},{2,0},{1,3},{3,1},{4,6},{6,4},{5,7},{7,5},{8,10},{10,8},{9,1... | collective-permute-start | bytes 589832 | tf_op jit(solution)/shard_map/ppermute | solution.py:20
  31.9 0.7 %collective-permute-done.12.arriving_ref = bf16[192,256]{1,0:T(8,128)(2,1)S(1)} collective-permute-done((bf16[192,256]{1,0:T(8,128)(2,1)S(1)}, bf16[192,256]{1,0:T(8,128)(2,1)S(1)}, u32[]{:S(2)}, u32[]{:S(2)}) %collective-permute-start.12) | collective-permute-done | bytes 98336 | tf_op jit(solution)/shard_map/ppermute | solution.py:20
  32.6 0.3 gradient.3
  32.9 0.8 %collective-permute-start.13 = (bf16[208,256]{1,0:T(8,128)(2,1)S(1)}, bf16[208,256]{1,0:T(8,128)(2,1)S(1)}, u32[]{:S(2)}, u32[]{:S(2)}) collective-permute-start(bf16[208,256]{1,0:T(8,128)(2,1)S(1)} %get-tuple-element.154), channel_id=1, source_target_pairs={{0,2},{2,0},{1,3},{3,1},{4,6},{6,4},{5,7},{7,5},{8,10},{10,8},{9,1... | collective-permute-start | bytes 319496 | tf_op jit(solution)/shard_map/ppermute | solution.py:20
  33.7 3.5 %first_blocks.1 = (bf16[1024,4096]{1,0:T(8,128)(2,1)}, f32[384,4096]{1,0:T(8,128)S(1)}) custom-call(s32[8,128]{1,0:T(8,128)S(1)} %broadcast_in_dim.10.starts_ref, bf16[384,256]{1,0:T(8,128)(2,1)S(1)} %get-tuple-element.155.g0, bf16[384,256]{1,0:T(8,128)(2,1)S(1)} %get-tuple-element.156.g1, bf16[256,4096]{1,0:T(8,128)(2,1)S(1)} %get-tuple-element.142.term_ref, ...), custom_call_target="tpu_custom_call" | custom-call | flops 400000000 | bytes 1 | tf_op jit(solution)/shard_map/first_blocks/pallas_call | solution.py:70
  37.2 0.0 collective-permute-done.11.rest_ref.kept_ref
  37.2 0.1 in_place.2.g0
  37.3 0.0 collective-permute-done.13.rest_ref.arriving_ref
  37.3 0.1 in_place.3.g1
  37.3 1.0 %leave_to_other.1 = (bf16[208,4096]{1,0:T(8,128)(2,1)S(1)}, f32[2,192]{1,0:T(2,128)S(1)}) custom-call(bf16[384,256]{1,0:T(8,128)(2,1)S(1)} %in_place.2.g0, bf16[256,4096]{1,0:T(8,128)(2,1)S(1)} %get-tuple-element.96.held_ref.rows0.w0, bf16[384,256]{1,0:T(8,128)(2,1)S(1)} %in_place.3.g1, bf16[256,4096]{1,0:T(8,128)(2,1)S(1)} %get-tuple-element.102.rows_ref.rows1.w1, ...), custom_call_target="tpu_custom_call" | custom-call | flops 400000000 | bytes 1 | tf_op jit(solution)/shard_map/leave_to_other/pallas_call | solution.py:70
  38.3 3.7 %collective-permute-start.14 = (bf16[208,4096]{1,0:T(8,128)(2,1)S(1)}, bf16[208,4096]{1,0:T(8,128)(2,1)S(1)}, u32[]{:S(2)}, u32[]{:S(2)}) collective-permute-start(bf16[208,4096]{1,0:T(8,128)(2,1)S(1)} %get-tuple-element.168), channel_id=1, source_target_pairs={{0,1},{1,0},{2,3},{3,2},{4,5},{5,4},{6,7},{7,6},{8,9},{9,8},{10,11... | collective-permute-start | bytes 5111816 | tf_op jit(solution)/shard_map/ppermute | solution.py:20
  42.0 3.7 %last_blocks.1 = (bf16[1024,4096]{1,0:T(8,128)(2,1)}, f32[192,4096]{1,0:T(8,128)S(1)}) custom-call(s32[8,128]{1,0:T(8,128)S(1)} %broadcast_in_dim.10.starts_ref, bf16[384,256]{1,0:T(8,128)(2,1)S(1)} %in_place.2.g0, bf16[384,256]{1,0:T(8,128)(2,1)S(1)} %in_place.3.g1, ...), custom_call_target="tpu_custom_call", output_to_operand_aliasing={{0}: (7, {})} | custom-call | flops 400000000 | bytes 1 | tf_op jit(solution)/shard_map/last_blocks/pallas_call | solution.py:70
  45.8 0.0 collective-permute-done.14.arrived_ref
  45.8 1.3 %last_grads.1 = (bf16[192,4096]{1,0:T(8,128)(2,1)}, f32[1,192]{1,0:T(1,128)}) custom-call(f32[192,4096]{1,0:T(8,128)S(1)} %get-tuple-element.174.before_ref, bf16[208,4096]{1,0:T(8,128)(2,1)S(1)} %collective-permute-done.14.arrived_ref, f32[192,4096]{1,0:T(8,128)S(1)} %slope_of.1.slope, f32[2,192]{1,0:T(2,128)S(1)} %get-tuple-element.176.spread_ref), custom_call_target="tpu_custom_call" | custom-call | flops 400000000 | bytes 1 | tf_op jit(solution)/shard_map/last_grads/pallas_call | solution.py:70
  (3 shorter events, 0.1 us)
Async XLA Ops:
  0.6 5.8 %collective-permute-start = (bf16[192,4096]{1,0:T(8,128)(2,1)}, bf16[192,4096]{1,0:T(8,128)(2,1)S(1)}, u32[]{:S(2)}, u32[]{:S(2)}) collective-permute-start(bf16[192,4096]{1,0:T(8,128)(2,1)} %bitcast.14), channel_id=1, source_target_pairs={{0,1},{1,0},{2,3},{3,2},{4,5},{5,4},{6,7},{7,6},{8,9},{9,8},{10,11... | collective-permute-start | bytes 4718600 | tf_op jit(solution)/shard_map/ppermute | solution.py:20
  3.7 8.6 %collective-permute-start.1 = (bf16[192,256]{1,0:T(8,128)(2,1)S(1)}, bf16[192,256]{1,0:T(8,128)(2,1)S(1)}, u32[]{:S(2)}, u32[]{:S(2)}) collective-permute-start(bf16[192,256]{1,0:T(8,128)(2,1)S(1)} %get-tuple-element.94), channel_id=1, source_target_pairs={{0,2},{2,0},{1,3},{3,1},{4,6},{6,4},{5,7},{7,5},{8,10},{10,8},{9,1... | collective-permute-start | bytes 294920 | tf_op jit(solution)/shard_map/ppermute | solution.py:20
  8.1 4.3 %collective-permute-start.2 = (bf16[192,256]{1,0:T(8,128)(2,1)S(1)}, bf16[192,256]{1,0:T(8,128)(2,1)S(1)}, u32[]{:S(2)}, u32[]{:S(2)}) collective-permute-start(bf16[192,256]{1,0:T(8,128)(2,1)S(1)} %get-tuple-element.101), channel_id=1, source_target_pairs={{0,2},{2,0},{1,3},{3,1},{4,6},{6,4},{5,7},{7,5},{8,10},{10,8},{9,1... | collective-permute-start | bytes 294920 | tf_op jit(solution)/shard_map/ppermute | solution.py:20
  10.0 6.3 %collective-permute-start.4 = (bf16[384,256]{1,0:T(8,128)(2,1)S(1)}, bf16[384,256]{1,0:T(8,128)(2,1)S(1)}, u32[]{:S(2)}, u32[]{:S(2)}) collective-permute-start(bf16[384,256]{1,0:T(8,128)(2,1)S(1)} %get-tuple-element.103), channel_id=1, source_target_pairs={{0,2},{2,0},{1,3},{3,1},{4,6},{6,4},{5,7},{7,5},{8,10},{10,8},{9,1... | collective-permute-start | bytes 589832 | tf_op jit(solution)/shard_map/ppermute | solution.py:20
  12.6 5.3 %collective-permute-start.3 = (bf16[192,256]{1,0:T(8,128)(2,1)S(1)}, bf16[192,256]{1,0:T(8,128)(2,1)S(1)}, u32[]{:S(2)}, u32[]{:S(2)}) collective-permute-start(bf16[192,256]{1,0:T(8,128)(2,1)S(1)} %get-tuple-element.109), channel_id=1, source_target_pairs={{0,4},{4,0},{8,12},{12,8},{1,5},{5,1},{9,13},{13,9},{2,6},{6,2},{1... | collective-permute-start | bytes 294920 | tf_op jit(solution)/shard_map/ppermute | solution.py:20
  14.9 5.3 %copy-start = (bf16[192]{0:T(256)(128)(2,1)S(1)}, bf16[192]{0:T(256)(128)(2,1)}, u32[]{:S(2)}) copy-start(bf16[192]{0:T(256)(128)(2,1)} %param.5) | copy-start | bytes 1156
  16.5 5.7 %collective-permute-start.6 = (bf16[208,256]{1,0:T(8,128)(2,1)S(1)}, bf16[208,256]{1,0:T(8,128)(2,1)S(1)}, u32[]{:S(2)}, u32[]{:S(2)}) collective-permute-start(bf16[208,256]{1,0:T(8,128)(2,1)S(1)} %get-tuple-element.116), channel_id=1, source_target_pairs={{0,4},{4,0},{8,12},{12,8},{1,5},{5,1},{9,13},{13,9},{2,6},{6,2},{1... | collective-permute-start | bytes 319496 | tf_op jit(solution)/shard_map/ppermute | solution.py:20
  17.9 5.4 %collective-permute-start.5 = (bf16[192,256]{1,0:T(8,128)(2,1)S(1)}, bf16[192,256]{1,0:T(8,128)(2,1)S(1)}, u32[]{:S(2)}, u32[]{:S(2)}) collective-permute-start(bf16[192,256]{1,0:T(8,128)(2,1)S(1)} %get-tuple-element.120), channel_id=1, source_target_pairs={{0,8},{4,12},{8,0},{12,4},{1,9},{5,13},{9,1},{13,5},{2,10},{6,14},... | collective-permute-start | bytes 294920 | tf_op jit(solution)/shard_map/ppermute | solution.py:20
  20.3 4.4 %collective-permute-start.7 = (bf16[192]{0:T(256)(128)(2,1)S(1)}, bf16[192]{0:T(256)(128)(2,1)S(1)}, u32[]{:S(2)}, u32[]{:S(2)}) collective-permute-start(bf16[192]{0:T(256)(128)(2,1)S(1)} %copy-done), channel_id=1, source_target_pairs={{0,1},{1,0},{2,3},{3,2},{4,5},{5,4},{6,7},{7,6},{8,9},{9,8},{10,11... | collective-permute-start | bytes 1160 | tf_op jit(solution)/shard_map/ppermute | solution.py:20
  22.2 6.5 %collective-permute-start.9 = (bf16[208,256]{1,0:T(8,128)(2,1)S(1)}, bf16[208,256]{1,0:T(8,128)(2,1)S(1)}, u32[]{:S(2)}, u32[]{:S(2)}) collective-permute-start(bf16[208,256]{1,0:T(8,128)(2,1)S(1)} %get-tuple-element.126), channel_id=1, source_target_pairs={{0,8},{4,12},{8,0},{12,4},{1,9},{5,13},{9,1},{13,5},{2,10},{6,14},... | collective-permute-start | bytes 319496 | tf_op jit(solution)/shard_map/ppermute | solution.py:20
  23.3 7.1 %collective-permute-start.10 = (bf16[192,256]{1,0:T(8,128)(2,1)S(1)}, bf16[192,256]{1,0:T(8,128)(2,1)S(1)}, u32[]{:S(2)}, u32[]{:S(2)}) collective-permute-start(bf16[192,256]{1,0:T(8,128)(2,1)S(1)} %get-tuple-element.131), channel_id=1, source_target_pairs={{0,4},{4,0},{8,12},{12,8},{1,5},{5,1},{9,13},{13,9},{2,6},{6,2},{1... | collective-permute-start | bytes 294920 | tf_op jit(solution)/shard_map/ppermute | solution.py:20
  25.0 5.4 %collective-permute-start.8 = (bf16[192,256]{1,0:T(8,128)(2,1)S(1)}, bf16[192,256]{1,0:T(8,128)(2,1)S(1)}, u32[]{:S(2)}, u32[]{:S(2)}) collective-permute-start(bf16[192,256]{1,0:T(8,128)(2,1)S(1)} %kept_gradient.2.kept_ref), channel_id=1, source_target_pairs={{0,2},{2,0},{1,3},{3,1},{4,6},{6,4},{5,7},{7,5},{8,10},{10,8},{9,1... | collective-permute-start | bytes 294920 | tf_op jit(solution)/shard_map/ppermute | solution.py:20
  28.8 3.8 %collective-permute-start.12 = (bf16[192,256]{1,0:T(8,128)(2,1)S(1)}, bf16[192,256]{1,0:T(8,128)(2,1)S(1)}, u32[]{:S(2)}, u32[]{:S(2)}) collective-permute-start(bf16[192,256]{1,0:T(8,128)(2,1)S(1)} %get-tuple-element.140), channel_id=1, source_target_pairs={{0,4},{4,0},{8,12},{12,8},{1,5},{5,1},{9,13},{13,9},{2,6},{6,2},{1... | collective-permute-start | bytes 294920 | tf_op jit(solution)/shard_map/ppermute | solution.py:20
  30.8 6.4 %collective-permute-start.11 = (bf16[384,256]{1,0:T(8,128)(2,1)S(1)}, bf16[384,256]{1,0:T(8,128)(2,1)S(1)}, u32[]{:S(2)}, u32[]{:S(2)}) collective-permute-start(bf16[384,256]{1,0:T(8,128)(2,1)S(1)} %get-tuple-element.147), channel_id=1, source_target_pairs={{0,2},{2,0},{1,3},{3,1},{4,6},{6,4},{5,7},{7,5},{8,10},{10,8},{9,1... | collective-permute-start | bytes 589832 | tf_op jit(solution)/shard_map/ppermute | solution.py:20
  32.9 4.3 %collective-permute-start.13 = (bf16[208,256]{1,0:T(8,128)(2,1)S(1)}, bf16[208,256]{1,0:T(8,128)(2,1)S(1)}, u32[]{:S(2)}, u32[]{:S(2)}) collective-permute-start(bf16[208,256]{1,0:T(8,128)(2,1)S(1)} %get-tuple-element.154), channel_id=1, source_target_pairs={{0,2},{2,0},{1,3},{3,1},{4,6},{6,4},{5,7},{7,5},{8,10},{10,8},{9,1... | collective-permute-start | bytes 319496 | tf_op jit(solution)/shard_map/ppermute | solution.py:20
  38.3 7.4 %collective-permute-start.14 = (bf16[208,4096]{1,0:T(8,128)(2,1)S(1)}, bf16[208,4096]{1,0:T(8,128)(2,1)S(1)}, u32[]{:S(2)}, u32[]{:S(2)}) collective-permute-start(bf16[208,4096]{1,0:T(8,128)(2,1)S(1)} %get-tuple-element.168), channel_id=1, source_target_pairs={{0,1},{1,0},{2,3},{3,2},{4,5},{5,4},{6,7},{7,6},{8,9},{9,8},{10,11... | collective-permute-start | bytes 5111816 | tf_op jit(solution)/shard_map/ppermute | solution.py:20

commit v6 on v5

--- a/solution.py
+++ b/solution.py
@@ -702,7 +702,8 @@
         starts += [(2 * piece + 1 - high) * half, (2 * piece + high) * half]
     assert len(starts) < 8
     starts += [0] * (7 - len(starts)) + [lax.axis_index("ensemble") % 2]
-    starts = jnp.broadcast_to(jnp.stack(starts).astype(jnp.int32)[:, None], (8, 128))
+    row = lax.broadcasted_iota(jnp.int32, (8, 128), 0)
+    starts = sum(jnp.where(row == at, value, 0) for at, value in enumerate(starts))
 
     pre_other = swap(pre_act, "seq", 1)
     pre_act, starts = lax.optimization_barrier((pre_act, starts))

time: 47.4 us -> 47.3 us (level)
  no operation moved by 1% of the time
where the time goes in v6:
time: 47.3 us; the launch traced here: 47.1 us
  Pallas kernels  21 us (44%)
  starting transfers between devices  20.2 us (43%)
  waiting for transfers between devices  4.7 us (10%)
  between operations  1.02 us (2%)
    pallas_call x23, Pallas kernels, placed(): result = run(*operands)  21 us
    ppermute x15, starting transfers between devices, swap(): return lax.ppermute(value, axis, [(i, i ^ distance) for i in range(size)])  20.2 us
    ppermute x15, waiting for transfers between devices, swap(): return lax.ppermute(value, axis, [(i, i ^ distance) for i in range(size)])  4.7 us
  transfers between devices with their start and end apart: 15, of which 3 were waited for; matrix products, arithmetic and copies ran while one was open for 1% of the time, Pallas kernels for 40%

profile of v6, /device:TPU:1, one launch (start us, length us, event | category | flops | bytes accessed | tf_op | source)
XLA Modules:
  0.0 47.1 jit_solution(8474478706552253320)
XLA Ops:
  0.6 0.1 collective-permute-start
  0.8 0.1 iota.19.starts_ref
  0.8 2.8 %load_first.1 = (bf16[192,256]{1,0:T(8,128)(2,1)S(1)}, bf16[384,4096]{1,0:T(8,128)(2,1)S(1)}, bf16[256,4096]{1,0:T(8,128)(2,1)S(1)}, bf16[256,4096]{1,0:T(8,128)(2,1)S(1)}, bf16[192,4096]{1,0:T(8,128)(2,1)S(1)}) custom-call(s32[8,128]{1,0:T(8,128)S(1)} %iota.19.starts_ref, bf16[192,4096]{1,0:T(8,128)(2,1)} %bitcast.10, bf16[1024,4096]{1,0:T(8,128)(2,1)} %bitcast.5), custom_call_target="tpu_custom_call" | custom-call | flops 400000000 | bytes 1 | tf_op jit(solution)/shard_map/load_first/pallas_call | solution.py:70
  3.7 2.7 %collective-permute-start.1 = (bf16[192,256]{1,0:T(8,128)(2,1)S(1)}, bf16[192,256]{1,0:T(8,128)(2,1)S(1)}, u32[]{:S(2)}, u32[]{:S(2)}) collective-permute-start(bf16[192,256]{1,0:T(8,128)(2,1)S(1)} %get-tuple-element.94), channel_id=1, source_target_pairs={{0,2},{2,0},{1,3},{3,1},{4,6},{6,4},{5,7},{7,5},{8,10},{10,8},{9,1... | collective-permute-start | bytes 294920 | tf_op jit(solution)/shard_map/ppermute | solution.py:20
  6.4 0.0 collective-permute-done.source_ref
  6.4 1.6 %load_second.1 = (bf16[192,256]{1,0:T(8,128)(2,1)S(1)}, bf16[384,4096]{1,0:T(8,128)(2,1)S(1)}, bf16[256,4096]{1,0:T(8,128)(2,1)S(1)}) custom-call(s32[8,128]{1,0:T(8,128)S(1)} %iota.19.starts_ref, bf16[192,4096]{1,0:T(8,128)(2,1)S(1)} %collective-permute-done.source_ref, bf16[1024,4096]{1,0:T(8,128)(2,1)} %bitcast.6, ...), custom_call_target="tpu_custom_call", output_to_operand_aliasing={{1}: (4, {})} | custom-call | flops 400000000 | bytes 1 | tf_op jit(solution)/shard_map/load_second/pallas_call | solution.py:70
  8.0 0.3 collective-permute-start.2
  8.4 1.6 %project.3 = (bf16[384,256]{1,0:T(8,128)(2,1)S(1)}, bf16[256,4096]{1,0:T(8,128)(2,1)S(1)}) custom-call(s32[8,128]{1,0:T(8,128)S(1)} %iota.19.starts_ref, bf16[1024,4096]{1,0:T(8,128)(2,1)} %bitcast.7, bf16[384,4096]{1,0:T(8,128)(2,1)S(1)} %get-tuple-element.98.hidden_ref.h, bf16[256,4096]{1,0:T(8,128)(2,1)S(1)} %get-tuple-element.102.rows_ref.rows1.w1), custom_call_target="tpu_custom_call" | custom-call | flops 400000000 | bytes 1 | tf_op jit(solution)/shard_map/project/pallas_call | solution.py:70
  10.0 1.3 %collective-permute-start.4 = (bf16[384,256]{1,0:T(8,128)(2,1)S(1)}, bf16[384,256]{1,0:T(8,128)(2,1)S(1)}, u32[]{:S(2)}, u32[]{:S(2)}) collective-permute-start(bf16[384,256]{1,0:T(8,128)(2,1)S(1)} %get-tuple-element.103), channel_id=1, source_target_pairs={{0,2},{2,0},{1,3},{3,1},{4,6},{6,4},{5,7},{7,5},{8,10},{10,8},{9,1... | collective-permute-start | bytes 589832 | tf_op jit(solution)/shard_map/ppermute | solution.py:20
  11.3 1.0 %project.4.kept_ref = f32[384,256]{1,0:T(8,128)S(1)} custom-call(bf16[384,4096]{1,0:T(8,128)(2,1)S(1)} %get-tuple-element.98.hidden_ref.h, bf16[256,4096]{1,0:T(8,128)(2,1)S(1)} %get-tuple-element.104.rows_ref.w0), custom_call_target="tpu_custom_call" | custom-call | flops 800000000 | bytes 1 | tf_op jit(solution)/shard_map/project/pallas_call | solution.py:70
  12.3 0.0 collective-permute-done.1.refs_0_
  12.3 0.0 collective-permute-done.2.refs_1_
  12.3 0.2 predicted.2
  12.5 1.4 %collective-permute-start.3 = (bf16[192,256]{1,0:T(8,128)(2,1)S(1)}, bf16[192,256]{1,0:T(8,128)(2,1)S(1)}, u32[]{:S(2)}, u32[]{:S(2)}) collective-permute-start(bf16[192,256]{1,0:T(8,128)(2,1)S(1)} %get-tuple-element.109), channel_id=1, source_target_pairs={{0,4},{4,0},{8,12},{12,8},{1,5},{5,1},{9,13},{13,9},{2,6},{6,2},{1... | collective-permute-start | bytes 294920 | tf_op jit(solution)/shard_map/ppermute | solution.py:20
  13.8 1.0 %project.5.kept_ref = f32[384,256]{1,0:T(8,128)S(1)} custom-call(bf16[384,4096]{1,0:T(8,128)(2,1)S(1)} %get-tuple-element.98.hidden_ref.h, bf16[256,4096]{1,0:T(8,128)(2,1)S(1)} %get-tuple-element.111.rows_ref.w1), custom_call_target="tpu_custom_call" | custom-call | flops 800000000 | bytes 1 | tf_op jit(solution)/shard_map/project/pallas_call | solution.py:70
  14.8 0.0 copy-start
  14.9 1.3 %collective-permute-done.4.refs_0_ = bf16[384,256]{1,0:T(8,128)(2,1)S(1)} collective-permute-done((bf16[384,256]{1,0:T(8,128)(2,1)S(1)}, bf16[384,256]{1,0:T(8,128)(2,1)S(1)}, u32[]{:S(2)}, u32[]{:S(2)}) %collective-permute-start.4) | collective-permute-done | bytes 196640 | tf_op jit(solution)/shard_map/ppermute | solution.py:20
  16.1 0.2 predicted.3
  16.3 1.4 %collective-permute-start.6 = (bf16[208,256]{1,0:T(8,128)(2,1)S(1)}, bf16[208,256]{1,0:T(8,128)(2,1)S(1)}, u32[]{:S(2)}, u32[]{:S(2)}) collective-permute-start(bf16[208,256]{1,0:T(8,128)(2,1)S(1)} %get-tuple-element.116), channel_id=1, source_target_pairs={{0,4},{4,0},{8,12},{12,8},{1,5},{5,1},{9,13},{13,9},{2,6},{6,2},{1... | collective-permute-start | bytes 319496 | tf_op jit(solution)/shard_map/ppermute | solution.py:20
  17.7 0.0 collective-permute-done.3.arriving_ref
  17.7 0.1 sum_of.4
  17.7 2.4 %collective-permute-start.5 = (bf16[192,256]{1,0:T(8,128)(2,1)S(1)}, bf16[192,256]{1,0:T(8,128)(2,1)S(1)}, u32[]{:S(2)}, u32[]{:S(2)}) collective-permute-start(bf16[192,256]{1,0:T(8,128)(2,1)S(1)} %get-tuple-element.120), channel_id=1, source_target_pairs={{0,8},{4,12},{8,0},{12,4},{1,9},{5,13},{9,1},{13,5},{2,10},{6,14},... | collective-permute-start | bytes 294920 | tf_op jit(solution)/shard_map/ppermute | solution.py:20
  20.1 0.0 copy-done
  20.1 1.9 %collective-permute-start.7 = (bf16[192]{0:T(256)(128)(2,1)S(1)}, bf16[192]{0:T(256)(128)(2,1)S(1)}, u32[]{:S(2)}, u32[]{:S(2)}) collective-permute-start(bf16[192]{0:T(256)(128)(2,1)S(1)} %copy-done), channel_id=1, source_target_pairs={{0,1},{1,0},{2,3},{3,2},{4,5},{5,4},{6,7},{7,6},{8,9},{9,8},{10,11... | collective-permute-start | bytes 1160 | tf_op jit(solution)/shard_map/ppermute | solution.py:20
  22.1 0.0 collective-permute-done.6.arriving_ref
  22.1 0.1 sum_of.5
  22.1 0.2 collective-permute-start.9
  22.4 0.8 %slope_of.1.slope = f32[192,4096]{1,0:T(8,128)S(1)} custom-call(bf16[192,4096]{1,0:T(8,128)(2,1)S(1)} %get-tuple-element.127.pre), custom_call_target="tpu_custom_call" | custom-call | flops 400000000 | bytes 1 | tf_op jit(solution)/shard_map/slope_of/pallas_call | solution.py:70
  23.1 0.0 collective-permute-done.5.arriving_ref
  23.2 1.4 %collective-permute-start.10 = (bf16[192,256]{1,0:T(8,128)(2,1)S(1)}, bf16[192,256]{1,0:T(8,128)(2,1)S(1)}, u32[]{:S(2)}, u32[]{:S(2)}) collective-permute-start(bf16[192,256]{1,0:T(8,128)(2,1)S(1)} %get-tuple-element.131), channel_id=1, source_target_pairs={{0,4},{4,0},{8,12},{12,8},{1,5},{5,1},{9,13},{13,9},{2,6},{6,2},{1... | collective-permute-start | bytes 294920 | tf_op jit(solution)/shard_map/ppermute | solution.py:20
  24.6 0.0 collective-permute-done.7
  24.6 0.1 broadcast_in_dim.53.own
  24.7 0.1 broadcast_in_dim.54.other
  24.7 0.1 kept_gradient.2.kept_ref
  24.9 1.1 %collective-permute-start.8 = (bf16[192,256]{1,0:T(8,128)(2,1)S(1)}, bf16[192,256]{1,0:T(8,128)(2,1)S(1)}, u32[]{:S(2)}, u32[]{:S(2)}) collective-permute-start(bf16[192,256]{1,0:T(8,128)(2,1)S(1)} %kept_gradient.2.kept_ref), channel_id=1, source_target_pairs={{0,2},{2,0},{1,3},{3,1},{4,6},{6,4},{5,7},{7,5},{8,10},{10,8},{9,1... | collective-permute-start | bytes 294920 | tf_op jit(solution)/shard_map/ppermute | solution.py:20
  25.9 2.7 %collective-permute-done.9.arriving_ref = bf16[208,256]{1,0:T(8,128)(2,1)S(1)} collective-permute-done((bf16[208,256]{1,0:T(8,128)(2,1)S(1)}, bf16[208,256]{1,0:T(8,128)(2,1)S(1)}, u32[]{:S(2)}, u32[]{:S(2)}) %collective-permute-start.9) | collective-permute-done | bytes 106528 | tf_op jit(solution)/shard_map/ppermute | solution.py:20
  28.7 0.5 %collective-permute-start.12 = (bf16[192,256]{1,0:T(8,128)(2,1)S(1)}, bf16[192,256]{1,0:T(8,128)(2,1)S(1)}, u32[]{:S(2)}, u32[]{:S(2)}) collective-permute-start(bf16[192,256]{1,0:T(8,128)(2,1)S(1)} %get-tuple-element.140), channel_id=1, source_target_pairs={{0,4},{4,0},{8,12},{12,8},{1,5},{5,1},{9,13},{13,9},{2,6},{6,2},{1... | collective-permute-start | bytes 294920 | tf_op jit(solution)/shard_map/ppermute | solution.py:20
  29.2 1.1 %kept_products.1 = (bf16[256,4096]{1,0:T(8,128)(2,1)S(1)}, f32[192,4096]{1,0:T(8,128)S(1)}) custom-call(s32[8,128]{1,0:T(8,128)S(1)} %iota.19.starts_ref, bf16[192,256]{1,0:T(8,128)(2,1)S(1)} %kept_gradient.2.kept_ref, bf16[384,4096]{1,0:T(8,128)(2,1)S(1)} %get-tuple-element.98.hidden_ref.h, bf16[256,4096]{1,0:T(8,128)(2,1)S(1)} %get-tuple-element.104.rows_ref.w0), custom_call_target="tpu_custom_call" | custom-call | flops 400000000 | bytes 1 | tf_op jit(solution)/shard_map/kept_products/pallas_call | solution.py:70
  30.3 0.1 kept_gradient.3.refs_0_
  30.5 0.0 collective-permute-done.8.kept_ref
  30.5 0.0 collective-permute-done.10.arriving_ref
  30.5 0.3 gradient.2
  30.8 1.0 %collective-permute-start.11 = (bf16[384,256]{1,0:T(8,128)(2,1)S(1)}, bf16[384,256]{1,0:T(8,128)(2,1)S(1)}, u32[]{:S(2)}, u32[]{:S(2)}) collective-permute-start(bf16[384,256]{1,0:T(8,128)(2,1)S(1)} %get-tuple-element.147), channel_id=1, source_target_pairs={{0,2},{2,0},{1,3},{3,1},{4,6},{6,4},{5,7},{7,5},{8,10},{10,8},{9,1... | collective-permute-start | bytes 589832 | tf_op jit(solution)/shard_map/ppermute | solution.py:20
  31.8 0.7 %collective-permute-done.12.arriving_ref = bf16[192,256]{1,0:T(8,128)(2,1)S(1)} collective-permute-done((bf16[192,256]{1,0:T(8,128)(2,1)S(1)}, bf16[192,256]{1,0:T(8,128)(2,1)S(1)}, u32[]{:S(2)}, u32[]{:S(2)}) %collective-permute-start.12) | collective-permute-done | bytes 98336 | tf_op jit(solution)/shard_map/ppermute | solution.py:20
  32.5 0.3 gradient.3
  32.8 0.8 %collective-permute-start.13 = (bf16[208,256]{1,0:T(8,128)(2,1)S(1)}, bf16[208,256]{1,0:T(8,128)(2,1)S(1)}, u32[]{:S(2)}, u32[]{:S(2)}) collective-permute-start(bf16[208,256]{1,0:T(8,128)(2,1)S(1)} %get-tuple-element.154), channel_id=1, source_target_pairs={{0,2},{2,0},{1,3},{3,1},{4,6},{6,4},{5,7},{7,5},{8,10},{10,8},{9,1... | collective-permute-start | bytes 319496 | tf_op jit(solution)/shard_map/ppermute | solution.py:20
  33.6 3.5 %first_blocks.1 = (bf16[1024,4096]{1,0:T(8,128)(2,1)}, f32[384,4096]{1,0:T(8,128)S(1)}) custom-call(s32[8,128]{1,0:T(8,128)S(1)} %iota.19.starts_ref, bf16[384,256]{1,0:T(8,128)(2,1)S(1)} %get-tuple-element.155.g0, bf16[384,256]{1,0:T(8,128)(2,1)S(1)} %get-tuple-element.156.g1, bf16[256,4096]{1,0:T(8,128)(2,1)S(1)} %get-tuple-element.142.term_ref, ...), custom_call_target="tpu_custom_call" | custom-call | flops 400000000 | bytes 1 | tf_op jit(solution)/shard_map/first_blocks/pallas_call | solution.py:70
  37.1 0.0 collective-permute-done.11.rest_ref.kept_ref
  37.1 0.1 in_place.2.g0
  37.2 0.0 collective-permute-done.13.rest_ref.arriving_ref
  37.2 0.1 in_place.3.g1
  37.3 1.0 %leave_to_other.1 = (bf16[208,4096]{1,0:T(8,128)(2,1)S(1)}, f32[2,192]{1,0:T(2,128)S(1)}) custom-call(bf16[384,256]{1,0:T(8,128)(2,1)S(1)} %in_place.2.g0, bf16[256,4096]{1,0:T(8,128)(2,1)S(1)} %get-tuple-element.96.held_ref.rows0.w0, bf16[384,256]{1,0:T(8,128)(2,1)S(1)} %in_place.3.g1, bf16[256,4096]{1,0:T(8,128)(2,1)S(1)} %get-tuple-element.102.rows_ref.rows1.w1, ...), custom_call_target="tpu_custom_call" | custom-call | flops 400000000 | bytes 1 | tf_op jit(solution)/shard_map/leave_to_other/pallas_call | solution.py:70
  38.3 3.7 %collective-permute-start.14 = (bf16[208,4096]{1,0:T(8,128)(2,1)S(1)}, bf16[208,4096]{1,0:T(8,128)(2,1)S(1)}, u32[]{:S(2)}, u32[]{:S(2)}) collective-permute-start(bf16[208,4096]{1,0:T(8,128)(2,1)S(1)} %get-tuple-element.168), channel_id=1, source_target_pairs={{0,1},{1,0},{2,3},{3,2},{4,5},{5,4},{6,7},{7,6},{8,9},{9,8},{10,11... | collective-permute-start | bytes 5111816 | tf_op jit(solution)/shard_map/ppermute | solution.py:20
  42.0 3.7 %last_blocks.1 = (bf16[1024,4096]{1,0:T(8,128)(2,1)}, f32[192,4096]{1,0:T(8,128)S(1)}) custom-call(s32[8,128]{1,0:T(8,128)S(1)} %iota.19.starts_ref, bf16[384,256]{1,0:T(8,128)(2,1)S(1)} %in_place.2.g0, bf16[384,256]{1,0:T(8,128)(2,1)S(1)} %in_place.3.g1, bf16[384,4096]{1,0:T(8,128)(2,1)S(1)} %get-tuple-element.98.hidden_ref.h, ...), custom_call_target="tpu_custom_call", output_to_operand_aliasing={{0}: (7, {})} | custom-call | flops 400000000 | bytes 1 | tf_op jit(solution)/shard_map/last_blocks/pallas_call | solution.py:70
  45.7 0.0 collective-permute-done.14.arrived_ref
  45.7 1.3 %last_grads.1 = (bf16[192,4096]{1,0:T(8,128)(2,1)}, f32[1,192]{1,0:T(1,128)}) custom-call(f32[192,4096]{1,0:T(8,128)S(1)} %get-tuple-element.174.before_ref, bf16[208,4096]{1,0:T(8,128)(2,1)S(1)} %collective-permute-done.14.arrived_ref, f32[192,4096]{1,0:T(8,128)S(1)} %slope_of.1.slope, f32[2,192]{1,0:T(2,128)S(1)} %get-tuple-element.176.spread_ref), custom_call_target="tpu_custom_call" | custom-call | flops 400000000 | bytes 1 | tf_op jit(solution)/shard_map/last_grads/pallas_call | solution.py:70
  (3 shorter events, 0.1 us)
Async XLA Ops:
  0.6 5.8 %collective-permute-start = (bf16[192,4096]{1,0:T(8,128)(2,1)}, bf16[192,4096]{1,0:T(8,128)(2,1)S(1)}, u32[]{:S(2)}, u32[]{:S(2)}) collective-permute-start(bf16[192,4096]{1,0:T(8,128)(2,1)} %bitcast.9), channel_id=1, source_target_pairs={{0,1},{1,0},{2,3},{3,2},{4,5},{5,4},{6,7},{7,6},{8,9},{9,8},{10,11... | collective-permute-start | bytes 4718600 | tf_op jit(solution)/shard_map/ppermute | solution.py:20
  3.7 8.6 %collective-permute-start.1 = (bf16[192,256]{1,0:T(8,128)(2,1)S(1)}, bf16[192,256]{1,0:T(8,128)(2,1)S(1)}, u32[]{:S(2)}, u32[]{:S(2)}) collective-permute-start(bf16[192,256]{1,0:T(8,128)(2,1)S(1)} %get-tuple-element.94), channel_id=1, source_target_pairs={{0,2},{2,0},{1,3},{3,1},{4,6},{6,4},{5,7},{7,5},{8,10},{10,8},{9,1... | collective-permute-start | bytes 294920 | tf_op jit(solution)/shard_map/ppermute | solution.py:20
  8.0 4.3 %collective-permute-start.2 = (bf16[192,256]{1,0:T(8,128)(2,1)S(1)}, bf16[192,256]{1,0:T(8,128)(2,1)S(1)}, u32[]{:S(2)}, u32[]{:S(2)}) collective-permute-start(bf16[192,256]{1,0:T(8,128)(2,1)S(1)} %get-tuple-element.101), channel_id=1, source_target_pairs={{0,2},{2,0},{1,3},{3,1},{4,6},{6,4},{5,7},{7,5},{8,10},{10,8},{9,1... | collective-permute-start | bytes 294920 | tf_op jit(solution)/shard_map/ppermute | solution.py:20
  10.0 6.1 %collective-permute-start.4 = (bf16[384,256]{1,0:T(8,128)(2,1)S(1)}, bf16[384,256]{1,0:T(8,128)(2,1)S(1)}, u32[]{:S(2)}, u32[]{:S(2)}) collective-permute-start(bf16[384,256]{1,0:T(8,128)(2,1)S(1)} %get-tuple-element.103), channel_id=1, source_target_pairs={{0,2},{2,0},{1,3},{3,1},{4,6},{6,4},{5,7},{7,5},{8,10},{10,8},{9,1... | collective-permute-start | bytes 589832 | tf_op jit(solution)/shard_map/ppermute | solution.py:20
  12.5 5.2 %collective-permute-start.3 = (bf16[192,256]{1,0:T(8,128)(2,1)S(1)}, bf16[192,256]{1,0:T(8,128)(2,1)S(1)}, u32[]{:S(2)}, u32[]{:S(2)}) collective-permute-start(bf16[192,256]{1,0:T(8,128)(2,1)S(1)} %get-tuple-element.109), channel_id=1, source_target_pairs={{0,4},{4,0},{8,12},{12,8},{1,5},{5,1},{9,13},{13,9},{2,6},{6,2},{1... | collective-permute-start | bytes 294920 | tf_op jit(solution)/shard_map/ppermute | solution.py:20
  14.8 5.3 %copy-start = (bf16[192]{0:T(256)(128)(2,1)S(1)}, bf16[192]{0:T(256)(128)(2,1)}, u32[]{:S(2)}) copy-start(bf16[192]{0:T(256)(128)(2,1)} %param.5) | copy-start | bytes 1156
  16.3 5.8 %collective-permute-start.6 = (bf16[208,256]{1,0:T(8,128)(2,1)S(1)}, bf16[208,256]{1,0:T(8,128)(2,1)S(1)}, u32[]{:S(2)}, u32[]{:S(2)}) collective-permute-start(bf16[208,256]{1,0:T(8,128)(2,1)S(1)} %get-tuple-element.116), channel_id=1, source_target_pairs={{0,4},{4,0},{8,12},{12,8},{1,5},{5,1},{9,13},{13,9},{2,6},{6,2},{1... | collective-permute-start | bytes 319496 | tf_op jit(solution)/shard_map/ppermute | solution.py:20
  17.7 5.4 %collective-permute-start.5 = (bf16[192,256]{1,0:T(8,128)(2,1)S(1)}, bf16[192,256]{1,0:T(8,128)(2,1)S(1)}, u32[]{:S(2)}, u32[]{:S(2)}) collective-permute-start(bf16[192,256]{1,0:T(8,128)(2,1)S(1)} %get-tuple-element.120), channel_id=1, source_target_pairs={{0,8},{4,12},{8,0},{12,4},{1,9},{5,13},{9,1},{13,5},{2,10},{6,14},... | collective-permute-start | bytes 294920 | tf_op jit(solution)/shard_map/ppermute | solution.py:20
  20.1 4.4 %collective-permute-start.7 = (bf16[192]{0:T(256)(128)(2,1)S(1)}, bf16[192]{0:T(256)(128)(2,1)S(1)}, u32[]{:S(2)}, u32[]{:S(2)}) collective-permute-start(bf16[192]{0:T(256)(128)(2,1)S(1)} %copy-done), channel_id=1, source_target_pairs={{0,1},{1,0},{2,3},{3,2},{4,5},{5,4},{6,7},{7,6},{8,9},{9,8},{10,11... | collective-permute-start | bytes 1160 | tf_op jit(solution)/shard_map/ppermute | solution.py:20
  22.1 6.5 %collective-permute-start.9 = (bf16[208,256]{1,0:T(8,128)(2,1)S(1)}, bf16[208,256]{1,0:T(8,128)(2,1)S(1)}, u32[]{:S(2)}, u32[]{:S(2)}) collective-permute-start(bf16[208,256]{1,0:T(8,128)(2,1)S(1)} %get-tuple-element.126), channel_id=1, source_target_pairs={{0,8},{4,12},{8,0},{12,4},{1,9},{5,13},{9,1},{13,5},{2,10},{6,14},... | collective-permute-start | bytes 319496 | tf_op jit(solution)/shard_map/ppermute | solution.py:20
  23.2 7.3 %collective-permute-start.10 = (bf16[192,256]{1,0:T(8,128)(2,1)S(1)}, bf16[192,256]{1,0:T(8,128)(2,1)S(1)}, u32[]{:S(2)}, u32[]{:S(2)}) collective-permute-start(bf16[192,256]{1,0:T(8,128)(2,1)S(1)} %get-tuple-element.131), channel_id=1, source_target_pairs={{0,4},{4,0},{8,12},{12,8},{1,5},{5,1},{9,13},{13,9},{2,6},{6,2},{1... | collective-permute-start | bytes 294920 | tf_op jit(solution)/shard_map/ppermute | solution.py:20
  24.9 5.6 %collective-permute-start.8 = (bf16[192,256]{1,0:T(8,128)(2,1)S(1)}, bf16[192,256]{1,0:T(8,128)(2,1)S(1)}, u32[]{:S(2)}, u32[]{:S(2)}) collective-permute-start(bf16[192,256]{1,0:T(8,128)(2,1)S(1)} %kept_gradient.2.kept_ref), channel_id=1, source_target_pairs={{0,2},{2,0},{1,3},{3,1},{4,6},{6,4},{5,7},{7,5},{8,10},{10,8},{9,1... | collective-permute-start | bytes 294920 | tf_op jit(solution)/shard_map/ppermute | solution.py:20
  28.7 3.8 %collective-permute-start.12 = (bf16[192,256]{1,0:T(8,128)(2,1)S(1)}, bf16[192,256]{1,0:T(8,128)(2,1)S(1)}, u32[]{:S(2)}, u32[]{:S(2)}) collective-permute-start(bf16[192,256]{1,0:T(8,128)(2,1)S(1)} %get-tuple-element.140), channel_id=1, source_target_pairs={{0,4},{4,0},{8,12},{12,8},{1,5},{5,1},{9,13},{13,9},{2,6},{6,2},{1... | collective-permute-start | bytes 294920 | tf_op jit(solution)/shard_map/ppermute | solution.py:20
  30.8 6.3 %collective-permute-start.11 = (bf16[384,256]{1,0:T(8,128)(2,1)S(1)}, bf16[384,256]{1,0:T(8,128)(2,1)S(1)}, u32[]{:S(2)}, u32[]{:S(2)}) collective-permute-start(bf16[384,256]{1,0:T(8,128)(2,1)S(1)} %get-tuple-element.147), channel_id=1, source_target_pairs={{0,2},{2,0},{1,3},{3,1},{4,6},{6,4},{5,7},{7,5},{8,10},{10,8},{9,1... | collective-permute-start | bytes 589832 | tf_op jit(solution)/shard_map/ppermute | solution.py:20
  32.8 4.4 %collective-permute-start.13 = (bf16[208,256]{1,0:T(8,128)(2,1)S(1)}, bf16[208,256]{1,0:T(8,128)(2,1)S(1)}, u32[]{:S(2)}, u32[]{:S(2)}) collective-permute-start(bf16[208,256]{1,0:T(8,128)(2,1)S(1)} %get-tuple-element.154), channel_id=1, source_target_pairs={{0,2},{2,0},{1,3},{3,1},{4,6},{6,4},{5,7},{7,5},{8,10},{10,8},{9,1... | collective-permute-start | bytes 319496 | tf_op jit(solution)/shard_map/ppermute | solution.py:20
  38.3 7.4 %collective-permute-start.14 = (bf16[208,4096]{1,0:T(8,128)(2,1)S(1)}, bf16[208,4096]{1,0:T(8,128)(2,1)S(1)}, u32[]{:S(2)}, u32[]{:S(2)}) collective-permute-start(bf16[208,4096]{1,0:T(8,128)(2,1)S(1)} %get-tuple-element.168), channel_id=1, source_target_pairs={{0,1},{1,0},{2,3},{3,2},{4,5},{5,4},{6,7},{7,6},{8,9},{9,8},{10,11... | collective-permute-start | bytes 5111816 | tf_op jit(solution)/shard_map/ppermute | solution.py:20
